TPU v7x, 32 devices: a whole 2x2x4 slice. The times are simulated.
32 devices in a mesh: src: 4 (over y, core), rcv: 8 (over z, x).
Axes of the slice: x: 2, y: 2, z: 4, core: 2. Of those that a mesh axis runs over, the one named last changes fastest.
Arguments:
- spectra: bfloat16 [256, 287, 192], P(('src', 'rcv')), may hold values from -6 to 6
- block_mask: int32 [4, 4], replicated, may hold values from 0 to 1, as said below
Outputs:
- correlations: bfloat16 [256, 4, 64, 576], P('src', None, 'rcv')
Inputs may be any that keep to these rules, and one draw needn't show every extreme that they name: `block_mask`: symmetric, with ones on the diagonal.
All inputs are finite; a program needn't handle non-finite values.
Results may differ from a plain program's by a relative error of at most 0.0055.
Values may be sent and summed in bfloat16 or wider, within the bound.
No kernel may reach another device: no remote copies, remote signals or barrier semaphores. Data moves between devices by JAX's collectives and lax.ppermute only.
A program may use at most 128 MiB of HBM per device.

v0:
```python
import math

import jax
import jax.numpy as jnp
from jax import lax
from jax.sharding import PartitionSpec as P


def whiten(spectra):
    values = spectra.astype(jnp.float32)
    mean_power = jnp.mean(values * values, axis=2, keepdims=True)
    return (values * lax.rsqrt(mean_power + 1e-06)).astype(jnp.bfloat16)


def rotate(right_rows):
    real_part = right_rows[:, :, :, 0]
    imag_part = right_rows[:, :, :, 1]
    as_real = jnp.stack([real_part, imag_part], axis=3)
    as_imag = jnp.stack([-imag_part, real_part], axis=3)
    return jnp.stack([as_real, as_imag], axis=4)


def crossing(left_rows, right_rows, norm_scale):
    values = jnp.einsum(
        "iwacf,jwbcef->ijabef", left_rows, rotate(right_rows), preferred_element_type=jnp.float32
    )
    return (
        values.reshape(left_rows.shape[0], right_rows.shape[0], 18, left_rows.shape[4]) * norm_scale
    )


def block_weights(mask_line, row_count, block_size):
    row_ids = lax.iota(jnp.int32, row_count)
    owner_block = row_ids // block_size
    hit_table = (owner_block[:, None] == lax.iota(jnp.int32, mask_line.shape[0])[None, :]).astype(
        jnp.float32
    )
    return jnp.sum(hit_table * mask_line[None, :], axis=1)


def masked_cross(left_rows, right_rows, mask_line, block_size, norm_scale):
    weights = block_weights(mask_line, right_rows.shape[0], block_size)
    return crossing(left_rows, right_rows, norm_scale) * weights[None, :, None, None]


def on_device(spectra, block_mask):
    seg_count = spectra.shape[1]
    bin_count = spectra.shape[2] // 6
    block_count = lax.axis_size("src")
    rcv_count = lax.axis_size("rcv")
    local_count = spectra.shape[0]
    block_size = local_count * rcv_count
    norm_scale = 1.0 / math.sqrt(seg_count)
    local_rows = whiten(spectra).reshape(local_count, seg_count, 3, 2, bin_count)
    source_block = lax.axis_index("src")
    mask_line = lax.dynamic_index_in_dim(block_mask, source_block, 0, keepdims=False).astype(
        jnp.float32
    )
    sources = lax.all_gather(local_rows, "rcv", axis=0, tiled=True)
    result = masked_cross(
        sources,
        lax.all_gather(local_rows, "src", axis=0, tiled=True),
        mask_line,
        local_count,
        norm_scale,
    )
    return result.reshape(block_size, block_count, local_count, 18 * bin_count).astype(jnp.bfloat16)


def solution(mesh):
    placed = (P(("src", "rcv"), None, None), P())
    return jax.shard_map(
        on_device,
        mesh=mesh,
        in_specs=placed,
        out_specs=P("src", None, "rcv", None),
        check_vma=False,
    )
```

profile of v0, /device:TPU:0, one launch (start us, length us, event | category | flops | bytes accessed | tf_op | source)
XLA Modules:
  0.0 232.8 jit_solution(1557560389013127714)
XLA Ops:
  6.5 0.0 all-gather.3.cloned.1.call-start
  6.5 2.0 copy.10
  8.5 0.3 fusion.7
  8.8 0.2 fusion.8
  9.1 1.7 copy.11
  10.8 0.0 all-gather.3.cloned.1.call-update
  10.8 0.0 all-gather.5.cloned.1.call-start
  10.9 0.7 all-gather.5.cloned.1.call-update
  11.6 0.7 convert_bitcast_fusion
  12.3 0.1 select_reduce_fusion
  12.4 0.1 mul.46
  12.4 38.6 %all-gather.3.cloned.1.call-done = bf16[32,287,3,2,32]{1,0,3,2,4:T(8,128)(2,1)} async-done(((bf16[8,287,3,2,32]{1,0,3,2,4:T(8,128)(2,1)}), bf16[32,287,3,2,32]{1,0,3,2,4:T(8,128)(2,1)}) %all-gather.3.cloned.1.call-update) | async-done | bytes 3526672 | tf_op jit(solution)/shard_map/all_gather | solution.py:62
  51.1 2.8 %slice_negate_fusion = (bf16[32,287,3,1,32]{1,0,3,2,4:T(8,128)(2,1)S(1)}, bf16[32,287,3,1,32]{1,0,3,2,4:T(8,128)(2,1)S(1)}) fusion(bf16[32,287,3,2,32]{1,0,3,2,4:T(8,128)(2,1)} %all-gather.3.cloned.1.call-done), kind=kLoop, calls=%fused_computation.12 | loop fusion | flops 881664 | bytes 7053312 | tf_op jit(solution)/shard_map/neg | solution.py:19
  53.9 3.1 %maximum_bitcast_fusion.2 = bf16[32,287,3,2,1,32]{1,0,3,4,2,5:T(8,128)(2,1)} fusion(bf16[32,287,3,1,32]{1,0,3,2,4:T(8,128)(2,1)S(1)} %get-tuple-element.6, bf16[32,287,3,1,32]{1,0,3,2,4:T(8,128)(2,1)S(1)} %get-tuple-element.5), kind=kLoop, calls=%fused_computation.6 | loop fusion | flops 1763328 | bytes 7053312 | tf_op jit(solution)/shard_map/stack | solution.py:20
  56.9 134.4 %all-gather.5.cloned.1.call-done = bf16[64,287,3,2,32]{1,0,3,2,4:T(8,128)(2,1)} async-done(((bf16[8,287,3,2,32]{1,0,3,2,4:T(8,128)(2,1)}), bf16[64,287,3,2,32]{1,0,3,2,4:T(8,128)(2,1)}) %all-gather.5.cloned.1.call-update) | async-done | bytes 7053328 | tf_op jit(solution)/shard_map/all_gather | solution.py:59
  191.3 15.3 %fusion.4 = f32[64,32,3,3,2,32]{0,1,2,4,3,5:T(8,128)} fusion(bf16[64,287,3,2,32]{1,0,3,2,4:T(8,128)(2,1)} %all-gather.5.cloned.1.call-done, bf16[32,287,3,2,1,32]{1,0,3,4,2,5:T(8,128)(2,1)} %maximum_bitcast_fusion.2, bf16[32,287,3,2,1,32]{1,0,3,4,2,5:T(8,128)(2,1)} %bitcast.29), kind=kOutput, calls=%fused_computation.7 | convolution fusion | flops 1368342528 | bytes 18825216 | tf_op jit(solution)/shard_map/iwacf,jwbcef->ijabef/dot_general | solution.py:24
  206.7 9.1 %copy.14 = f32[64,32,3,3,2,32]{0,5,4,3,2,1:T(8,128)S(1)} copy(f32[64,32,3,3,2,32]{0,1,2,4,3,5:T(8,128)} %fusion.4) | data formatting | bytes 9437184 | tf_op jit(solution)/shard_map/iwacf,jwbcef->ijabef/transpose | solution.py:24
  215.8 3.3 %multiply_convert_fusion = bf16[64,4,8,576]{0,3,2,1:T(8,128)(2,1)} fusion(f32[64,4,8,576]{0,3,2,1:T(8,128)S(1)} %bitcast.28, f32[4,8]{1,0:T(4,128)S(1)} %mul.46), kind=kLoop, calls=%fused_computation.5 | loop fusion | flops 2359296 | bytes 7078016 | tf_op jit(solution)/shard_map/convert_element_type | solution.py:67
  219.2 6.8 %copy.15 = bf16[64,4,8,576]{3,2,1,0:T(8,128)(2,1)} copy(bf16[64,4,8,576]{0,3,2,1:T(8,128)(2,1)} %multiply_convert_fusion) | data formatting | bytes 4718592 | tf_op jit(solution)/shard_map/convert_element_type | solution.py:67
  (3 shorter events, 0.0 us)
Async XLA Ops:
  6.5 44.5 %all-gather.3.cloned.1.call-start = ((), (), s32[]{:S(2)}) async-start(), calls=%async_computation | async-start | bytes 5898240 | tf_op jit(solution)/shard_map/all_gather | solution.py:62
  10.8 180.5 %all-gather.5.cloned.1.call-start = ((), (), s32[]{:S(2)}) async-start(), calls=%async_computation.1 | async-start | bytes 10616832 | tf_op jit(solution)/shard_map/all_gather | solution.py:59
Sparse Core Ops, SparseCore 0:
  10.9 40.0 all-gather.2
  53.1 138.1 all-gather.4
where the time goes:
time: 233 us
  waiting for transfers between devices  174 us (75%)
  local copies, waits for them, and re-layouts  19.7 us (8%)
  matrix products  15.3 us (7%)
  between operations  13.5 us (6%)
  other arithmetic  10.5 us (5%)
    all_gather x1, waiting for transfers between devices, on_device(): sources = lax.all_gather(local_rows, 'rcv', axis=0, tiled=True)  134 us
    all_gather x1, waiting for transfers between devices, on_device(): lax.all_gather(local_rows, 'src', axis=0, tiled=True)  38.6 us
    dot_general x1, matrix products, crossing(): jnp.einsum('iwacf,jwbcef->ijabef', left_rows, rotate(right_rows), preferr...  15.3 us
    transpose x1, local copies, waits for them, and re-layouts, crossing(): jnp.einsum('iwacf,jwbcef->ijabef', left_rows, rotate(right_rows), preferr...  9.14 us
    convert_element_type x1, local copies, waits for them, and re-layouts, on_device(): result.reshape(block_size, block_count, local_count, 18 * bin_count)  6.78 us
  transfers between devices with their start and end apart: 2, of which 2 were waited for; matrix products, arithmetic and copies ran while one was open for 3% of the time, Pallas kernels for 0%

commit v1 on v0

v1 whole, which is shorter than its diff:
```python
import functools
import math

import jax
import jax.numpy as jnp
from jax import lax
from jax.experimental import pallas as pl
from jax.experimental.pallas import tpu as pltpu
from jax.sharding import PartitionSpec as P

GROUPS = 8
TILES = 27
PAIR_ROWS = 13 * 16
GROUP_ROWS = TILES * 16
BLOCK_ROWS = GROUPS * GROUP_ROWS
HALF_ROWS = BLOCK_ROWS // 2
STATIONS = 8
F32 = jnp.float32
BF16 = jnp.bfloat16


def prepare_kernel(x_ref, first_ref, second_ref, d_ref):
    count, segs = x_ref.shape[0], x_ref.shape[1]
    tail = segs - 256
    if count < STATIONS:
        d_ref[...] = jnp.zeros_like(d_ref)
    lane_group = lax.broadcasted_iota(jnp.int32, (8, 128), 1) // 32
    for i in range(count):
        values = x_ref[i].astype(F32)
        power = jnp.mean(values * values, axis=1, keepdims=True)
        white = (values * lax.rsqrt(power + 1e-06)).astype(BF16).astype(F32)
        main = white[:256].T
        rest = jnp.concatenate([white[256:], jnp.zeros((32 - tail, 192), F32)], axis=0)
        rest = jnp.concatenate([rest] * 4, axis=0).T
        for group in range(4):
            half, pair = group // 2, group % 2
            row = pair * PAIR_ROWS + half * 8 + i
            for line in range(6):
                rows = slice(line * 32 + group * 8, line * 32 + group * 8 + 8)
                for side in range(2):
                    tile = line * 2 + side
                    d_ref[pl.ds(row + tile * 16, 8, stride=GROUP_ROWS), :] = main[
                        rows, side * 128 : side * 128 + 128
                    ]
            first = jnp.zeros((8, 128), F32)
            for line in range(4):
                rows = slice(line * 32 + group * 8, line * 32 + group * 8 + 8)
                first = jnp.where(lane_group == line, rest[rows], first)
            d_ref[pl.ds(row + 12 * 16, 8, stride=GROUP_ROWS), :] = first
        for half in range(2):
            last = jnp.zeros((8, 128), F32)
            for pair in range(2):
                for part in range(2):
                    start = (4 + part) * 32 + (half * 2 + pair) * 8
                    last = jnp.where(
                        lane_group == pair * 2 + part, rest[start : start + 8], last
                    )
            d_ref[pl.ds(26 * 16 + half * 8 + i, 8, stride=GROUP_ROWS), :] = last
    first_ref[...] = d_ref[:HALF_ROWS].astype(BF16)
    second_ref[...] = d_ref[HALF_ROWS:].astype(BF16)


def prepare(spectra):
    half = jax.ShapeDtypeStruct((HALF_ROWS, 128), BF16)
    return pl.pallas_call(
        prepare_kernel,
        out_shape=(half, half),
        scratch_shapes=[pltpu.VMEM((BLOCK_ROWS, 128), F32)],
        compiler_params=pltpu.CompilerParams(vmem_limit_bytes=48 * 2**20),
        name="prepare",
    )(spectra)


def turn_matrix():
    source = lax.broadcasted_iota(jnp.int32, (128, 1024), 0)
    column = lax.broadcasted_iota(jnp.int32, (128, 1024), 1)
    block, lane = column // 128, column % 128
    half, imag, slot = block // 4, (block // 2) % 2, block % 2
    part, seg = (lane % 64) // 32, lane % 32
    wanted = half * 64 + jnp.where(imag == 1, 1 - part, part) * 32 + seg
    sign = jnp.where((imag == 1) & (part == 1), -1.0, 1.0)
    hit = (source == wanted) & (lane // 64 == slot)
    return jnp.where(hit, sign, 0.0).astype(BF16)


def nt(left, right):
    return lax.dot_general(left, right, (((1,), (1,)), ((), ())), preferred_element_type=F32)


def products_kernel(block_count, src_count, place_ref, scale_ref, turn_ref, *refs):
    halves = refs[: 2 + 2 * block_count]
    own_ref, other_ref = refs[2 + 2 * block_count : 4 + 2 * block_count]
    left, right, sums, sems = refs[4 + 2 * block_count :]
    count = own_ref.shape[0]
    copies = [[], []]
    for h in range(2):
        rows = pl.ds(h * HALF_ROWS, HALF_ROWS)
        for n in range(block_count + 1):
            target = left.at[rows] if n == 0 else right.at[n - 1, rows]
            copy = pltpu.make_async_copy(halves[2 * n + h], target, sems.at[h, n])
            copy.start()
            copies[h].append(copy)
    lanes = block_count * 16

    def tile_of(base, tile):
        return right[:, pl.ds(base + tile * 16, 16), :].reshape(lanes, 128)

    def group(q, carry):
        base = pl.multiple_of(q * GROUP_ROWS, 16)
        turn = turn_ref[...]
        last_left = left[pl.ds(base + 26 * 16, 16), :]
        last_turned = jnp.dot(last_left, turn, preferred_element_type=F32).astype(BF16)
        last_right = tile_of(base, 26)
        for pair in range(2):
            start = base + pair * PAIR_ROWS
            tiles = [left[pl.ds(start + t * 16, 16), :] for t in range(13)]
            turned = jnp.dot(tiles[12], turn, preferred_element_type=F32).astype(BF16)
            lines = []
            for a in range(3):
                real, imag = tiles[a * 4 : a * 4 + 2], tiles[a * 4 + 2 : a * 4 + 4]
                lines.append(jnp.concatenate(real + imag, axis=1))
                lines.append(jnp.concatenate(imag + [-real[0], -real[1]], axis=1))
            main = jnp.concatenate(lines, axis=0)
            rest_right = tile_of(start, 12)
            for b in range(3):
                slot = b if b < 2 else pair
                rest = []
                for a in range(3):
                    for e in range(2):
                        of, half = (turned, a) if a < 2 else (last_turned, pair)
                        at = (half * 4 + e * 2 + slot) * 128
                        rest.append(of[:, at : at + 128])
                rest = jnp.concatenate(rest, axis=0)
                weights = jnp.concatenate([tile_of(start, b * 4 + t) for t in range(4)], axis=1)
                result = nt(main, weights) + nt(rest, rest_right if b < 2 else last_right)
                for a in range(3):
                    for e in range(2):
                        for half in range(2):
                            rows = slice((a * 2 + e) * 16 + half * 8, (a * 2 + e) * 16 + half * 8 + 8)
                            at = (a * 6 + b * 2 + e) * 32 + half * 16 + pair * 8 + q
                            for m in range(lanes // 128):
                                sums[pl.ds(m * STATIONS * 576 + at, 8, stride=576), :] = result[
                                    rows, m * 128 : m * 128 + 128
                                ]
        return carry

    for h in range(2):
        for copy in copies[h]:
            copy.wait()
        lax.fori_loop(h * (GROUPS // 2), (h + 1) * (GROUPS // 2), group, 0)

    bin_half = (lax.broadcasted_iota(jnp.int32, (8, 576), 1) % 32) < 16
    for i in range(count):
        for m in range(lanes // 128):
            start = (m * STATIONS + i) * 576
            turned = sums[start : start + 576, :].T
            for n in range(8):
                low, high = turned[n * 16 : n * 16 + 8], turned[n * 16 + 8 : n * 16 + 16]
                at = place_ref[(m * 8 + n) % src_count]
                value = (jnp.where(bin_half, low, high) * scale_ref[at]).astype(BF16)
                out = own_ref if m * 8 + n < src_count else other_ref
                out[i, at] = value[: out.shape[2]]


def products(place, scale, turn, source, blocks, count, src_count):
    out = jax.ShapeDtypeStruct((count, src_count, count, 576), BF16)
    n = len(blocks)
    smem, vmem = pl.BlockSpec(memory_space=pltpu.SMEM), pl.BlockSpec(memory_space=pltpu.VMEM)
    operands = [half for block in (source, *blocks) for half in block]
    return pl.pallas_call(
        functools.partial(products_kernel, n, src_count),
        out_shape=(out, out),
        in_specs=[smem, smem, vmem] + [pl.BlockSpec(memory_space=pl.ANY)] * len(operands),
        out_specs=(vmem, vmem),
        scratch_shapes=[
            pltpu.VMEM((BLOCK_ROWS, 128), BF16),
            pltpu.VMEM((n, BLOCK_ROWS, 128), BF16),
            pltpu.VMEM((n // 8 * STATIONS * 576, 128), F32),
            pltpu.SemaphoreType.DMA((2, n + 1)),
        ],
        compiler_params=pltpu.CompilerParams(vmem_limit_bytes=60 * 2**20),
        cost_estimate=pl.CostEstimate(
            flops=2 * 16 * 3 * 96 * 16 * n * 768, bytes_accessed=8 * 2**20, transcendentals=0
        ),
        name="products",
    )(place, scale, turn, *operands)


def on_device(spectra, block_mask):
    count, segs = spectra.shape[0], spectra.shape[1]
    src_count, rcv_count = lax.axis_size("src"), lax.axis_size("rcv")
    src, rcv = lax.axis_index("src"), lax.axis_index("rcv")
    highs, steps = src_count // 2, rcv_count // 2

    def over_core(half):
        return lax.ppermute(half, "src", [(s, s ^ 1) for s in range(src_count)])

    def over_high(half):
        return lax.ppermute(half, "src", [(s, (s + 2) % src_count) for s in range(src_count)])

    def over_x(half):
        return lax.ppermute(half, "rcv", [(r, r ^ 1) for r in range(rcv_count)])

    def over_z(half):
        return lax.ppermute(half, "rcv", [(r, (r + 2) % rcv_count) for r in range(rcv_count)])

    def each(move, block):
        return tuple(move(half) for half in block)

    scale = lax.dynamic_index_in_dim(block_mask, src, 0, keepdims=False).astype(F32) * (
        1.0 / math.sqrt(segs)
    )
    own = prepare(spectra)
    sources = [own]
    for _ in range(steps - 1):
        sources.append(each(over_z, sources[-1]))
    mine, theirs = [own], [each(over_x, own)]
    for _ in range(highs - 1):
        mine.append(each(over_high, mine[-1]))
        theirs.append((over_high(theirs[-1][0]), over_x(mine[-1][1])))
    blocks = []
    for line in (mine, theirs):
        for block in line:
            blocks += [block, each(over_core, block)]
    place = jnp.stack(
        [((src // 2 - k + highs) % highs) * 2 + lax.rem(src + c, 2) for k in range(highs) for c in range(2)]
    ).astype(jnp.int32)
    turn = turn_matrix()
    result = jnp.zeros((steps, 2, count, src_count, count, 576), BF16)
    x, z = rcv % 2, rcv // 2
    for k, source in enumerate(sources):
        kept, sent = products(place, scale, turn, source, blocks, count, src_count)
        got = over_x(sent)
        at = lax.rem(z - k + steps, steps)
        result = lax.dynamic_update_slice(result, kept[None, None], (at, x, 0, 0, 0, 0))
        result = lax.dynamic_update_slice(result, got[None, None], (at, 1 - x, 0, 0, 0, 0))
    return result.reshape(steps * 2 * count, src_count, count, 576)


def solution(mesh):
    placed = (P(("src", "rcv"), None, None), P())
    return jax.shard_map(
        on_device,
        mesh=mesh,
        in_specs=placed,
        out_specs=P("src", None, "rcv", None),
        check_vma=False,
    )
```

time: 233 us -> 127 us (0.55)
  waiting for transfers between devices: 174 us -> 54.9 us
  Pallas kernels: 0 us -> 45.6 us
  starting transfers between devices: 0.04 us -> 17.3 us
  matrix products: 15.3 us -> 0 us
  local copies, waits for them, and re-layouts: 19.7 us -> 5.58 us
  between operations: 13.5 us -> 0.33 us
  other arithmetic: 10.5 us -> 2.78 us
    all_gather x2 -> x0, waiting for transfers between devices: 173 us -> none  [the longest x1 134 us: on_device(): sources = lax.all_gather(local_rows, 'rcv', axis=0, tiled=True)]
    ppermute x0 -> x24, waiting for transfers between devices: none -> 54.9 us  [the longest x6 32.1 us: over_z(): lax.ppermute(half, 'rcv', [(r, (r + 2) % rcv_count) for r in range(rcv_co...]
    pallas_call x0 -> x5, Pallas kernels: none -> 45.6 us  [the longest x4 44.1 us: products(): pl.pallas_call(functools.partial(products_kernel, n, src_count), out_shap...]
    ppermute x0 -> x24, starting transfers between devices: none -> 17.3 us  [the longest x7 7.92 us: over_x(): return lax.ppermute(half, 'rcv', [(r, r ^ 1) for r in range(rcv_count)])]
    dot_general x1 -> x0, matrix products: 15.3 us -> none  [crossing(): jnp.einsum('iwacf,jwbcef->ijabef', left_rows, rotate(right_rows), preferr...]
    transpose x1 -> x0, local copies, waits for them, and re-layouts: 9.14 us -> none  [crossing(): jnp.einsum('iwacf,jwbcef->ijabef', left_rows, rotate(right_rows), preferr...]
    convert_element_type x1 -> x0, local copies, waits for them, and re-layouts: 6.78 us -> none  [on_device(): result.reshape(block_size, block_count, local_count, 18 * bin_count)]
    unnamed x1 -> x35, local copies, waits for them, and re-layouts: 1.99 us -> 4.98 us
  transfers between devices with their start and end apart: 2 -> 24, of which waited for: 2 -> 8; matrix products, arithmetic and copies ran while one was open for 3% -> 3% of each run, Pallas kernels for 0% -> 35%
where the time goes in v1:
time: 127 us; the launch traced here: 126 us
  waiting for transfers between devices  54.9 us (43%)
  Pallas kernels  45.6 us (36%)
  starting transfers between devices  17.3 us (14%)
  local copies, waits for them, and re-layouts  5.58 us (4%)
  other arithmetic  2.78 us (2%)
    pallas_call x4, Pallas kernels, products(): pl.pallas_call(functools.partial(products_kernel, n, src_count), out_shap...  44.1 us
    ppermute x6, waiting for transfers between devices, over_z(): lax.ppermute(half, 'rcv', [(r, (r + 2) % rcv_count) for r in range(rcv_co...  32.1 us
    ppermute x7, waiting for transfers between devices, over_x(): return lax.ppermute(half, 'rcv', [(r, r ^ 1) for r in range(rcv_count)])  14.3 us
    ppermute x3, waiting for transfers between devices, over_high(): lax.ppermute(half, 'src', [(s, (s + 2) % src_count) for s in range(src_co...  8.53 us
    ppermute x7, starting transfers between devices, over_x(): return lax.ppermute(half, 'rcv', [(r, r ^ 1) for r in range(rcv_count)])  7.92 us
    unnamed x35, local copies, waits for them, and re-layouts  4.98 us
    ppermute x6, starting transfers between devices, over_z(): lax.ppermute(half, 'rcv', [(r, (r + 2) % rcv_count) for r in range(rcv_co...  4.68 us
    ppermute x3, starting transfers between devices, over_high(): lax.ppermute(half, 'src', [(s, (s + 2) % src_count) for s in range(src_co...  3.55 us
  transfers between devices with their start and end apart: 24, of which 8 were waited for; matrix products, arithmetic and copies ran while one was open for 3% of the time, Pallas kernels for 35%

profile of v1, /device:TPU:0, one launch (start us, length us, event | category | flops | bytes accessed | tf_op | source)
XLA Modules:
  0.0 126.4 jit_solution(5781338746107338394)
XLA Ops:
  0.0 1.5 %copy.3.x_ref = bf16[8,287,192]{2,1,0:T(8,128)(2,1)S(1)} copy(bf16[8,287,192]{2,0,1:T(8,128)(2,1)} %param.2) | data formatting | bytes 1763328 | tf_op args[0]
  1.5 1.5 %prepare.1 = (bf16[1728,128]{1,0:T(8,128)(2,1)S(1)}, bf16[1728,128]{1,0:T(8,128)(2,1)S(1)}) custom-call(bf16[8,287,192]{2,1,0:T(8,128)(2,1)S(1)} %copy.3.x_ref), custom_call_target="tpu_custom_call" | custom-call | tf_op jit(solution)/shard_map/prepare/pallas_call | solution.py:65
  3.0 0.0 copy-start
  3.0 3.0 %collective-permute-start.6 = (bf16[1728,128]{1,0:T(8,128)(2,1)S(1)}, bf16[1728,128]{1,0:T(8,128)(2,1)S(1)}, u32[]{:S(2)}, u32[]{:S(2)}) collective-permute-start(bf16[1728,128]{1,0:T(8,128)(2,1)S(1)} %get-tuple-element.15.refs_0_.refs_2_), channel_id=1, source_target_pairs={{0,1},{1,0},{2,3},{3,2},{4,5},{5,4},{6,7},{7,6},{8,9},{9,8},{10,11... | collective-permute-start | bytes 1327112 | tf_op jit(solution)/shard_map/ppermute | solution.py:202
  6.0 1.5 %collective-permute-start.3 = (bf16[1728,128]{1,0:T(8,128)(2,1)S(1)}, bf16[1728,128]{1,0:T(8,128)(2,1)S(1)}, u32[]{:S(2)}, u32[]{:S(2)}) collective-permute-start(bf16[1728,128]{1,0:T(8,128)(2,1)S(1)} %get-tuple-element.16.refs_1_.refs_3_), channel_id=1, source_target_pairs={{0,16},{8,24},{16,0},{24,8},{1,17},{9,25},{17,1},{25,9},{2,18},{10... | collective-permute-start | bytes 1327112 | tf_op jit(solution)/shard_map/ppermute | solution.py:199
  7.5 0.5 collective-permute-start.2
  8.0 0.1 collective-permute-start.7
  8.1 0.0 collective-permute-start
  8.1 8.9 %collective-permute-done.6.refs_10_ = bf16[1728,128]{1,0:T(8,128)(2,1)S(1)} collective-permute-done((bf16[1728,128]{1,0:T(8,128)(2,1)S(1)}, bf16[1728,128]{1,0:T(8,128)(2,1)S(1)}, u32[]{:S(2)}, u32[]{:S(2)}) %collective-permute-start.6) | collective-permute-done | bytes 442400 | tf_op jit(solution)/shard_map/ppermute | solution.py:202
  17.0 0.0 collective-permute-start.1
  17.0 2.1 %collective-permute-done.3.refs_7_ = bf16[1728,128]{1,0:T(8,128)(2,1)S(1)} collective-permute-done((bf16[1728,128]{1,0:T(8,128)(2,1)S(1)}, bf16[1728,128]{1,0:T(8,128)(2,1)S(1)}, u32[]{:S(2)}, u32[]{:S(2)}) %collective-permute-start.3) | collective-permute-done | bytes 442400 | tf_op jit(solution)/shard_map/ppermute | solution.py:199
  19.1 1.6 %collective-permute-start.15 = (bf16[1728,128]{1,0:T(8,128)(2,1)S(1)}, bf16[1728,128]{1,0:T(8,128)(2,1)}, u32[]{:S(2)}, u32[]{:S(2)}) collective-permute-start(bf16[1728,128]{1,0:T(8,128)(2,1)S(1)} %get-tuple-element.15.refs_0_.refs_2_), channel_id=1, source_target_pairs={{0,2},{1,3},{2,4},{3,5},{4,6},{5,7},{6,0},{7,1},{8,10},{9,11},{10,... | collective-permute-start | bytes 1327112 | tf_op jit(solution)/shard_map/ppermute | solution.py:205
  20.7 6.4 %collective-permute-done.2.refs_6_ = bf16[1728,128]{1,0:T(8,128)(2,1)S(1)} collective-permute-done((bf16[1728,128]{1,0:T(8,128)(2,1)S(1)}, bf16[1728,128]{1,0:T(8,128)(2,1)S(1)}, u32[]{:S(2)}, u32[]{:S(2)}) %collective-permute-start.2) | collective-permute-done | bytes 442400 | tf_op jit(solution)/shard_map/ppermute | solution.py:199
  27.1 1.6 %collective-permute-start.16 = (bf16[1728,128]{1,0:T(8,128)(2,1)S(1)}, bf16[1728,128]{1,0:T(8,128)(2,1)}, u32[]{:S(2)}, u32[]{:S(2)}) collective-permute-start(bf16[1728,128]{1,0:T(8,128)(2,1)S(1)} %get-tuple-element.16.refs_1_.refs_3_), channel_id=1, source_target_pairs={{0,2},{1,3},{2,4},{3,5},{4,6},{5,7},{6,0},{7,1},{8,10},{9,11},{10,... | collective-permute-start | bytes 1327112 | tf_op jit(solution)/shard_map/ppermute | solution.py:205
  28.7 0.0 collective-permute-done.7.refs_11_
  28.7 1.5 %collective-permute-start.10 = (bf16[1728,128]{1,0:T(8,128)(2,1)S(1)}, bf16[1728,128]{1,0:T(8,128)(2,1)}, u32[]{:S(2)}, u32[]{:S(2)}) collective-permute-start(bf16[1728,128]{1,0:T(8,128)(2,1)S(1)} %collective-permute-done.6.refs_10_), channel_id=1, source_target_pairs={{0,16},{8,24},{16,0},{24,8},{1,17},{9,25},{17,1},{25,9},{2,18},{10... | collective-permute-start | bytes 1327112 | tf_op jit(solution)/shard_map/ppermute | solution.py:199
  30.2 0.0 collective-permute-done.refs_4_
  30.2 0.5 collective-permute-start.11
  30.7 0.0 collective-permute-done.1.refs_5_
  30.8 0.0 collective-permute-start.5
  30.8 3.0 %collective-permute-done.15.refs_0_ = bf16[1728,128]{1,0:T(8,128)(2,1)} collective-permute-done((bf16[1728,128]{1,0:T(8,128)(2,1)S(1)}, bf16[1728,128]{1,0:T(8,128)(2,1)}, u32[]{:S(2)}, u32[]{:S(2)}) %collective-permute-start.15) | collective-permute-done | bytes 442400 | tf_op jit(solution)/shard_map/ppermute | solution.py:205
  33.7 0.0 collective-permute-start.8
  33.8 7.8 %collective-permute-done.16.refs_1_ = bf16[1728,128]{1,0:T(8,128)(2,1)} collective-permute-done((bf16[1728,128]{1,0:T(8,128)(2,1)S(1)}, bf16[1728,128]{1,0:T(8,128)(2,1)}, u32[]{:S(2)}, u32[]{:S(2)}) %collective-permute-start.16) | collective-permute-done | bytes 442400 | tf_op jit(solution)/shard_map/ppermute | solution.py:205
  41.6 0.0 collective-permute-start.4
  41.6 0.0 collective-permute-done.10.refs_14_
  41.6 0.6 collective-permute-start.9
  42.2 0.0 collective-permute-done.11.refs_15_
  42.2 0.0 collective-permute-start.18
  42.2 0.0 collective-permute-done.5.refs_9_
  42.2 1.5 %collective-permute-start.19 = (bf16[1728,128]{1,0:T(8,128)(2,1)}, bf16[1728,128]{1,0:T(8,128)(2,1)}, u32[]{:S(2)}, u32[]{:S(2)}) collective-permute-start(bf16[1728,128]{1,0:T(8,128)(2,1)} %collective-permute-done.16.refs_1_), channel_id=1, source_target_pairs={{0,2},{1,3},{2,4},{3,5},{4,6},{5,7},{6,0},{7,1},{8,10},{9,11},{10,... | collective-permute-start | bytes 1327112 | tf_op jit(solution)/shard_map/ppermute | solution.py:205
  43.7 0.0 collective-permute-done.8.refs_12_
  43.7 0.0 collective-permute-start.12
  43.8 0.0 collective-permute-done.4.refs_8_
  43.8 0.5 collective-permute-start.13
  44.3 0.2 copy-done.9
  44.5 0.2 copy-done.10
  44.7 0.9 select_convert_fusion.turn_ref
  45.6 11.8 %collective-permute-done.18.refs_0_ = bf16[1728,128]{1,0:T(8,128)(2,1)} collective-permute-done((bf16[1728,128]{1,0:T(8,128)(2,1)}, bf16[1728,128]{1,0:T(8,128)(2,1)}, u32[]{:S(2)}, u32[]{:S(2)}) %collective-permute-start.18) | collective-permute-done | bytes 442400 | tf_op jit(solution)/shard_map/ppermute | solution.py:205
  57.3 0.0 collective-permute-start.21
  57.3 9.5 %collective-permute-done.19.refs_1_ = bf16[1728,128]{1,0:T(8,128)(2,1)} collective-permute-done((bf16[1728,128]{1,0:T(8,128)(2,1)}, bf16[1728,128]{1,0:T(8,128)(2,1)}, u32[]{:S(2)}, u32[]{:S(2)}) %collective-permute-start.19) | collective-permute-done | bytes 442400 | tf_op jit(solution)/shard_map/ppermute | solution.py:205
  66.8 0.0 collective-permute-start.22
  66.8 1.2 fusion.30.scale_ref
  68.1 0.7 pad_add_fusion.place_ref
  68.7 0.0 collective-permute-done.9.refs_13_
  68.7 0.0 collective-permute-done.12.refs_16_
  68.7 0.0 collective-permute-done.13.refs_17_
  68.8 11.0 %products.4 = (bf16[8,4,8,576]{3,2,1,0:T(8,128)(2,1)}, bf16[8,4,8,576]{3,2,1,0:T(8,128)(2,1)}) custom-call(s32[4]{0:T(128)} %pad_add_fusion.place_ref, f32[4]{0:T(128)} %fusion.30.scale_ref, bf16[128,1024]{1,0:T(8,128)(2,1)} %select_convert_fusion.turn_ref, bf16[1728,128]{1,0:T(8,128)(2,1)} %copy-done, bf16[1728,128]{1,0:T(8,128)(2,1)} %copy-done.1, ...), custom_call_target="tpu_custom_call" | custom-call | flops 905969664 | bytes 8388608 | tf_op jit(solution)/shard_map/products/pallas_call | solution.py:170
  79.8 1.6 %collective-permute-start.14 = (bf16[8,4,8,576]{3,2,1,0:T(8,128)(2,1)}, bf16[8,4,8,576]{3,2,1,0:T(8,128)(2,1)S(1)}, u32[]{:S(2)}, u32[]{:S(2)}) collective-permute-start(bf16[8,4,8,576]{3,2,1,0:T(8,128)(2,1)} %get-tuple-element.18), channel_id=1, source_target_pairs={{0,1},{1,0},{2,3},{3,2},{4,5},{5,4},{6,7},{7,6},{8,9},{9,8},{10,11... | collective-permute-start | bytes 884744 | tf_op jit(solution)/shard_map/ppermute | solution.py:202
  81.4 11.0 %products.5 = (bf16[8,4,8,576]{3,2,1,0:T(8,128)(2,1)}, bf16[8,4,8,576]{3,2,1,0:T(8,128)(2,1)}) custom-call(s32[4]{0:T(128)} %pad_add_fusion.place_ref, f32[4]{0:T(128)} %fusion.30.scale_ref, bf16[128,1024]{1,0:T(8,128)(2,1)} %select_convert_fusion.turn_ref, bf16[1728,128]{1,0:T(8,128)(2,1)} %collective-permute-done.15.refs_0_, ...), custom_call_target="tpu_custom_call" | custom-call | flops 905969664 | bytes 8388608 | tf_op jit(solution)/shard_map/products/pallas_call | solution.py:170
  92.4 0.6 collective-permute-start.17
  93.0 11.0 %products.6 = (bf16[8,4,8,576]{3,2,1,0:T(8,128)(2,1)}, bf16[8,4,8,576]{3,2,1,0:T(8,128)(2,1)}) custom-call(s32[4]{0:T(128)} %pad_add_fusion.place_ref, f32[4]{0:T(128)} %fusion.30.scale_ref, bf16[128,1024]{1,0:T(8,128)(2,1)} %select_convert_fusion.turn_ref, bf16[1728,128]{1,0:T(8,128)(2,1)} %collective-permute-done.18.refs_0_, ...), custom_call_target="tpu_custom_call" | custom-call | flops 905969664 | bytes 8388608 | tf_op jit(solution)/shard_map/products/pallas_call | solution.py:170
  104.0 1.6 %collective-permute-start.20 = (bf16[8,4,8,576]{3,2,1,0:T(8,128)(2,1)}, bf16[8,4,8,576]{3,2,1,0:T(8,128)(2,1)S(1)}, u32[]{:S(2)}, u32[]{:S(2)}) collective-permute-start(bf16[8,4,8,576]{3,2,1,0:T(8,128)(2,1)} %get-tuple-element.22), channel_id=1, source_target_pairs={{0,1},{1,0},{2,3},{3,2},{4,5},{5,4},{6,7},{7,6},{8,9},{9,8},{10,11... | collective-permute-start | bytes 884744 | tf_op jit(solution)/shard_map/ppermute | solution.py:202
  105.6 0.0 collective-permute-done.21.refs_0_
  105.6 0.0 collective-permute-done.22.refs_1_
  105.6 0.8 copy-done.12
  106.4 11.1 %products.7 = (bf16[8,4,8,576]{3,2,1,0:T(8,128)(2,1)}, bf16[8,4,8,576]{3,2,1,0:T(8,128)(2,1)}) custom-call(s32[4]{0:T(128)} %pad_add_fusion.place_ref, f32[4]{0:T(128)} %fusion.30.scale_ref, bf16[128,1024]{1,0:T(8,128)(2,1)} %select_convert_fusion.turn_ref, bf16[1728,128]{1,0:T(8,128)(2,1)} %copy-done.12, bf16[1728,128]{1,0:T(8,128)(2,1)} %collective-permute-done.22.refs_1_, ...), custom_call_target="tpu_custom_call" | custom-call | flops 905969664 | bytes 8388608 | tf_op jit(solution)/shard_map/products/pallas_call | solution.py:170
  117.5 0.6 collective-permute-start.23
  118.0 0.3 broadcast_in_dim.39
  118.3 0.1 copy-done.16
  118.7 0.4 copy-done.13
  119.2 0.3 copy-done.14
  119.5 5.4 %collective-permute-done.23 = bf16[8,4,8,576]{3,2,1,0:T(8,128)(2,1)S(1)} collective-permute-done((bf16[8,4,8,576]{3,2,1,0:T(8,128)(2,1)}, bf16[8,4,8,576]{3,2,1,0:T(8,128)(2,1)S(1)}, u32[]{:S(2)}, u32[]{:S(2)}) %collective-permute-start.23) | collective-permute-done | bytes 294944 | tf_op jit(solution)/shard_map/ppermute | solution.py:202
  124.9 0.0 copy-start.11
  124.9 1.5 %copy-done.11 = bf16[4,2,8,4,8,576]{5,4,3,2,1,0:T(8,128)(2,1)} copy-done((bf16[4,2,8,4,8,576]{5,4,3,2,1,0:T(8,128)(2,1)}, bf16[4,2,8,4,8,576]{5,4,3,2,1,0:T(8,128)(2,1)S(1)}, u32[]{:S(2)}) %copy-start.11) | copy-done | bytes 2359320
  (39 shorter events, 0.4 us)
Async XLA Ops:
  3.0 65.8 %copy-start = (bf16[1728,128]{1,0:T(8,128)(2,1)}, bf16[1728,128]{1,0:T(8,128)(2,1)S(1)}, u32[]{:S(2)}) copy-start(bf16[1728,128]{1,0:T(8,128)(2,1)S(1)} %get-tuple-element.15.refs_0_.refs_2_) | copy-start | bytes 1327108
  3.0 65.8 %copy-start.1 = (bf16[1728,128]{1,0:T(8,128)(2,1)}, bf16[1728,128]{1,0:T(8,128)(2,1)S(1)}, u32[]{:S(2)}) copy-start(bf16[1728,128]{1,0:T(8,128)(2,1)S(1)} %get-tuple-element.16.refs_1_.refs_3_) | copy-start | bytes 1327108
  3.0 14.0 %collective-permute-start.6 = (bf16[1728,128]{1,0:T(8,128)(2,1)S(1)}, bf16[1728,128]{1,0:T(8,128)(2,1)S(1)}, u32[]{:S(2)}, u32[]{:S(2)}) collective-permute-start(bf16[1728,128]{1,0:T(8,128)(2,1)S(1)} %get-tuple-element.15.refs_0_.refs_2_), channel_id=1, source_target_pairs={{0,1},{1,0},{2,3},{3,2},{4,5},{5,4},{6,7},{7,6},{8,9},{9,8},{10,11... | collective-permute-start | bytes 1327112 | tf_op jit(solution)/shard_map/ppermute | solution.py:202
  6.0 13.1 %collective-permute-start.3 = (bf16[1728,128]{1,0:T(8,128)(2,1)S(1)}, bf16[1728,128]{1,0:T(8,128)(2,1)S(1)}, u32[]{:S(2)}, u32[]{:S(2)}) collective-permute-start(bf16[1728,128]{1,0:T(8,128)(2,1)S(1)} %get-tuple-element.16.refs_1_.refs_3_), channel_id=1, source_target_pairs={{0,16},{8,24},{16,0},{24,8},{1,17},{9,25},{17,1},{25,9},{2,18},{10... | collective-permute-start | bytes 1327112 | tf_op jit(solution)/shard_map/ppermute | solution.py:199
  7.5 19.6 %collective-permute-start.2 = (bf16[1728,128]{1,0:T(8,128)(2,1)S(1)}, bf16[1728,128]{1,0:T(8,128)(2,1)S(1)}, u32[]{:S(2)}, u32[]{:S(2)}) collective-permute-start(bf16[1728,128]{1,0:T(8,128)(2,1)S(1)} %get-tuple-element.15.refs_0_.refs_2_), channel_id=1, source_target_pairs={{0,16},{8,24},{16,0},{24,8},{1,17},{9,25},{17,1},{25,9},{2,18},{10... | collective-permute-start | bytes 1327112 | tf_op jit(solution)/shard_map/ppermute | solution.py:199
  8.0 20.7 %collective-permute-start.7 = (bf16[1728,128]{1,0:T(8,128)(2,1)S(1)}, bf16[1728,128]{1,0:T(8,128)(2,1)S(1)}, u32[]{:S(2)}, u32[]{:S(2)}) collective-permute-start(bf16[1728,128]{1,0:T(8,128)(2,1)S(1)} %get-tuple-element.16.refs_1_.refs_3_), channel_id=1, source_target_pairs={{0,1},{1,0},{2,3},{3,2},{4,5},{5,4},{6,7},{7,6},{8,9},{9,8},{10,11... | collective-permute-start | bytes 1327112 | tf_op jit(solution)/shard_map/ppermute | solution.py:202
  8.1 22.1 %collective-permute-start = (bf16[1728,128]{1,0:T(8,128)(2,1)S(1)}, bf16[1728,128]{1,0:T(8,128)(2,1)S(1)}, u32[]{:S(2)}, u32[]{:S(2)}) collective-permute-start(bf16[1728,128]{1,0:T(8,128)(2,1)S(1)} %get-tuple-element.15.refs_0_.refs_2_), channel_id=1, source_target_pairs={{0,8},{8,0},{16,24},{24,16},{1,9},{9,1},{17,25},{25,17},{2,10},{10... | collective-permute-start | bytes 1327112 | tf_op jit(solution)/shard_map/ppermute | solution.py:196
  17.0 51.8 %copy-start.2 = (bf16[1728,128]{1,0:T(8,128)(2,1)}, bf16[1728,128]{1,0:T(8,128)(2,1)S(1)}, u32[]{:S(2)}) copy-start(bf16[1728,128]{1,0:T(8,128)(2,1)S(1)} %collective-permute-done.6.refs_10_) | copy-start | bytes 1327108
  17.0 13.8 %collective-permute-start.1 = (bf16[1728,128]{1,0:T(8,128)(2,1)S(1)}, bf16[1728,128]{1,0:T(8,128)(2,1)S(1)}, u32[]{:S(2)}, u32[]{:S(2)}) collective-permute-start(bf16[1728,128]{1,0:T(8,128)(2,1)S(1)} %get-tuple-element.16.refs_1_.refs_3_), channel_id=1, source_target_pairs={{0,8},{8,0},{16,24},{24,16},{1,9},{9,1},{17,25},{25,17},{2,10},{10... | collective-permute-start | bytes 1327112 | tf_op jit(solution)/shard_map/ppermute | solution.py:196
  19.1 49.7 %copy-start.3 = (bf16[1728,128]{1,0:T(8,128)(2,1)}, bf16[1728,128]{1,0:T(8,128)(2,1)S(1)}, u32[]{:S(2)}) copy-start(bf16[1728,128]{1,0:T(8,128)(2,1)S(1)} %collective-permute-done.3.refs_7_) | copy-start | bytes 1327108
  19.1 14.7 %collective-permute-start.15 = (bf16[1728,128]{1,0:T(8,128)(2,1)S(1)}, bf16[1728,128]{1,0:T(8,128)(2,1)}, u32[]{:S(2)}, u32[]{:S(2)}) collective-permute-start(bf16[1728,128]{1,0:T(8,128)(2,1)S(1)} %get-tuple-element.15.refs_0_.refs_2_), channel_id=1, source_target_pairs={{0,2},{1,3},{2,4},{3,5},{4,6},{5,7},{6,0},{7,1},{8,10},{9,11},{10,... | collective-permute-start | bytes 1327112 | tf_op jit(solution)/shard_map/ppermute | solution.py:205
  27.1 41.7 %copy-start.4 = (bf16[1728,128]{1,0:T(8,128)(2,1)}, bf16[1728,128]{1,0:T(8,128)(2,1)S(1)}, u32[]{:S(2)}) copy-start(bf16[1728,128]{1,0:T(8,128)(2,1)S(1)} %collective-permute-done.2.refs_6_) | copy-start | bytes 1327108
  27.1 14.5 %collective-permute-start.16 = (bf16[1728,128]{1,0:T(8,128)(2,1)S(1)}, bf16[1728,128]{1,0:T(8,128)(2,1)}, u32[]{:S(2)}, u32[]{:S(2)}) collective-permute-start(bf16[1728,128]{1,0:T(8,128)(2,1)S(1)} %get-tuple-element.16.refs_1_.refs_3_), channel_id=1, source_target_pairs={{0,2},{1,3},{2,4},{3,5},{4,6},{5,7},{6,0},{7,1},{8,10},{9,11},{10,... | collective-permute-start | bytes 1327112 | tf_op jit(solution)/shard_map/ppermute | solution.py:205
  28.7 40.1 %copy-start.5 = (bf16[1728,128]{1,0:T(8,128)(2,1)}, bf16[1728,128]{1,0:T(8,128)(2,1)S(1)}, u32[]{:S(2)}) copy-start(bf16[1728,128]{1,0:T(8,128)(2,1)S(1)} %collective-permute-done.7.refs_11_) | copy-start | bytes 1327108
  28.7 12.9 %collective-permute-start.10 = (bf16[1728,128]{1,0:T(8,128)(2,1)S(1)}, bf16[1728,128]{1,0:T(8,128)(2,1)}, u32[]{:S(2)}, u32[]{:S(2)}) collective-permute-start(bf16[1728,128]{1,0:T(8,128)(2,1)S(1)} %collective-permute-done.6.refs_10_), channel_id=1, source_target_pairs={{0,16},{8,24},{16,0},{24,8},{1,17},{9,25},{17,1},{25,9},{2,18},{10... | collective-permute-start | bytes 1327112 | tf_op jit(solution)/shard_map/ppermute | solution.py:199
  30.2 38.6 %copy-start.6 = (bf16[1728,128]{1,0:T(8,128)(2,1)}, bf16[1728,128]{1,0:T(8,128)(2,1)S(1)}, u32[]{:S(2)}) copy-start(bf16[1728,128]{1,0:T(8,128)(2,1)S(1)} %collective-permute-done.refs_4_) | copy-start | bytes 1327108
  30.2 12.0 %collective-permute-start.11 = (bf16[1728,128]{1,0:T(8,128)(2,1)S(1)}, bf16[1728,128]{1,0:T(8,128)(2,1)}, u32[]{:S(2)}, u32[]{:S(2)}) collective-permute-start(bf16[1728,128]{1,0:T(8,128)(2,1)S(1)} %collective-permute-done.3.refs_7_), channel_id=1, source_target_pairs={{0,1},{1,0},{2,3},{3,2},{4,5},{5,4},{6,7},{7,6},{8,9},{9,8},{10,11... | collective-permute-start | bytes 1327112 | tf_op jit(solution)/shard_map/ppermute | solution.py:202
  30.8 38.0 %copy-start.7 = (bf16[1728,128]{1,0:T(8,128)(2,1)}, bf16[1728,128]{1,0:T(8,128)(2,1)S(1)}, u32[]{:S(2)}) copy-start(bf16[1728,128]{1,0:T(8,128)(2,1)S(1)} %collective-permute-done.1.refs_5_) | copy-start | bytes 1327108
  30.8 11.5 %collective-permute-start.5 = (bf16[1728,128]{1,0:T(8,128)(2,1)S(1)}, bf16[1728,128]{1,0:T(8,128)(2,1)S(1)}, u32[]{:S(2)}, u32[]{:S(2)}) collective-permute-start(bf16[1728,128]{1,0:T(8,128)(2,1)S(1)} %collective-permute-done.3.refs_7_), channel_id=1, source_target_pairs={{0,8},{8,0},{16,24},{24,16},{1,9},{9,1},{17,25},{25,17},{2,10},{10... | collective-permute-start | bytes 1327112 | tf_op jit(solution)/shard_map/ppermute | solution.py:196
  33.7 10.0 %collective-permute-start.8 = (bf16[1728,128]{1,0:T(8,128)(2,1)S(1)}, bf16[1728,128]{1,0:T(8,128)(2,1)S(1)}, u32[]{:S(2)}, u32[]{:S(2)}) collective-permute-start(bf16[1728,128]{1,0:T(8,128)(2,1)S(1)} %collective-permute-done.6.refs_10_), channel_id=1, source_target_pairs={{0,8},{8,0},{16,24},{24,16},{1,9},{9,1},{17,25},{25,17},{2,10},{10... | collective-permute-start | bytes 1327112 | tf_op jit(solution)/shard_map/ppermute | solution.py:196
  41.6 2.2 %collective-permute-start.4 = (bf16[1728,128]{1,0:T(8,128)(2,1)S(1)}, bf16[1728,128]{1,0:T(8,128)(2,1)S(1)}, u32[]{:S(2)}, u32[]{:S(2)}) collective-permute-start(bf16[1728,128]{1,0:T(8,128)(2,1)S(1)} %collective-permute-done.2.refs_6_), channel_id=1, source_target_pairs={{0,8},{8,0},{16,24},{24,16},{1,9},{9,1},{17,25},{25,17},{2,10},{10... | collective-permute-start | bytes 1327112 | tf_op jit(solution)/shard_map/ppermute | solution.py:196
  41.6 27.1 %collective-permute-start.9 = (bf16[1728,128]{1,0:T(8,128)(2,1)S(1)}, bf16[1728,128]{1,0:T(8,128)(2,1)}, u32[]{:S(2)}, u32[]{:S(2)}) collective-permute-start(bf16[1728,128]{1,0:T(8,128)(2,1)S(1)} %collective-permute-done.7.refs_11_), channel_id=1, source_target_pairs={{0,8},{8,0},{16,24},{24,16},{1,9},{9,1},{17,25},{25,17},{2,10},{10... | collective-permute-start | bytes 1327112 | tf_op jit(solution)/shard_map/ppermute | solution.py:196
  42.2 15.1 %collective-permute-start.18 = (bf16[1728,128]{1,0:T(8,128)(2,1)}, bf16[1728,128]{1,0:T(8,128)(2,1)}, u32[]{:S(2)}, u32[]{:S(2)}) collective-permute-start(bf16[1728,128]{1,0:T(8,128)(2,1)} %collective-permute-done.15.refs_0_), channel_id=1, source_target_pairs={{0,2},{1,3},{2,4},{3,5},{4,6},{5,7},{6,0},{7,1},{8,10},{9,11},{10,... | collective-permute-start | bytes 1327112 | tf_op jit(solution)/shard_map/ppermute | solution.py:205
  42.2 1.5 %copy-start.8 = (bf16[1728,128]{1,0:T(8,128)(2,1)}, bf16[1728,128]{1,0:T(8,128)(2,1)S(1)}, u32[]{:S(2)}) copy-start(bf16[1728,128]{1,0:T(8,128)(2,1)S(1)} %collective-permute-done.5.refs_9_) | copy-start | bytes 1327108
  42.2 24.6 %collective-permute-start.19 = (bf16[1728,128]{1,0:T(8,128)(2,1)}, bf16[1728,128]{1,0:T(8,128)(2,1)}, u32[]{:S(2)}, u32[]{:S(2)}) collective-permute-start(bf16[1728,128]{1,0:T(8,128)(2,1)} %collective-permute-done.16.refs_1_), channel_id=1, source_target_pairs={{0,2},{1,3},{2,4},{3,5},{4,6},{5,7},{6,0},{7,1},{8,10},{9,11},{10,... | collective-permute-start | bytes 1327112 | tf_op jit(solution)/shard_map/ppermute | solution.py:205
  43.7 0.8 copy-start.9
  43.7 25.0 %collective-permute-start.12 = (bf16[1728,128]{1,0:T(8,128)(2,1)}, bf16[1728,128]{1,0:T(8,128)(2,1)}, u32[]{:S(2)}, u32[]{:S(2)}) collective-permute-start(bf16[1728,128]{1,0:T(8,128)(2,1)} %collective-permute-done.10.refs_14_), channel_id=1, source_target_pairs={{0,8},{8,0},{16,24},{24,16},{1,9},{9,1},{17,25},{25,17},{2,10},{10... | collective-permute-start | bytes 1327112 | tf_op jit(solution)/shard_map/ppermute | solution.py:196
  43.8 0.9 copy-start.10
  43.8 24.9 %collective-permute-start.13 = (bf16[1728,128]{1,0:T(8,128)(2,1)}, bf16[1728,128]{1,0:T(8,128)(2,1)}, u32[]{:S(2)}, u32[]{:S(2)}) collective-permute-start(bf16[1728,128]{1,0:T(8,128)(2,1)} %collective-permute-done.11.refs_15_), channel_id=1, source_target_pairs={{0,8},{8,0},{16,24},{24,16},{1,9},{9,1},{17,25},{25,17},{2,10},{10... | collective-permute-start | bytes 1327112 | tf_op jit(solution)/shard_map/ppermute | solution.py:196
  57.3 48.3 %collective-permute-start.21 = (bf16[1728,128]{1,0:T(8,128)(2,1)}, bf16[1728,128]{1,0:T(8,128)(2,1)S(1)}, u32[]{:S(2)}, u32[]{:S(2)}) collective-permute-start(bf16[1728,128]{1,0:T(8,128)(2,1)} %collective-permute-done.18.refs_0_), channel_id=1, source_target_pairs={{0,2},{1,3},{2,4},{3,5},{4,6},{5,7},{6,0},{7,1},{8,10},{9,11},{10,... | collective-permute-start | bytes 1327112 | tf_op jit(solution)/shard_map/ppermute | solution.py:205
  66.8 38.8 %collective-permute-start.22 = (bf16[1728,128]{1,0:T(8,128)(2,1)}, bf16[1728,128]{1,0:T(8,128)(2,1)}, u32[]{:S(2)}, u32[]{:S(2)}) collective-permute-start(bf16[1728,128]{1,0:T(8,128)(2,1)} %collective-permute-done.19.refs_1_), channel_id=1, source_target_pairs={{0,2},{1,3},{2,4},{3,5},{4,6},{5,7},{6,0},{7,1},{8,10},{9,11},{10,... | collective-permute-start | bytes 1327112 | tf_op jit(solution)/shard_map/ppermute | solution.py:205
  79.8 38.7 %collective-permute-start.14 = (bf16[8,4,8,576]{3,2,1,0:T(8,128)(2,1)}, bf16[8,4,8,576]{3,2,1,0:T(8,128)(2,1)S(1)}, u32[]{:S(2)}, u32[]{:S(2)}) collective-permute-start(bf16[8,4,8,576]{3,2,1,0:T(8,128)(2,1)} %get-tuple-element.18), channel_id=1, source_target_pairs={{0,1},{1,0},{2,3},{3,2},{4,5},{5,4},{6,7},{7,6},{8,9},{9,8},{10,11... | collective-permute-start | bytes 884744 | tf_op jit(solution)/shard_map/ppermute | solution.py:202
  92.4 26.2 %collective-permute-start.17 = (bf16[8,4,8,576]{3,2,1,0:T(8,128)(2,1)}, bf16[8,4,8,576]{3,2,1,0:T(8,128)(2,1)S(1)}, u32[]{:S(2)}, u32[]{:S(2)}) collective-permute-start(bf16[8,4,8,576]{3,2,1,0:T(8,128)(2,1)} %get-tuple-element.20), channel_id=1, source_target_pairs={{0,1},{1,0},{2,3},{3,2},{4,5},{5,4},{6,7},{7,6},{8,9},{9,8},{10,11... | collective-permute-start | bytes 884744 | tf_op jit(solution)/shard_map/ppermute | solution.py:202
  104.0 15.1 %collective-permute-start.20 = (bf16[8,4,8,576]{3,2,1,0:T(8,128)(2,1)}, bf16[8,4,8,576]{3,2,1,0:T(8,128)(2,1)S(1)}, u32[]{:S(2)}, u32[]{:S(2)}) collective-permute-start(bf16[8,4,8,576]{3,2,1,0:T(8,128)(2,1)} %get-tuple-element.22), channel_id=1, source_target_pairs={{0,1},{1,0},{2,3},{3,2},{4,5},{5,4},{6,7},{7,6},{8,9},{9,8},{10,11... | collective-permute-start | bytes 884744 | tf_op jit(solution)/shard_map/ppermute | solution.py:202
  105.6 0.8 copy-start.12
  117.5 1.0 copy-start.16
  117.5 1.1 copy-start.15
  117.5 7.4 %collective-permute-start.23 = (bf16[8,4,8,576]{3,2,1,0:T(8,128)(2,1)}, bf16[8,4,8,576]{3,2,1,0:T(8,128)(2,1)S(1)}, u32[]{:S(2)}, u32[]{:S(2)}) collective-permute-start(bf16[8,4,8,576]{3,2,1,0:T(8,128)(2,1)} %get-tuple-element.24), channel_id=1, source_target_pairs={{0,1},{1,0},{2,3},{3,2},{4,5},{5,4},{6,7},{7,6},{8,9},{9,8},{10,11... | collective-permute-start | bytes 884744 | tf_op jit(solution)/shard_map/ppermute | solution.py:202
  118.0 1.0 copy-start.13
  118.4 1.0 copy-start.14
  124.9 1.5 %copy-start.11 = (bf16[4,2,8,4,8,576]{5,4,3,2,1,0:T(8,128)(2,1)}, bf16[4,2,8,4,8,576]{5,4,3,2,1,0:T(8,128)(2,1)S(1)}, u32[]{:S(2)}) copy-start(bf16[4,2,8,4,8,576]{5,4,3,2,1,0:T(8,128)(2,1)S(1)} %bitcast_dynamic-update-slice_fusion) | copy-start | bytes 7077892

commit v2 on v1

v2 whole, which is shorter than its diff:
```python
import functools
import math

import jax
import jax.numpy as jnp
from jax import lax
from jax.experimental import pallas as pl
from jax.experimental.pallas import tpu as pltpu
from jax.sharding import PartitionSpec as P

GROUPS = 8
TILES = 27
PAIR_ROWS = 13 * 16
GROUP_ROWS = TILES * 16
BLOCK_ROWS = GROUPS * GROUP_ROWS
HALF_ROWS = BLOCK_ROWS // 2
STATIONS = 8
PACE = 40 * 2**20
F32 = jnp.float32
BF16 = jnp.bfloat16


def prepare_kernel(x_ref, whole_ref, first_ref, second_ref, d_ref):
    count, segs = x_ref.shape[0], x_ref.shape[1]
    tail = segs - 256
    if count < STATIONS:
        d_ref[...] = jnp.zeros_like(d_ref)
    lane_group = lax.broadcasted_iota(jnp.int32, (8, 128), 1) // 32
    for i in range(count):
        values = x_ref[i].astype(F32)
        power = jnp.mean(values * values, axis=1, keepdims=True)
        white = (values * lax.rsqrt(power + 1e-06)).astype(BF16).astype(F32)
        main = white[:256].T
        rest = jnp.concatenate([white[256:], jnp.zeros((32 - tail, 192), F32)], axis=0)
        rest = jnp.concatenate([rest] * 4, axis=0).T
        for group in range(4):
            half, pair = group // 2, group % 2
            row = pair * PAIR_ROWS + half * 8 + i
            for line in range(6):
                rows = slice(line * 32 + group * 8, line * 32 + group * 8 + 8)
                for side in range(2):
                    tile = line * 2 + side
                    d_ref[pl.ds(row + tile * 16, 8, stride=GROUP_ROWS), :] = main[
                        rows, side * 128 : side * 128 + 128
                    ]
            first = jnp.zeros((8, 128), F32)
            for line in range(4):
                rows = slice(line * 32 + group * 8, line * 32 + group * 8 + 8)
                first = jnp.where(lane_group == line, rest[rows], first)
            d_ref[pl.ds(row + 12 * 16, 8, stride=GROUP_ROWS), :] = first
        for half in range(2):
            last = jnp.zeros((8, 128), F32)
            for pair in range(2):
                for part in range(2):
                    start = (4 + part) * 32 + (half * 2 + pair) * 8
                    last = jnp.where(
                        lane_group == pair * 2 + part, rest[start : start + 8], last
                    )
            d_ref[pl.ds(26 * 16 + half * 8 + i, 8, stride=GROUP_ROWS), :] = last
    for h, half_ref in enumerate((first_ref, second_ref)):
        rows = slice(h * HALF_ROWS, (h + 1) * HALF_ROWS)
        value = d_ref[rows].astype(BF16)
        half_ref[...] = value
        whole_ref[rows] = value


def in_vmem(array):
    return pltpu.with_memory_space_constraint(array, pltpu.VMEM)


def prepare(spectra):
    half = jax.ShapeDtypeStruct((HALF_ROWS, 128), BF16)
    whole = jax.ShapeDtypeStruct((BLOCK_ROWS, 128), BF16)
    return pl.pallas_call(
        prepare_kernel,
        out_shape=(whole, half, half),
        scratch_shapes=[pltpu.VMEM((BLOCK_ROWS, 128), F32)],
        compiler_params=pltpu.CompilerParams(vmem_limit_bytes=16 * 2**20),
        name="prepare",
    )(spectra)


def turn_matrix():
    source = lax.broadcasted_iota(jnp.int32, (128, 1024), 0)
    column = lax.broadcasted_iota(jnp.int32, (128, 1024), 1)
    block, lane = column // 128, column % 128
    half, imag, slot = block // 4, (block // 2) % 2, block % 2
    part, seg = (lane % 64) // 32, lane % 32
    wanted = half * 64 + jnp.where(imag == 1, 1 - part, part) * 32 + seg
    sign = jnp.where((imag == 1) & (part == 1), -1.0, 1.0)
    hit = (source == wanted) & (lane // 64 == slot)
    return jnp.where(hit, sign, 0.0).astype(BF16)


def nt(left, right):
    return lax.dot_general(left, right, (((1,), (1,)), ((), ())), preferred_element_type=F32)


def products_kernel(parts, src_count, place_ref, scale_ref, turn_ref, *refs):
    operands, outs = refs[: sum(parts)], refs[sum(parts) : sum(parts) + 2]
    own_ref, other_ref = outs
    sums, turned_ref = refs[sum(parts) + 2 :]
    count = own_ref.shape[0]
    block_count = len(parts) - 1
    lanes = block_count * 16
    pieces = []
    for n in parts:
        of, operands = operands[:n], operands[n:]
        pieces.append([(of[h], 0) if n == 2 else (of[0], h * HALF_ROWS) for h in range(2)])

    for h in range(2):
        left, offset = pieces[0][h]
        steps = GROUPS // 2
        tails = []
        for q in range(steps):
            for tile in (12, 25, 26):
                start = offset + q * GROUP_ROWS + tile * 16
                tails.append(left[start : start + 16, :])
        turned_ref[...] = jnp.dot(
            jnp.concatenate(tails, axis=0), turn_ref[...], preferred_element_type=F32
        ).astype(BF16)
        for q in range(steps):

            def tile_of(tile):
                start = q * GROUP_ROWS + tile * 16
                return jnp.concatenate(
                    [ref[at + start : at + start + 16, :] for ref, at in (p[h] for p in pieces[1:])],
                    axis=0,
                )

            last_right = tile_of(26)
            for pair in range(2):
                base = offset + q * GROUP_ROWS + pair * PAIR_ROWS
                tiles = [left[base + t * 16 : base + t * 16 + 16, :] for t in range(12)]
                lines = []
                for a in range(3):
                    real, imag = tiles[a * 4 : a * 4 + 2], tiles[a * 4 + 2 : a * 4 + 4]
                    lines.append(jnp.concatenate(real + imag, axis=1))
                    lines.append(jnp.concatenate(imag + [-real[0], -real[1]], axis=1))
                main = jnp.concatenate(lines, axis=0)
                rest_right = tile_of(pair * 13 + 12)
                for b in range(3):
                    slot = b if b < 2 else pair
                    rest = []
                    for a in range(3):
                        row, half = (q * 3 + pair, a) if a < 2 else (q * 3 + 2, pair)
                        for e in range(2):
                            at = (half * 4 + e * 2 + slot) * 128
                            rest.append(turned_ref[row * 16 : row * 16 + 16, at : at + 128])
                    rest = jnp.concatenate(rest, axis=0)
                    weights = [tile_of(pair * 13 + b * 4 + t) for t in range(4)]
                    weights.append(rest_right if b < 2 else last_right)
                    result = nt(
                        jnp.concatenate([main, rest], axis=1), jnp.concatenate(weights, axis=1)
                    )
                    for a in range(3):
                        for e in range(2):
                            for half in range(2):
                                row = (a * 2 + e) * 16 + half * 8
                                bin_ = half * 16 + pair * 8 + h * steps + q
                                at = (a * 6 + b * 2 + e) * 32 + bin_
                                for m in range(lanes // 128):
                                    sums[
                                        pl.ds(m * STATIONS * 576 + at, 8, stride=576), :
                                    ] = result[row : row + 8, m * 128 : m * 128 + 128]

    bin_half = (lax.broadcasted_iota(jnp.int32, (8, 576), 1) % 32) < 16
    for i in range(count):
        for m in range(lanes // 128):
            start = (m * STATIONS + i) * 576
            turned = sums[start : start + 576, :].T
            for n in range(8):
                low, high = turned[n * 16 : n * 16 + 8], turned[n * 16 + 8 : n * 16 + 16]
                at = place_ref[(m * 8 + n) % src_count]
                value = (jnp.where(bin_half, low, high) * scale_ref[at]).astype(BF16)
                out = own_ref if m * 8 + n < src_count else other_ref
                out[i, at] = value[: out.shape[2]]


def products(place, scale, turn, source, blocks, count, src_count):
    out = jax.ShapeDtypeStruct((count, src_count, count, 576), BF16)
    n = len(blocks)
    parts = tuple(len(block) for block in (source, *blocks))
    smem, vmem = pl.BlockSpec(memory_space=pltpu.SMEM), pl.BlockSpec(memory_space=pltpu.VMEM)
    operands = [in_vmem(piece) for block in (source, *blocks) for piece in block]
    return pl.pallas_call(
        functools.partial(products_kernel, parts, src_count),
        out_shape=(out, out),
        in_specs=[smem, smem, vmem] + [vmem] * len(operands),
        out_specs=(vmem, vmem),
        scratch_shapes=[
            pltpu.VMEM((n // 8 * STATIONS * 576, 128), F32),
            pltpu.VMEM((GROUPS // 2 * 3 * 16, 1024), BF16),
        ],
        compiler_params=pltpu.CompilerParams(vmem_limit_bytes=24 * 2**20),
        cost_estimate=pl.CostEstimate(
            flops=2 * 16 * 3 * 96 * 16 * n * 768, bytes_accessed=8 * 2**20, transcendentals=0
        ),
        name="products",
    )(place, scale, turn, *operands)


def paced(array):
    return pl.pallas_call(
        lambda x_ref, o_ref: None,
        out_shape=jax.ShapeDtypeStruct(array.shape, array.dtype),
        in_specs=[pl.BlockSpec(memory_space=pl.ANY)],
        out_specs=pl.BlockSpec(memory_space=pl.ANY),
        input_output_aliases={0: 0},
        cost_estimate=pl.CostEstimate(flops=0, bytes_accessed=PACE, transcendentals=0),
        name="paced",
    )(array)


def on_device(spectra, block_mask):
    count, segs = spectra.shape[0], spectra.shape[1]
    src_count, rcv_count = lax.axis_size("src"), lax.axis_size("rcv")
    src, rcv = lax.axis_index("src"), lax.axis_index("rcv")
    highs, steps = src_count // 2, rcv_count // 2

    def over_core(half):
        return lax.ppermute(half, "src", [(s, s ^ 1) for s in range(src_count)])

    def over_high(half):
        return lax.ppermute(half, "src", [(s, (s + 2) % src_count) for s in range(src_count)])

    def over_x(half):
        return lax.ppermute(half, "rcv", [(r, r ^ 1) for r in range(rcv_count)])

    def over_z(half):
        return lax.ppermute(half, "rcv", [(r, (r + 2) % rcv_count) for r in range(rcv_count)])

    scale = lax.dynamic_index_in_dim(block_mask, src, 0, keepdims=False).astype(F32) * (
        1.0 / math.sqrt(segs)
    )
    whole, *halves = prepare(spectra)
    sources = [halves]
    for k in range(steps - 1):
        pace = paced if k < steps - 2 else (lambda half: half)
        sources.append([pace(over_z(half)) for half in sources[-1]])
    high, beside = whole, over_x(whole)
    mine, theirs = [(high,)], [(beside,)]
    for _ in range(highs - 1):
        first = beside[:HALF_ROWS]
        high, first = lax.optimization_barrier((over_high(high), first))
        beside = over_high(first)
        mine.append((high,))
        theirs.append((beside, over_x(high[HALF_ROWS:])))
    blocks = []
    for line in (mine, theirs):
        for block in line:
            blocks += [block, tuple(over_core(piece) for piece in block)]
    place = jnp.stack(
        [((src // 2 - k + highs) % highs) * 2 + lax.rem(src + c, 2) for k in range(highs) for c in range(2)]
    ).astype(jnp.int32)
    turn = turn_matrix()
    result = jnp.zeros((steps, 2, count, src_count, count, 576), BF16)
    x, z = rcv % 2, rcv // 2
    for k, source in enumerate(sources):
        kept, sent = products(place, scale, turn, source, blocks, count, src_count)
        got = over_x(sent)
        at = lax.rem(z - k + steps, steps)
        result = lax.dynamic_update_slice(result, kept[None, None], (at, x, 0, 0, 0, 0))
        result = lax.dynamic_update_slice(result, got[None, None], (at, 1 - x, 0, 0, 0, 0))
    return result.reshape(steps * 2 * count, src_count, count, 576)


def solution(mesh):
    placed = (P(("src", "rcv"), None, None), P())
    return jax.shard_map(
        on_device,
        mesh=mesh,
        in_specs=placed,
        out_specs=P("src", None, "rcv", None),
        check_vma=False,
    )
```

time: 127 us -> 95.7 us (0.75)
  Pallas kernels: 45.6 us -> 27.9 us
  waiting for transfers between devices: 54.9 us -> 44.3 us
  starting transfers between devices: 17.3 us -> 13.5 us
  local copies, waits for them, and re-layouts: 5.58 us -> 7.95 us
    pallas_call x5 -> x9, Pallas kernels: 45.6 us -> 27.9 us  [the longest x4 25.6 us: products(): pl.pallas_call(functools.partial(products_kernel, parts, src_count), out_...]
    ppermute x3 -> x2, waiting for transfers between devices: 8.53 us -> 0.01 us  [over_high(): lax.ppermute(half, 'src', [(s, (s + 2) % src_count) for s in range(src_co...]
    ppermute x7 -> x6, waiting for transfers between devices: 14.3 us -> 7.16 us  [over_x(): return lax.ppermute(half, 'rcv', [(r, r ^ 1) for r in range(rcv_count)])]
    ppermute x6, waiting for transfers between devices: 32.1 us -> 35.3 us  [over_z(): lax.ppermute(half, 'rcv', [(r, (r + 2) % rcv_count) for r in range(rcv_co...]
    unnamed x35 -> x17, local copies, waits for them, and re-layouts: 4.98 us -> 7.26 us
    ppermute x8 -> x5, waiting for transfers between devices: 0.02 us -> 1.81 us  [over_core(): return lax.ppermute(half, 'src', [(s, s ^ 1) for s in range(src_count)])]
    ppermute x3 -> x2, starting transfers between devices: 3.55 us -> 1.81 us  [over_high(): lax.ppermute(half, 'src', [(s, (s + 2) % src_count) for s in range(src_co...]
    ppermute x6, starting transfers between devices: 4.68 us -> 3.16 us  [over_z(): lax.ppermute(half, 'rcv', [(r, (r + 2) % rcv_count) for r in range(rcv_co...]
  transfers between devices with their start and end apart: 24 -> 19, of which waited for: 8 -> 7; matrix products, arithmetic and copies ran while one was open for 3% -> 2% of each run, Pallas kernels for 35% -> 27%
where the time goes in v2:
time: 95.7 us; the launch traced here: 95.4 us
  waiting for transfers between devices  44.3 us (46%)
  Pallas kernels  27.9 us (29%)
  starting transfers between devices  13.5 us (14%)
  local copies, waits for them, and re-layouts  7.95 us (8%)
  other arithmetic  1.68 us (2%)
    ppermute x6, waiting for transfers between devices, over_z(): lax.ppermute(half, 'rcv', [(r, (r + 2) % rcv_count) for r in range(rcv_co...  35.3 us
    pallas_call x4, Pallas kernels, products(): pl.pallas_call(functools.partial(products_kernel, parts, src_count), out_...  25.6 us
    ppermute x6, starting transfers between devices, over_x(): return lax.ppermute(half, 'rcv', [(r, r ^ 1) for r in range(rcv_count)])  7.84 us
    unnamed x17, local copies, waits for them, and re-layouts  7.26 us
    ppermute x6, waiting for transfers between devices, over_x(): return lax.ppermute(half, 'rcv', [(r, r ^ 1) for r in range(rcv_count)])  7.16 us
    ppermute x6, starting transfers between devices, over_z(): lax.ppermute(half, 'rcv', [(r, (r + 2) % rcv_count) for r in range(rcv_co...  3.16 us
    pallas_call x1, Pallas kernels, prepare(): pl.pallas_call(prepare_kernel, out_shape=(whole, half, half), scratch_sha...  2.25 us
  transfers between devices with their start and end apart: 19, of which 7 were waited for; matrix products, arithmetic and copies ran while one was open for 2% of the time, Pallas kernels for 27%

profile of v2, /device:TPU:0, one launch (start us, length us, event | category | flops | bytes accessed | tf_op | source)
XLA Modules:
  0.0 95.4 jit_solution(15242360194461994068)
XLA Ops:
  0.0 1.5 %copy.7.x_ref = bf16[8,287,192]{2,1,0:T(8,128)(2,1)S(1)} copy(bf16[8,287,192]{2,0,1:T(8,128)(2,1)} %param.2) | data formatting | bytes 1763328 | tf_op args[0]
  1.5 2.3 %prepare.1 = (bf16[3456,128]{1,0:T(8,128)(2,1)S(1)}, bf16[1728,128]{1,0:T(8,128)(2,1)S(1)}, bf16[1728,128]{1,0:T(8,128)(2,1)}) custom-call(bf16[8,287,192]{2,1,0:T(8,128)(2,1)S(1)} %copy.7.x_ref), custom_call_target="tpu_custom_call" | custom-call | tf_op jit(solution)/shard_map/prepare/pallas_call | solution.py:74
  3.8 2.9 %collective-permute-start.2 = (bf16[3456,128]{1,0:T(8,128)(2,1)S(1)}, bf16[3456,128]{1,0:T(8,128)(2,1)S(1)}, u32[]{:S(2)}, u32[]{:S(2)}) collective-permute-start(bf16[3456,128]{1,0:T(8,128)(2,1)S(1)} %get-tuple-element.20.refs_2_), channel_id=1, source_target_pairs={{0,1},{1,0},{2,3},{3,2},{4,5},{5,4},{6,7},{7,6},{8,9},{9,8},{10,11... | collective-permute-start | bytes 2654216 | tf_op jit(solution)/shard_map/ppermute | solution.py:228
  6.7 1.5 %collective-permute-start.1 = (bf16[3456,128]{1,0:T(8,128)(2,1)S(1)}, bf16[3456,128]{1,0:T(8,128)(2,1)S(1)}, u32[]{:S(2)}, u32[]{:S(2)}) collective-permute-start(bf16[3456,128]{1,0:T(8,128)(2,1)S(1)} %get-tuple-element.20.refs_2_), channel_id=1, source_target_pairs={{0,16},{8,24},{16,0},{24,8},{1,17},{9,25},{17,1},{25,9},{2,18},{10... | collective-permute-start | bytes 2654216 | tf_op jit(solution)/shard_map/ppermute | solution.py:225
  8.2 1.6 %collective-permute-start.10 = (bf16[1728,128]{1,0:T(8,128)(2,1)S(1)}, bf16[1728,128]{1,0:T(8,128)(2,1)S(1)}, u32[]{:S(2)}, u32[]{:S(2)}) collective-permute-start(bf16[1728,128]{1,0:T(8,128)(2,1)S(1)} %get-tuple-element.18.refs_0_), channel_id=1, source_target_pairs={{0,2},{1,3},{2,4},{3,5},{4,6},{5,7},{6,0},{7,1},{8,10},{9,11},{10,... | collective-permute-start | bytes 1327112 | tf_op jit(solution)/shard_map/ppermute | solution.py:231
  9.8 0.0 copy-start.5
  9.8 0.8 copy-done.5
  10.6 1.6 %collective-permute-start.11 = (bf16[1728,128]{1,0:T(8,128)(2,1)}, bf16[1728,128]{1,0:T(8,128)(2,1)S(1)}, u32[]{:S(2)}, u32[]{:S(2)}) collective-permute-start(bf16[1728,128]{1,0:T(8,128)(2,1)} %get-tuple-element.19.refs_1_), channel_id=1, source_target_pairs={{0,2},{1,3},{2,4},{3,5},{4,6},{5,7},{6,0},{7,1},{8,10},{9,11},{10,... | collective-permute-start | bytes 1327112 | tf_op jit(solution)/shard_map/ppermute | solution.py:231
  12.1 11.0 %collective-permute-done.10.x_ref = bf16[1728,128]{1,0:T(8,128)(2,1)S(1)} collective-permute-done((bf16[1728,128]{1,0:T(8,128)(2,1)S(1)}, bf16[1728,128]{1,0:T(8,128)(2,1)S(1)}, u32[]{:S(2)}, u32[]{:S(2)}) %collective-permute-start.10) | collective-permute-done | bytes 442400 | tf_op jit(solution)/shard_map/ppermute | solution.py:231
  23.1 0.0 copy-start.3
  23.1 0.8 copy-done.3
  23.9 0.0 collective-permute-start.13
  23.9 8.7 %collective-permute-done.11.x_ref = bf16[1728,128]{1,0:T(8,128)(2,1)S(1)} collective-permute-done((bf16[1728,128]{1,0:T(8,128)(2,1)}, bf16[1728,128]{1,0:T(8,128)(2,1)S(1)}, u32[]{:S(2)}, u32[]{:S(2)}) %collective-permute-start.11) | collective-permute-done | bytes 442400 | tf_op jit(solution)/shard_map/ppermute | solution.py:231
  32.6 0.0 copy-start.1
  32.6 0.8 copy-done.1
  33.4 0.0 collective-permute-start.14
  33.4 0.0 collective-permute-done.2.refs_6_
  33.4 0.0 collective-permute-done.1.refs_4_
  33.5 0.6 collective-permute-start.6
  34.1 0.3 collective-permute-start.5
  34.4 0.0 collective-permute-start
  34.4 7.8 %collective-permute-done.13.x_ref = bf16[1728,128]{1,0:T(8,128)(2,1)} collective-permute-done((bf16[1728,128]{1,0:T(8,128)(2,1)}, bf16[1728,128]{1,0:T(8,128)(2,1)}, u32[]{:S(2)}, u32[]{:S(2)}) %collective-permute-start.13) | collective-permute-done | bytes 442400 | tf_op jit(solution)/shard_map/ppermute | solution.py:231
  42.2 0.0 collective-permute-start.3
  42.2 7.8 %collective-permute-done.14.x_ref = bf16[1728,128]{1,0:T(8,128)(2,1)} collective-permute-done((bf16[1728,128]{1,0:T(8,128)(2,1)}, bf16[1728,128]{1,0:T(8,128)(2,1)}, u32[]{:S(2)}, u32[]{:S(2)}) %collective-permute-start.14) | collective-permute-done | bytes 442400 | tf_op jit(solution)/shard_map/ppermute | solution.py:231
  50.0 0.0 collective-permute-start.4
  50.0 0.0 collective-permute-done.6.refs_9_
  50.0 0.6 collective-permute-start.8
  50.6 0.0 collective-permute-done.5.refs_8_
  50.6 0.1 collective-permute-start.7
  50.7 0.9 select_convert_fusion.turn_ref
  51.6 0.0 collective-permute-done.refs_3_
  51.6 0.0 collective-permute-start.16
  51.6 1.8 %collective-permute-done.8.refs_11_ = bf16[1728,128]{1,0:T(8,128)(2,1)} collective-permute-done((bf16[1728,128]{1,0:T(8,128)(2,1)}, bf16[1728,128]{1,0:T(8,128)(2,1)}, u32[]{:S(2)}, u32[]{:S(2)}) %collective-permute-start.8) | collective-permute-done | bytes 442400 | tf_op jit(solution)/shard_map/ppermute | solution.py:222
  53.4 0.0 collective-permute-start.17
  53.4 0.7 fusion.30.scale_ref
  54.1 0.1 pad_add_fusion.place_ref
  54.1 0.0 collective-permute-done.3.refs_5_
  54.1 0.0 collective-permute-done.7.refs_10_
  54.2 0.0 collective-permute-done.4.refs_7_
  54.2 0.0 copy-start
  54.2 0.9 copy-done
  55.1 0.0 copy-start.6
  55.1 1.0 %copy-done.6 = bf16[1728,128]{1,0:T(8,128)(2,1)S(1)} copy-done((bf16[1728,128]{1,0:T(8,128)(2,1)S(1)}, bf16[1728,128]{1,0:T(8,128)(2,1)}, u32[]{:S(2)}) %copy-start.6) | copy-done | bytes 442392
  56.1 0.0 copy-start.2
  56.1 0.0 copy-start.4
  56.1 6.5 %products.4 = (bf16[8,4,8,576]{3,2,1,0:T(8,128)(2,1)S(1)}, bf16[8,4,8,576]{3,2,1,0:T(8,128)(2,1)S(1)}) custom-call(s32[4]{0:T(128)S(1)} %pad_add_fusion.place_ref, f32[4]{0:T(128)S(1)} %fusion.30.scale_ref, bf16[128,1024]{1,0:T(8,128)(2,1)S(1)} %copy-done, bf16[1728,128]{1,0:T(8,128)(2,1)S(1)} %copy-done.6, bf16[1728,128]{1,0:T(8,128)(2,1)} %get-tuple-element.19.refs_1_, ...), custom_call_target="tpu_custom_call" | custom-call | flops 905969664 | bytes 8388608 | tf_op jit(solution)/shard_map/products/pallas_call | solution.py:186
  62.6 0.6 collective-permute-start.9
  63.2 0.0 copy-done.2
  63.2 0.0 copy-done.4
  63.2 6.3 %products.5 = (bf16[8,4,8,576]{3,2,1,0:T(8,128)(2,1)S(1)}, bf16[8,4,8,576]{3,2,1,0:T(8,128)(2,1)S(1)}) custom-call(s32[4]{0:T(128)S(1)} %pad_add_fusion.place_ref, f32[4]{0:T(128)S(1)} %fusion.30.scale_ref, bf16[128,1024]{1,0:T(8,128)(2,1)S(1)} %copy-done, bf16[1728,128]{1,0:T(8,128)(2,1)S(1)} %copy-done.4, bf16[1728,128]{1,0:T(8,128)(2,1)S(1)} %copy-done.2, ...), custom_call_target="tpu_custom_call" | custom-call | flops 905969664 | bytes 8388608 | tf_op jit(solution)/shard_map/products/pallas_call | solution.py:186
  69.5 1.5 %collective-permute-start.12 = (bf16[8,4,8,576]{3,2,1,0:T(8,128)(2,1)S(1)}, bf16[8,4,8,576]{3,2,1,0:T(8,128)(2,1)S(1)}, u32[]{:S(2)}, u32[]{:S(2)}) collective-permute-start(bf16[8,4,8,576]{3,2,1,0:T(8,128)(2,1)S(1)} %get-tuple-element.26), channel_id=1, source_target_pairs={{0,1},{1,0},{2,3},{3,2},{4,5},{5,4},{6,7},{7,6},{8,9},{9,8},{10,11... | collective-permute-start | bytes 884744 | tf_op jit(solution)/shard_map/ppermute | solution.py:228
  71.1 6.5 %products.6 = (bf16[8,4,8,576]{3,2,1,0:T(8,128)(2,1)S(1)}, bf16[8,4,8,576]{3,2,1,0:T(8,128)(2,1)S(1)}) custom-call(s32[4]{0:T(128)S(1)} %pad_add_fusion.place_ref, f32[4]{0:T(128)S(1)} %fusion.30.scale_ref, bf16[128,1024]{1,0:T(8,128)(2,1)S(1)} %copy-done, bf16[1728,128]{1,0:T(8,128)(2,1)} %paced.6.refs_0_, bf16[1728,128]{1,0:T(8,128)(2,1)} %paced.7.refs_1_, ...), custom_call_target="tpu_custom_call" | custom-call | flops 905969664 | bytes 8388608 | tf_op jit(solution)/shard_map/products/pallas_call | solution.py:186
  77.6 0.6 collective-permute-start.15
  78.2 0.0 collective-permute-done.16.refs_0_
  78.2 0.0 collective-permute-done.17.refs_1_
  78.2 6.3 %products.7 = (bf16[8,4,8,576]{3,2,1,0:T(8,128)(2,1)S(1)}, bf16[8,4,8,576]{3,2,1,0:T(8,128)(2,1)S(1)}) custom-call(s32[4]{0:T(128)S(1)} %pad_add_fusion.place_ref, f32[4]{0:T(128)S(1)} %fusion.30.scale_ref, bf16[128,1024]{1,0:T(8,128)(2,1)S(1)} %copy-done, bf16[1728,128]{1,0:T(8,128)(2,1)S(1)} %collective-permute-done.16.refs_0_, ...), custom_call_target="tpu_custom_call" | custom-call | flops 905969664 | bytes 8388608 | tf_op jit(solution)/shard_map/products/pallas_call | solution.py:186
  84.5 1.6 %collective-permute-start.18 = (bf16[8,4,8,576]{3,2,1,0:T(8,128)(2,1)S(1)}, bf16[8,4,8,576]{3,2,1,0:T(8,128)(2,1)S(1)}, u32[]{:S(2)}, u32[]{:S(2)}) collective-permute-start(bf16[8,4,8,576]{3,2,1,0:T(8,128)(2,1)S(1)} %get-tuple-element.30), channel_id=1, source_target_pairs={{0,1},{1,0},{2,3},{3,2},{4,5},{5,4},{6,7},{7,6},{8,9},{9,8},{10,11... | collective-permute-start | bytes 884744 | tf_op jit(solution)/shard_map/ppermute | solution.py:228
  86.1 0.3 broadcast_in_dim.39
  86.4 0.0 collective-permute-done.9
  86.5 0.0 collective-permute-done.12
  86.6 0.5 collective-permute-done.15
  87.3 6.6 %collective-permute-done.18 = bf16[8,4,8,576]{3,2,1,0:T(8,128)(2,1)S(1)} collective-permute-done((bf16[8,4,8,576]{3,2,1,0:T(8,128)(2,1)S(1)}, bf16[8,4,8,576]{3,2,1,0:T(8,128)(2,1)S(1)}, u32[]{:S(2)}, u32[]{:S(2)}) %collective-permute-start.18) | collective-permute-done | bytes 294944 | tf_op jit(solution)/shard_map/ppermute | solution.py:228
  93.9 0.0 copy-start.7
  94.0 1.5 %copy-done.7 = bf16[4,2,8,4,8,576]{5,4,3,2,1,0:T(8,128)(2,1)} copy-done((bf16[4,2,8,4,8,576]{5,4,3,2,1,0:T(8,128)(2,1)}, bf16[4,2,8,4,8,576]{5,4,3,2,1,0:T(8,128)(2,1)S(1)}, u32[]{:S(2)}) %copy-start.7) | copy-done | bytes 2359320
  (17 shorter events, 0.4 us)
Async XLA Ops:
  3.8 29.6 %collective-permute-start.2 = (bf16[3456,128]{1,0:T(8,128)(2,1)S(1)}, bf16[3456,128]{1,0:T(8,128)(2,1)S(1)}, u32[]{:S(2)}, u32[]{:S(2)}) collective-permute-start(bf16[3456,128]{1,0:T(8,128)(2,1)S(1)} %get-tuple-element.20.refs_2_), channel_id=1, source_target_pairs={{0,1},{1,0},{2,3},{3,2},{4,5},{5,4},{6,7},{7,6},{8,9},{9,8},{10,11... | collective-permute-start | bytes 2654216 | tf_op jit(solution)/shard_map/ppermute | solution.py:228
  6.7 26.7 %collective-permute-start.1 = (bf16[3456,128]{1,0:T(8,128)(2,1)S(1)}, bf16[3456,128]{1,0:T(8,128)(2,1)S(1)}, u32[]{:S(2)}, u32[]{:S(2)}) collective-permute-start(bf16[3456,128]{1,0:T(8,128)(2,1)S(1)} %get-tuple-element.20.refs_2_), channel_id=1, source_target_pairs={{0,16},{8,24},{16,0},{24,8},{1,17},{9,25},{17,1},{25,9},{2,18},{10... | collective-permute-start | bytes 2654216 | tf_op jit(solution)/shard_map/ppermute | solution.py:225
  8.2 14.9 %collective-permute-start.10 = (bf16[1728,128]{1,0:T(8,128)(2,1)S(1)}, bf16[1728,128]{1,0:T(8,128)(2,1)S(1)}, u32[]{:S(2)}, u32[]{:S(2)}) collective-permute-start(bf16[1728,128]{1,0:T(8,128)(2,1)S(1)} %get-tuple-element.18.refs_0_), channel_id=1, source_target_pairs={{0,2},{1,3},{2,4},{3,5},{4,6},{5,7},{6,0},{7,1},{8,10},{9,11},{10,... | collective-permute-start | bytes 1327112 | tf_op jit(solution)/shard_map/ppermute | solution.py:231
  9.8 0.8 copy-start.5
  10.6 22.0 %collective-permute-start.11 = (bf16[1728,128]{1,0:T(8,128)(2,1)}, bf16[1728,128]{1,0:T(8,128)(2,1)S(1)}, u32[]{:S(2)}, u32[]{:S(2)}) collective-permute-start(bf16[1728,128]{1,0:T(8,128)(2,1)} %get-tuple-element.19.refs_1_), channel_id=1, source_target_pairs={{0,2},{1,3},{2,4},{3,5},{4,6},{5,7},{6,0},{7,1},{8,10},{9,11},{10,... | collective-permute-start | bytes 1327112 | tf_op jit(solution)/shard_map/ppermute | solution.py:231
  23.1 0.8 copy-start.3
  23.9 18.3 %collective-permute-start.13 = (bf16[1728,128]{1,0:T(8,128)(2,1)}, bf16[1728,128]{1,0:T(8,128)(2,1)}, u32[]{:S(2)}, u32[]{:S(2)}) collective-permute-start(bf16[1728,128]{1,0:T(8,128)(2,1)} %paced.4.refs_0_), channel_id=1, source_target_pairs={{0,2},{1,3},{2,4},{3,5},{4,6},{5,7},{6,0},{7,1},{8,10},{9,11},{10,... | collective-permute-start | bytes 1327112 | tf_op jit(solution)/shard_map/ppermute | solution.py:231
  32.6 0.8 copy-start.1
  33.4 16.6 %collective-permute-start.14 = (bf16[1728,128]{1,0:T(8,128)(2,1)}, bf16[1728,128]{1,0:T(8,128)(2,1)}, u32[]{:S(2)}, u32[]{:S(2)}) collective-permute-start(bf16[1728,128]{1,0:T(8,128)(2,1)} %paced.5.refs_1_), channel_id=1, source_target_pairs={{0,2},{1,3},{2,4},{3,5},{4,6},{5,7},{6,0},{7,1},{8,10},{9,11},{10,... | collective-permute-start | bytes 1327112 | tf_op jit(solution)/shard_map/ppermute | solution.py:231
  33.5 16.5 %collective-permute-start.6 = (bf16[1728,128]{1,0:T(8,128)(2,1)S(1)}, bf16[1728,128]{1,0:T(8,128)(2,1)}, u32[]{:S(2)}, u32[]{:S(2)}) collective-permute-start(bf16[1728,128]{1,0:T(8,128)(2,1)S(1)} %slice.7), channel_id=1, source_target_pairs={{0,1},{1,0},{2,3},{3,2},{4,5},{5,4},{6,7},{7,6},{8,9},{9,8},{10,11... | collective-permute-start | bytes 1327112 | tf_op jit(solution)/shard_map/ppermute | solution.py:228
  34.1 16.5 %collective-permute-start.5 = (bf16[1728,128]{1,0:T(8,128)(2,1)S(1)}, bf16[1728,128]{1,0:T(8,128)(2,1)}, u32[]{:S(2)}, u32[]{:S(2)}) collective-permute-start(bf16[1728,128]{1,0:T(8,128)(2,1)S(1)} %slice.8), channel_id=1, source_target_pairs={{0,16},{8,24},{16,0},{24,8},{1,17},{9,25},{17,1},{25,9},{2,18},{10... | collective-permute-start | bytes 1327112 | tf_op jit(solution)/shard_map/ppermute | solution.py:225
  34.4 17.2 %collective-permute-start = (bf16[3456,128]{1,0:T(8,128)(2,1)S(1)}, bf16[3456,128]{1,0:T(8,128)(2,1)S(1)}, u32[]{:S(2)}, u32[]{:S(2)}) collective-permute-start(bf16[3456,128]{1,0:T(8,128)(2,1)S(1)} %get-tuple-element.20.refs_2_), channel_id=1, source_target_pairs={{0,8},{8,0},{16,24},{24,16},{1,9},{9,1},{17,25},{25,17},{2,10},{10... | collective-permute-start | bytes 2654216 | tf_op jit(solution)/shard_map/ppermute | solution.py:222
  42.2 12.0 %collective-permute-start.3 = (bf16[3456,128]{1,0:T(8,128)(2,1)S(1)}, bf16[3456,128]{1,0:T(8,128)(2,1)}, u32[]{:S(2)}, u32[]{:S(2)}) collective-permute-start(bf16[3456,128]{1,0:T(8,128)(2,1)S(1)} %collective-permute-done.1.refs_4_), channel_id=1, source_target_pairs={{0,8},{8,0},{16,24},{24,16},{1,9},{9,1},{17,25},{25,17},{2,10},{10... | collective-permute-start | bytes 2654216 | tf_op jit(solution)/shard_map/ppermute | solution.py:222
  50.0 4.2 %collective-permute-start.4 = (bf16[3456,128]{1,0:T(8,128)(2,1)S(1)}, bf16[3456,128]{1,0:T(8,128)(2,1)}, u32[]{:S(2)}, u32[]{:S(2)}) collective-permute-start(bf16[3456,128]{1,0:T(8,128)(2,1)S(1)} %collective-permute-done.2.refs_6_), channel_id=1, source_target_pairs={{0,8},{8,0},{16,24},{24,16},{1,9},{9,1},{17,25},{25,17},{2,10},{10... | collective-permute-start | bytes 2654216 | tf_op jit(solution)/shard_map/ppermute | solution.py:222
  50.0 3.4 %collective-permute-start.8 = (bf16[1728,128]{1,0:T(8,128)(2,1)}, bf16[1728,128]{1,0:T(8,128)(2,1)}, u32[]{:S(2)}, u32[]{:S(2)}) collective-permute-start(bf16[1728,128]{1,0:T(8,128)(2,1)} %collective-permute-done.6.refs_9_), channel_id=1, source_target_pairs={{0,8},{8,0},{16,24},{24,16},{1,9},{9,1},{17,25},{25,17},{2,10},{10... | collective-permute-start | bytes 1327112 | tf_op jit(solution)/shard_map/ppermute | solution.py:222
  50.6 3.6 %collective-permute-start.7 = (bf16[1728,128]{1,0:T(8,128)(2,1)}, bf16[1728,128]{1,0:T(8,128)(2,1)}, u32[]{:S(2)}, u32[]{:S(2)}) collective-permute-start(bf16[1728,128]{1,0:T(8,128)(2,1)} %collective-permute-done.5.refs_8_), channel_id=1, source_target_pairs={{0,8},{8,0},{16,24},{24,16},{1,9},{9,1},{17,25},{25,17},{2,10},{10... | collective-permute-start | bytes 1327112 | tf_op jit(solution)/shard_map/ppermute | solution.py:222
  51.6 26.7 %collective-permute-start.16 = (bf16[1728,128]{1,0:T(8,128)(2,1)}, bf16[1728,128]{1,0:T(8,128)(2,1)S(1)}, u32[]{:S(2)}, u32[]{:S(2)}) collective-permute-start(bf16[1728,128]{1,0:T(8,128)(2,1)} %paced.6.refs_0_), channel_id=1, source_target_pairs={{0,2},{1,3},{2,4},{3,5},{4,6},{5,7},{6,0},{7,1},{8,10},{9,11},{10,... | collective-permute-start | bytes 1327112 | tf_op jit(solution)/shard_map/ppermute | solution.py:231
  53.4 24.8 %collective-permute-start.17 = (bf16[1728,128]{1,0:T(8,128)(2,1)}, bf16[1728,128]{1,0:T(8,128)(2,1)S(1)}, u32[]{:S(2)}, u32[]{:S(2)}) collective-permute-start(bf16[1728,128]{1,0:T(8,128)(2,1)} %paced.7.refs_1_), channel_id=1, source_target_pairs={{0,2},{1,3},{2,4},{3,5},{4,6},{5,7},{6,0},{7,1},{8,10},{9,11},{10,... | collective-permute-start | bytes 1327112 | tf_op jit(solution)/shard_map/ppermute | solution.py:231
  54.2 1.0 copy-start
  55.1 1.0 %copy-start.6 = (bf16[1728,128]{1,0:T(8,128)(2,1)S(1)}, bf16[1728,128]{1,0:T(8,128)(2,1)}, u32[]{:S(2)}) copy-start(bf16[1728,128]{1,0:T(8,128)(2,1)} %copy-done.5) | copy-start | bytes 1327108
  56.1 7.1 %copy-start.2 = (bf16[1728,128]{1,0:T(8,128)(2,1)S(1)}, bf16[1728,128]{1,0:T(8,128)(2,1)}, u32[]{:S(2)}) copy-start(bf16[1728,128]{1,0:T(8,128)(2,1)} %paced.5.refs_1_) | copy-start | bytes 1327108
  56.1 7.1 %copy-start.4 = (bf16[1728,128]{1,0:T(8,128)(2,1)S(1)}, bf16[1728,128]{1,0:T(8,128)(2,1)}, u32[]{:S(2)}) copy-start(bf16[1728,128]{1,0:T(8,128)(2,1)} %paced.4.refs_0_) | copy-start | bytes 1327108
  62.6 23.8 %collective-permute-start.9 = (bf16[8,4,8,576]{3,2,1,0:T(8,128)(2,1)S(1)}, bf16[8,4,8,576]{3,2,1,0:T(8,128)(2,1)S(1)}, u32[]{:S(2)}, u32[]{:S(2)}) collective-permute-start(bf16[8,4,8,576]{3,2,1,0:T(8,128)(2,1)S(1)} %get-tuple-element.24), channel_id=1, source_target_pairs={{0,1},{1,0},{2,3},{3,2},{4,5},{5,4},{6,7},{7,6},{8,9},{9,8},{10,11... | collective-permute-start | bytes 884744 | tf_op jit(solution)/shard_map/ppermute | solution.py:228
  69.5 17.0 %collective-permute-start.12 = (bf16[8,4,8,576]{3,2,1,0:T(8,128)(2,1)S(1)}, bf16[8,4,8,576]{3,2,1,0:T(8,128)(2,1)S(1)}, u32[]{:S(2)}, u32[]{:S(2)}) collective-permute-start(bf16[8,4,8,576]{3,2,1,0:T(8,128)(2,1)S(1)} %get-tuple-element.26), channel_id=1, source_target_pairs={{0,1},{1,0},{2,3},{3,2},{4,5},{5,4},{6,7},{7,6},{8,9},{9,8},{10,11... | collective-permute-start | bytes 884744 | tf_op jit(solution)/shard_map/ppermute | solution.py:228
  77.6 9.6 %collective-permute-start.15 = (bf16[8,4,8,576]{3,2,1,0:T(8,128)(2,1)S(1)}, bf16[8,4,8,576]{3,2,1,0:T(8,128)(2,1)S(1)}, u32[]{:S(2)}, u32[]{:S(2)}) collective-permute-start(bf16[8,4,8,576]{3,2,1,0:T(8,128)(2,1)S(1)} %get-tuple-element.28), channel_id=1, source_target_pairs={{0,1},{1,0},{2,3},{3,2},{4,5},{5,4},{6,7},{7,6},{8,9},{9,8},{10,11... | collective-permute-start | bytes 884744 | tf_op jit(solution)/shard_map/ppermute | solution.py:228
  84.5 9.4 %collective-permute-start.18 = (bf16[8,4,8,576]{3,2,1,0:T(8,128)(2,1)S(1)}, bf16[8,4,8,576]{3,2,1,0:T(8,128)(2,1)S(1)}, u32[]{:S(2)}, u32[]{:S(2)}) collective-permute-start(bf16[8,4,8,576]{3,2,1,0:T(8,128)(2,1)S(1)} %get-tuple-element.30), channel_id=1, source_target_pairs={{0,1},{1,0},{2,3},{3,2},{4,5},{5,4},{6,7},{7,6},{8,9},{9,8},{10,11... | collective-permute-start | bytes 884744 | tf_op jit(solution)/shard_map/ppermute | solution.py:228
  93.9 1.5 %copy-start.7 = (bf16[4,2,8,4,8,576]{5,4,3,2,1,0:T(8,128)(2,1)}, bf16[4,2,8,4,8,576]{5,4,3,2,1,0:T(8,128)(2,1)S(1)}, u32[]{:S(2)}) copy-start(bf16[4,2,8,4,8,576]{5,4,3,2,1,0:T(8,128)(2,1)S(1)} %bitcast_dynamic-update-slice_fusion) | copy-start | bytes 7077892

commit v3 on v2

v3 whole, which is shorter than its diff:
```python
import functools
import math

import jax
import jax.numpy as jnp
import numpy as np
from jax import lax
from jax.experimental import pallas as pl
from jax.experimental.pallas import tpu as pltpu
from jax.sharding import PartitionSpec as P

GROUPS = 8
TILES = 27
PAIR_ROWS = 13 * 16
GROUP_ROWS = TILES * 16
BLOCK_ROWS = GROUPS * GROUP_ROWS
HALF_ROWS = BLOCK_ROWS // 2
STATIONS = 8
CUTS = (0, 4, 8)
PACE = 80 * 2**20
F32 = jnp.float32
BF16 = jnp.bfloat16


def prepare_kernel(x_ref, whole_ref, d_ref):
    count, segs = x_ref.shape[0], x_ref.shape[1]
    tail = segs - 256
    if count < STATIONS:
        d_ref[...] = jnp.zeros_like(d_ref)
    lane_group = lax.broadcasted_iota(jnp.int32, (8, 128), 1) // 32
    for i in range(count):
        values = x_ref[i].astype(F32)
        power = jnp.mean(values * values, axis=1, keepdims=True)
        white = (values * lax.rsqrt(power + 1e-06)).astype(BF16).astype(F32)
        main = white[:256].T
        rest = jnp.concatenate([white[256:], jnp.zeros((32 - tail, 192), F32)], axis=0)
        rest = jnp.concatenate([rest] * 4, axis=0).T
        for group in range(4):
            half, pair = group // 2, group % 2
            row = pair * PAIR_ROWS + half * 8 + i
            for line in range(6):
                rows = slice(line * 32 + group * 8, line * 32 + group * 8 + 8)
                for side in range(2):
                    tile = line * 2 + side
                    d_ref[pl.ds(row + tile * 16, 8, stride=GROUP_ROWS), :] = main[
                        rows, side * 128 : side * 128 + 128
                    ]
            first = jnp.zeros((8, 128), F32)
            for line in range(4):
                rows = slice(line * 32 + group * 8, line * 32 + group * 8 + 8)
                first = jnp.where(lane_group == line, rest[rows], first)
            d_ref[pl.ds(row + 12 * 16, 8, stride=GROUP_ROWS), :] = first
        for half in range(2):
            last = jnp.zeros((8, 128), F32)
            for pair in range(2):
                for part in range(2):
                    start = (4 + part) * 32 + (half * 2 + pair) * 8
                    last = jnp.where(
                        lane_group == pair * 2 + part, rest[start : start + 8], last
                    )
            d_ref[pl.ds(26 * 16 + half * 8 + i, 8, stride=GROUP_ROWS), :] = last
    for start in range(0, BLOCK_ROWS, 144):
        whole_ref[start : start + 144] = d_ref[start : start + 144].astype(BF16)


def in_vmem(array):
    return pltpu.with_memory_space_constraint(array, pltpu.VMEM)


def prepare(spectra):
    vmem = pl.BlockSpec(memory_space=pltpu.VMEM)
    return pl.pallas_call(
        prepare_kernel,
        out_shape=pltpu.VMEM((BLOCK_ROWS, 128), BF16),
        in_specs=[vmem],
        out_specs=vmem,
        scratch_shapes=[pltpu.VMEM((BLOCK_ROWS, 128), F32)],
        compiler_params=pltpu.CompilerParams(vmem_limit_bytes=8 * 2**20),
        name="prepare",
    )(spectra)


def turn_matrix():
    lane = np.arange(128)
    late, imag = lane // 64, lane // 32 % 2
    lines = np.stack([late == 0, late == 1, imag == 0, -imag]).astype(np.float32)
    return jnp.asarray(np.repeat(lines, 16, axis=0), BF16)


def nt(left, right):
    return lax.dot_general(left, right, (((1,), (1,)), ((), ())), preferred_element_type=F32)


def products_kernel(layout, source_count, src_count, norm, mask_ref, turn_ref, *refs):
    arrays = 1 + max(n for block in layout for n, _ in block)
    operands, outs, (token_ref, sums) = refs[:arrays], refs[arrays:-2], refs[-2:]
    token_ref[...] = jnp.zeros_like(token_ref)
    count = outs[0].shape[0]
    block_count = len(layout) - source_count
    lanes = block_count * 16
    tiles_wide = sums.shape[0] // (source_count * STATIONS * 576)
    pieces = [[(operands[n], at) for n, at in block] for block in layout]
    lefts, rights = pieces[:source_count], pieces[source_count:]
    steps = GROUPS // 2
    for h in range(2):
        def group(q, carry, h=h):
            def rows_of(ref, at, tile):
                return ref[pl.ds(pl.multiple_of(q * GROUP_ROWS + at + tile * 16, 16), 16), :]

            def tile_of(tile):
                return jnp.concatenate([rows_of(*p[h], tile) for p in rights], axis=0)

            def turned(tile):
                swapped = pltpu.roll(tile, 96, 1) * signs[2] + pltpu.roll(tile, 32, 1) * signs[3]
                lines = []
                for value in (tile, swapped):
                    across = pltpu.roll(value, 64, 1)
                    lines.append((value * signs[0], across * signs[1], across * signs[0], value * signs[1]))
                return [[line[2 * half : 2 * half + 2] for line in lines] for half in range(2)]

            signs = [turn_ref[16 * k : 16 * k + 16] for k in range(4)]
            last_right = tile_of(26)
            last_turned = [turned(rows_of(*p[h], 26)) for p in lefts]
            for pair in range(2):
                lines = []
                for p in lefts:
                    tiles = [rows_of(*p[h], pair * 13 + t) for t in range(12)]
                    for a in range(3):
                        real, imag = tiles[a * 4 : a * 4 + 2], tiles[a * 4 + 2 : a * 4 + 4]
                        lines.append(jnp.concatenate(real + imag, axis=1))
                        lines.append(jnp.concatenate(imag + [-real[0], -real[1]], axis=1))
                main = jnp.concatenate(lines, axis=0)
                rest_right = tile_of(pair * 13 + 12)
                first_turned = [turned(rows_of(*p[h], pair * 13 + 12)) for p in lefts]
                for b in range(3):
                    slot = b if b < 2 else pair
                    rest = []
                    for source in range(source_count):
                        for a in range(3):
                            of = first_turned[source][a] if a < 2 else last_turned[source][pair]
                            rest += [of[e][slot] for e in range(2)]
                    rest = jnp.concatenate(rest, axis=0)
                    weights = [tile_of(pair * 13 + b * 4 + t) for t in range(4)]
                    weights.append(rest_right if b < 2 else last_right)
                    result = nt(
                        jnp.concatenate([main, rest], axis=1), jnp.concatenate(weights, axis=1)
                    )
                    for n in range(source_count * 12):
                        source, a, e, half = n // 12, n // 4 % 3, n // 2 % 2, n % 2
                        at = (a * 6 + b * 2 + e) * 32 + half * 16 + pair * 8 + h * steps
                        for m in range(tiles_wide):
                            start = (source * tiles_wide + m) * STATIONS * 576 + at + q
                            wide = min(128, lanes)
                            sums[pl.ds(start, 8, stride=576), :wide] = result[
                                n * 8 : n * 8 + 8, m * 128 : m * 128 + wide
                            ]
            return carry

        lax.fori_loop(0, steps, group, 0, unroll=block_count <= 8)

    src = lax.axis_index("src")
    highs = src_count // 2
    places, scales = [], []
    for block in range(src_count):
        high = lax.rem(src // 2 + highs - block // 2, highs)
        places.append(high * 2 + lax.rem(src + block, 2))
        scales.append(mask_ref[src, places[-1]].astype(F32) * norm)

    bin_half = (lax.broadcasted_iota(jnp.int32, (8, 576), 1) % 32) < 16
    for source in range(source_count):
        for i in range(count):
            for m in range(tiles_wide):
                start = ((source * tiles_wide + m) * STATIONS + i) * 576
                turned = sums[start : start + 576, :].T
                for n in range(min(8, block_count)):
                    low, high = turned[n * 16 : n * 16 + 8], turned[n * 16 + 8 : n * 16 + 16]
                    which, block = divmod(m * 8 + n, src_count)
                    at = places[block]
                    value = (jnp.where(bin_half, low, high) * scales[block]).astype(BF16)
                    outs[2 * source + which][i, at] = value[: outs[0].shape[2]]


@functools.partial(jax.jit, static_argnums=(3, 4, 5, 6))
def products_of(mask, turn, operands, layout, s, count, norm):
    n = len(layout) - s
    src_count = n // 2
    sum_rows = s * ((n + 7) // 8) * STATIONS * 576
    out = jax.ShapeDtypeStruct((count, src_count, count, 576), BF16)
    smem, vmem = pl.BlockSpec(memory_space=pltpu.SMEM), pl.BlockSpec(memory_space=pltpu.VMEM)
    operands = [in_vmem(operand) for operand in operands]
    return pl.pallas_call(
        functools.partial(products_kernel, layout, s, src_count, norm),
        out_shape=(out,) * (2 * s) + (jax.ShapeDtypeStruct((8, 128), F32),),
        in_specs=[smem, vmem] + [vmem] * len(operands),
        out_specs=(vmem,) * (2 * s + 1),
        scratch_shapes=[pltpu.VMEM((sum_rows, 128), F32)],
        compiler_params=pltpu.CompilerParams(vmem_limit_bytes=2 * sum_rows // s * 512 + 12 * 2**20),
        cost_estimate=pl.CostEstimate(
            flops=2 * 16 * 3 * 96 * s * 16 * n * 768, bytes_accessed=8 * 2**20, transcendentals=0
        ),
        name="products",
    )(mask, turn, *operands)


def products(mask, turn, sources, blocks, count, norm):
    operands, layout = [], []
    for block in (*sources, *blocks):
        layout.append([])
        for array, at in block:
            known = [n for n, operand in enumerate(operands) if operand is array]
            layout[-1].append((known[0] if known else len(operands), at))
            if not known:
                operands.append(array)
    layout = tuple(map(tuple, layout))
    return products_of(mask, turn, operands, layout, len(sources), count, norm)


def paced(array, after=(), wait_bytes=0):
    any_ = pl.BlockSpec(memory_space=pl.ANY)
    return pl.pallas_call(
        lambda *refs: None,
        out_shape=pltpu.VMEM(array.shape, array.dtype),
        in_specs=[any_] * (1 + len(after)),
        out_specs=any_,
        input_output_aliases={0: 0},
        cost_estimate=pl.CostEstimate(flops=0, bytes_accessed=wait_bytes, transcendentals=0),
        compiler_params=pltpu.CompilerParams(vmem_limit_bytes=2**20),
        name="paced",
    )(in_vmem(array), *after)


def rearranged(arrays, outputs, after=()):
    def kernel(*refs):
        ins, outs = refs[: len(arrays)], refs[len(arrays) + len(after) :]
        for out_ref, pieces in zip(outs, outputs):
            at = 0
            for array, start, rows in pieces:
                for row in range(0, rows, 144):
                    out_ref[at + row : at + row + 144] = ins[array][start + row : start + row + 144]
                at += rows

    vmem = pl.BlockSpec(memory_space=pltpu.VMEM)
    sizes = [sum(rows for _, _, rows in pieces) for pieces in outputs]
    total = sum(sizes) + sum(array.shape[0] for array in arrays)
    return pl.pallas_call(
        kernel,
        out_shape=tuple(pltpu.VMEM((size, 128), BF16) for size in sizes),
        in_specs=[vmem] * len(arrays) + [pl.BlockSpec(memory_space=pl.ANY)] * len(after),
        out_specs=(vmem,) * len(outputs),
        compiler_params=pltpu.CompilerParams(vmem_limit_bytes=total * 256 + 2 * 2**20),
        name="rearranged",
    )(*map(in_vmem, arrays), *after)


def blank(shape, token):
    return pl.pallas_call(
        lambda token_ref, o_ref: None,
        out_shape=pltpu.HBM(shape, BF16),
        in_specs=[pl.BlockSpec(memory_space=pl.ANY)],
        out_specs=pl.BlockSpec(memory_space=pltpu.HBM),
        compiler_params=pltpu.CompilerParams(vmem_limit_bytes=2**20),
        name="blank",
    )(token)


def on_device(spectra, block_mask):
    count, segs = spectra.shape[0], spectra.shape[1]
    src_count, rcv_count = lax.axis_size("src"), lax.axis_size("rcv")
    src, rcv = lax.axis_index("src"), lax.axis_index("rcv")
    highs, steps = src_count // 2, rcv_count // 2

    def over_core(half):
        return lax.ppermute(half, "src", [(s, s ^ 1) for s in range(src_count)])

    def over_high(half):
        return lax.ppermute(half, "src", [(s, (s + 2) % src_count) for s in range(src_count)])

    def over_x(half):
        return lax.ppermute(half, "rcv", [(r, r ^ 1) for r in range(rcv_count)])

    def over_z(half):
        return lax.ppermute(half, "rcv", [(r, (r + 2) % rcv_count) for r in range(rcv_count)])

    def whole_at(array, start=0):
        return (array, start), (array, start + HALF_ROWS)

    own = prepare(spectra)
    passing = paced(over_z(own), wait_bytes=PACE)
    sources = [whole_at(own), whole_at(passing)]
    beside, high = over_x(own), over_high(own)
    cuts, ahead = [n * GROUP_ROWS for n in CUTS], []
    if steps > 2:
        listed = [[(0, start, end - start)] for start, end in zip(cuts, cuts[1:])]
        ahead = [over_z(piece) for piece in rearranged([passing], listed)]
    mine, theirs = [whole_at(own)], [whole_at(beside)]
    if highs > 1:
        three = [(n, 0, BLOCK_ROWS) for n in range(3)]
        joined, first, second = rearranged(
            [own, beside, high],
            [three, [(1, 0, HALF_ROWS)], [(2, HALF_ROWS, HALF_ROWS)]],
            (passing,),
        )
        joined = over_core(joined)
        mine += [whole_at(joined), whole_at(high), whole_at(joined, 2 * BLOCK_ROWS)]
        theirs += [whole_at(joined, BLOCK_ROWS)]
    else:
        mine += [whole_at(over_core(own))]
        theirs += [whole_at(over_core(beside))]
    for k in range(1, highs):
        if k > 1:
            high = over_high(high)
            (second,) = rearranged([high], [[(0, HALF_ROWS, HALF_ROWS)]])
            mine += [whole_at(high), whole_at(over_core(high))]
        first, across = over_high(first), over_x(second)
        (pair,) = rearranged(
            [first, across], [[(0, 0, HALF_ROWS), (1, 0, HALF_ROWS)]], ahead[:1] if k == 1 else ()
        )
        theirs += [((first, 0), (across, 0)), whole_at(over_core(pair))]
    blocks = mine + theirs
    if len(blocks) <= 8:
        arrays, listed = [], []
        for block in blocks:
            for array, at in block:
                if not any(array is known for known in arrays):
                    arrays.append(array)
                listed.append(([array is known for known in arrays].index(True), at, HALF_ROWS))
        (together,) = rearranged(arrays, [listed], ahead[1:-1])
        blocks = [whole_at(together, n * BLOCK_ROWS) for n in range(len(blocks))]
    held = list({id(array): array for block in blocks for array, _ in block}.values())
    turn = turn_matrix()
    x, z = rcv % 2, rcv // 2
    pieces = []
    for k in range(1, steps):
        batch = sources
        if k + 1 < steps:
            early, late = ahead if k == 1 else (over_z(early), over_z(late))
        *outs, token = products(block_mask, turn, batch, blocks, count, 1.0 / math.sqrt(segs))
        if k + 2 < steps:
            late = paced(late, (token,), PACE)
        sources = [((early, 0), (late, 0))]
        pieces += [(kept, over_x(sent)) for kept, sent in zip(outs[::2], outs[1::2])]
    result = blank((steps, 2, count, src_count, count, 576), token)
    for k, (kept, got) in enumerate(pieces):
        at = lax.rem(z - k + steps, steps)
        result = lax.dynamic_update_slice(result, kept[None, None], (at, x, 0, 0, 0, 0))
        result = lax.dynamic_update_slice(result, got[None, None], (at, 1 - x, 0, 0, 0, 0))
    return result.reshape(steps * 2 * count, src_count, count, 576)


def solution(mesh):
    placed = (P(("src", "rcv"), None, None), P())
    return jax.shard_map(
        on_device,
        mesh=mesh,
        in_specs=placed,
        out_specs=P("src", None, "rcv", None),
        check_vma=False,
    )
```

time: 95.7 us -> 93.3 us (0.975)
  Pallas kernels: 27.9 us -> 18.4 us
  waiting for transfers between devices: 44.3 us -> 48.6 us
  local copies, waits for them, and re-layouts: 7.95 us -> 10.5 us
  starting transfers between devices: 13.5 us -> 15.4 us
  other arithmetic: 1.68 us -> 0 us
    ppermute x2, waiting for transfers between devices: 0.01 us -> 9.57 us  [over_high(): lax.ppermute(half, 'src', [(s, (s + 2) % src_count) for s in range(src_co...]
    pallas_call x9 -> x11, Pallas kernels: 27.9 us -> 18.4 us  [the longest x3 16.2 us: products_of(): pl.pallas_call(functools.partial(products_kernel, layout, s, src_count, n...]
    ppermute x6, waiting for transfers between devices: 7.16 us -> 4.06 us  [over_x(): return lax.ppermute(half, 'rcv', [(r, r ^ 1) for r in range(rcv_count)])]
    dynamic_update_slice x4, local copies, waits for them, and re-layouts: 0.17 us -> 3.01 us  [on_device(): lax.dynamic_update_slice(result, got[None, None], (at, 1 - x, 0, 0, 0, 0))]
    dynamic_update_slice x4, local copies, waits for them, and re-layouts: 0.19 us -> 3.01 us  [on_device(): lax.dynamic_update_slice(result, kept[None, None], (at, x, 0, 0, 0, 0))]
    unnamed x17 -> x11, local copies, waits for them, and re-layouts: 7.26 us -> 4.53 us
    ppermute x6 -> x5, starting transfers between devices: 3.16 us -> 5.42 us  [over_z(): lax.ppermute(half, 'rcv', [(r, (r + 2) % rcv_count) for r in range(rcv_co...]
    ppermute x6 -> x5, waiting for transfers between devices: 35.3 us -> 33.6 us  [over_z(): lax.ppermute(half, 'rcv', [(r, (r + 2) % rcv_count) for r in range(rcv_co...]
  transfers between devices with their start and end apart: 19 -> 15, of which waited for: 7 -> 9; matrix products, arithmetic and copies ran while one was open for 2% -> 6% of each run, Pallas kernels for 27% -> 18%
where the time goes in v3:
time: 93.3 us; the launch traced here: 93.1 us
  waiting for transfers between devices  48.6 us (52%)
  Pallas kernels  18.4 us (20%)
  starting transfers between devices  15.4 us (17%)
  local copies, waits for them, and re-layouts  10.5 us (11%)
    ppermute x5, waiting for transfers between devices, over_z(): lax.ppermute(half, 'rcv', [(r, (r + 2) % rcv_count) for r in range(rcv_co...  33.6 us
    pallas_call x3, Pallas kernels, products_of(): pl.pallas_call(functools.partial(products_kernel, layout, s, src_count, n...  16.2 us
    ppermute x2, waiting for transfers between devices, over_high(): lax.ppermute(half, 'src', [(s, (s + 2) % src_count) for s in range(src_co...  9.57 us
    ppermute x6, starting transfers between devices, over_x(): return lax.ppermute(half, 'rcv', [(r, r ^ 1) for r in range(rcv_count)])  6.78 us
    ppermute x5, starting transfers between devices, over_z(): lax.ppermute(half, 'rcv', [(r, (r + 2) % rcv_count) for r in range(rcv_co...  5.42 us
    unnamed x11, local copies, waits for them, and re-layouts  4.53 us
    ppermute x6, waiting for transfers between devices, over_x(): return lax.ppermute(half, 'rcv', [(r, r ^ 1) for r in range(rcv_count)])  4.06 us
    ppermute x2, starting transfers between devices, over_high(): lax.ppermute(half, 'src', [(s, (s + 2) % src_count) for s in range(src_co...  3.1 us
  transfers between devices with their start and end apart: 15, of which 9 were waited for; matrix products, arithmetic and copies ran while one was open for 6% of the time, Pallas kernels for 18%

profile of v3, /device:TPU:0, one launch (start us, length us, event | category | flops | bytes accessed | tf_op | source)
XLA Modules:
  0.0 93.1 jit_solution(14570957142618487974)
XLA Ops:
  0.0 1.5 %copy.6.x_ref = bf16[8,287,192]{2,1,0:T(8,128)(2,1)S(1)} copy(bf16[8,287,192]{2,0,1:T(8,128)(2,1)} %param.3) | data formatting | bytes 1763328 | tf_op args[0]
  1.5 1.5 %prepare.1.refs_0_ = bf16[3456,128]{1,0:T(8,128)(2,1)S(1)} custom-call(bf16[8,287,192]{2,1,0:T(8,128)(2,1)S(1)} %copy.6.x_ref), custom_call_target="tpu_custom_call" | custom-call | tf_op jit(solution)/shard_map/prepare/pallas_call | solution.py:72
  3.0 3.1 %collective-permute-start = (bf16[3456,128]{1,0:T(8,128)(2,1)S(1)}, bf16[3456,128]{1,0:T(8,128)(2,1)S(1)}, u32[]{:S(2)}, u32[]{:S(2)}) collective-permute-start(bf16[3456,128]{1,0:T(8,128)(2,1)S(1)} %prepare.1.refs_0_), channel_id=1, source_target_pairs={{0,2},{1,3},{2,4},{3,5},{4,6},{5,7},{6,0},{7,1},{8,10},{9,11},{10,... | collective-permute-start | bytes 2654216 | tf_op jit(solution)/shard_map/ppermute | solution.py:282
  6.0 1.5 %collective-permute-start.4 = (bf16[3456,128]{1,0:T(8,128)(2,1)S(1)}, bf16[3456,128]{1,0:T(8,128)(2,1)S(1)}, u32[]{:S(2)}, u32[]{:S(2)}) collective-permute-start(bf16[3456,128]{1,0:T(8,128)(2,1)S(1)} %prepare.1.refs_0_), channel_id=1, source_target_pairs={{0,1},{1,0},{2,3},{3,2},{4,5},{5,4},{6,7},{7,6},{8,9},{9,8},{10,11... | collective-permute-start | bytes 2654216 | tf_op jit(solution)/shard_map/ppermute | solution.py:279
  7.5 1.5 %collective-permute-start.5 = (bf16[3456,128]{1,0:T(8,128)(2,1)S(1)}, bf16[3456,128]{1,0:T(8,128)(2,1)S(1)}, u32[]{:S(2)}, u32[]{:S(2)}) collective-permute-start(bf16[3456,128]{1,0:T(8,128)(2,1)S(1)} %prepare.1.refs_0_), channel_id=1, source_target_pairs={{0,16},{8,24},{16,0},{24,8},{1,17},{9,25},{17,1},{25,9},{2,18},{10... | collective-permute-start | bytes 2654216 | tf_op jit(solution)/shard_map/ppermute | solution.py:276
  9.1 18.7 %collective-permute-done.refs_0_ = bf16[3456,128]{1,0:T(8,128)(2,1)S(1)} collective-permute-done((bf16[3456,128]{1,0:T(8,128)(2,1)S(1)}, bf16[3456,128]{1,0:T(8,128)(2,1)S(1)}, u32[]{:S(2)}, u32[]{:S(2)}) %collective-permute-start) | collective-permute-done | bytes 884768 | tf_op jit(solution)/shard_map/ppermute | solution.py:282
  27.7 0.0 collective-permute-done.4.refs_1_.refs_3_
  27.7 0.6 collective-permute-done.5.refs_2_
  28.4 0.2 rearranged.5
  28.6 0.1 collective-permute-start.6
  28.7 0.1 rearranged.4
  28.7 1.6 %collective-permute-start.7 = (bf16[1728,128]{1,0:T(8,128)(2,1)S(1)}, bf16[1728,128]{1,0:T(8,128)(2,1)S(1)}, u32[]{:S(2)}, u32[]{:S(2)}) collective-permute-start(bf16[1728,128]{1,0:T(8,128)(2,1)S(1)} %get-tuple-element.23), channel_id=1, source_target_pairs={{0,16},{8,24},{16,0},{24,8},{1,17},{9,25},{17,1},{25,9},{2,18},{10... | collective-permute-start | bytes 1327112 | tf_op jit(solution)/shard_map/ppermute | solution.py:276
  30.3 0.9 collective-permute-start.8
  31.2 1.3 %collective-permute-start.1 = (bf16[1728,128]{1,0:T(8,128)(2,1)S(1)}, bf16[1728,128]{1,0:T(8,128)(2,1)S(1)}, u32[]{:S(2)}, u32[]{:S(2)}) collective-permute-start(bf16[1728,128]{1,0:T(8,128)(2,1)S(1)} %get-tuple-element.20), channel_id=1, source_target_pairs={{0,2},{1,3},{2,4},{3,5},{4,6},{5,7},{6,0},{7,1},{8,10},{9,11},{10,... | collective-permute-start | bytes 1327112 | tf_op jit(solution)/shard_map/ppermute | solution.py:282
  32.4 8.9 %collective-permute-done.7.refs_0_.refs_4_ = bf16[1728,128]{1,0:T(8,128)(2,1)S(1)} collective-permute-done((bf16[1728,128]{1,0:T(8,128)(2,1)S(1)}, bf16[1728,128]{1,0:T(8,128)(2,1)S(1)}, u32[]{:S(2)}, u32[]{:S(2)}) %collective-permute-start.7) | collective-permute-done | bytes 442400 | tf_op jit(solution)/shard_map/ppermute | solution.py:276
  41.4 1.2 %collective-permute-done.8.refs_1_.refs_5_ = bf16[1728,128]{1,0:T(8,128)(2,1)S(1)} collective-permute-done((bf16[1728,128]{1,0:T(8,128)(2,1)S(1)}, bf16[1728,128]{1,0:T(8,128)(2,1)S(1)}, u32[]{:S(2)}, u32[]{:S(2)}) %collective-permute-start.8) | collective-permute-done | bytes 442400 | tf_op jit(solution)/shard_map/ppermute | solution.py:279
  42.6 2.4 %collective-permute-done.1.refs_2_.refs_0_ = bf16[1728,128]{1,0:T(8,128)(2,1)S(1)} collective-permute-done((bf16[1728,128]{1,0:T(8,128)(2,1)S(1)}, bf16[1728,128]{1,0:T(8,128)(2,1)S(1)}, u32[]{:S(2)}, u32[]{:S(2)}) %collective-permute-start.1) | collective-permute-done | bytes 442400 | tf_op jit(solution)/shard_map/ppermute | solution.py:282
  45.0 0.1 rearranged.6
  45.0 0.1 collective-permute-start.9
  45.1 0.0 copy-start.3
  45.1 0.0 copy-start.4
  45.2 0.1 collective-permute-start.3
  45.2 1.0 %collective-permute-start.2 = (bf16[1728,128]{1,0:T(8,128)(2,1)S(1)}, bf16[1728,128]{1,0:T(8,128)(2,1)S(1)}, u32[]{:S(2)}, u32[]{:S(2)}) collective-permute-start(bf16[1728,128]{1,0:T(8,128)(2,1)S(1)} %collective-permute-done.1.refs_2_.refs_0_), channel_id=1, source_target_pairs={{0,2},{1,3},{2,4},{3,5},{4,6},{5,7},{6,0},{7,1},{8,10},{9,11},{10,... | collective-permute-start | bytes 1327112 | tf_op jit(solution)/shard_map/ppermute | solution.py:282
  46.2 1.3 %collective-permute-done.9.refs_6_ = bf16[3456,128]{1,0:T(8,128)(2,1)S(1)} collective-permute-done((bf16[3456,128]{1,0:T(8,128)(2,1)S(1)}, bf16[3456,128]{1,0:T(8,128)(2,1)S(1)}, u32[]{:S(2)}, u32[]{:S(2)}) %collective-permute-start.9) | collective-permute-done | bytes 884768 | tf_op jit(solution)/shard_map/ppermute | solution.py:273
  47.5 0.0 collective-permute-done.6.refs_1_
  47.5 0.5 rearranged.7.refs_2_
  48.0 0.0 copy-done.3
  48.0 0.0 copy-done.4
  48.0 0.0 copy-start
  48.0 6.6 %products.3 = (bf16[8,4,8,576]{3,2,1,0:T(8,128)(2,1)S(1)}, bf16[8,4,8,576]{3,2,1,0:T(8,128)(2,1)S(1)}, bf16[8,4,8,576]{3,2,1,0:T(8,128)(2,1)S(1)}, bf16[8,4,8,576]{3,2,1,0:T(8,128)(2,1)S(1)}, f32[8,128]{1,0:T(8,128)S(1)}) custom-call(s32[4,4]{1,0:T(4,128)S(1)} %copy-done.4, bf16[64,128]{1,0:T(8,128)(2,1)S(1)} %copy-done.3, ...), custom_call_target="tpu_custom_call" | custom-call | flops 1811939328 | bytes 8388608 | tf_op jit(solution)/shard_map/jit(products_of)/products/pallas_call | solution.py:191
  54.6 0.0 copy-done
  54.7 5.3 %collective-permute-done.3.refs_0_ = bf16[1728,128]{1,0:T(8,128)(2,1)S(1)} collective-permute-done((bf16[1728,128]{1,0:T(8,128)(2,1)S(1)}, bf16[1728,128]{1,0:T(8,128)(2,1)S(1)}, u32[]{:S(2)}, u32[]{:S(2)}) %collective-permute-start.3) | collective-permute-done | bytes 442400 | tf_op jit(solution)/shard_map/ppermute | solution.py:282
  60.0 0.0 collective-permute-start.10
  60.0 1.2 %collective-permute-start.11 = (bf16[8,4,8,576]{3,2,1,0:T(8,128)(2,1)S(1)}, bf16[8,4,8,576]{3,2,1,0:T(8,128)(2,1)S(1)}, u32[]{:S(2)}, u32[]{:S(2)}) collective-permute-start(bf16[8,4,8,576]{3,2,1,0:T(8,128)(2,1)S(1)} %get-tuple-element.28), channel_id=1, source_target_pairs={{0,1},{1,0},{2,3},{3,2},{4,5},{5,4},{6,7},{7,6},{8,9},{9,8},{10,11... | collective-permute-start | bytes 884744 | tf_op jit(solution)/shard_map/ppermute | solution.py:279
  61.2 0.9 collective-permute-start.12
  62.0 0.0 copy-start.1
  62.0 3.0 %copy-done.1 = bf16[27648,128]{1,0:T(8,128)(2,1)S(1)} copy-done((bf16[27648,128]{1,0:T(8,128)(2,1)S(1)}, bf16[27648,128]{1,0:T(8,128)(2,1)}, u32[]{:S(2)}) %copy-start.1) | copy-done | bytes 7077912
  65.0 0.0 copy-start.2
  65.0 5.0 %products.5 = (bf16[8,4,8,576]{3,2,1,0:T(8,128)(2,1)S(1)}, bf16[8,4,8,576]{3,2,1,0:T(8,128)(2,1)S(1)}, f32[8,128]{1,0:T(8,128)}) custom-call(s32[4,4]{1,0:T(4,128)S(1)} %copy-done.4, bf16[64,128]{1,0:T(8,128)(2,1)S(1)} %copy-done.3, bf16[1728,128]{1,0:T(8,128)(2,1)S(1)} %collective-permute-done.1.refs_2_.refs_0_, bf16[1728,128]{1,0:T(8,128)(2,1)S(1)} %paced.3.refs_1_, ...), custom_call_target="tpu_custom_call" | custom-call | flops 905969664 | bytes 8388608 | tf_op jit(solution)/shard_map/jit(products_of)/products/pallas_call | solution.py:191
  70.0 1.2 %collective-permute-start.13 = (bf16[8,4,8,576]{3,2,1,0:T(8,128)(2,1)S(1)}, bf16[8,4,8,576]{3,2,1,0:T(8,128)(2,1)S(1)}, u32[]{:S(2)}, u32[]{:S(2)}) collective-permute-start(bf16[8,4,8,576]{3,2,1,0:T(8,128)(2,1)S(1)} %get-tuple-element.32), channel_id=1, source_target_pairs={{0,1},{1,0},{2,3},{3,2},{4,5},{5,4},{6,7},{7,6},{8,9},{9,8},{10,11... | collective-permute-start | bytes 884744 | tf_op jit(solution)/shard_map/ppermute | solution.py:279
  71.2 0.0 collective-permute-done.2.refs_0_
  71.2 7.3 %collective-permute-done.10.refs_1_ = bf16[1728,128]{1,0:T(8,128)(2,1)S(1)} collective-permute-done((bf16[1728,128]{1,0:T(8,128)(2,1)S(1)}, bf16[1728,128]{1,0:T(8,128)(2,1)S(1)}, u32[]{:S(2)}, u32[]{:S(2)}) %collective-permute-start.10) | collective-permute-done | bytes 442400 | tf_op jit(solution)/shard_map/ppermute | solution.py:282
  78.5 0.0 copy-done.2
  78.5 4.5 %products.4 = (bf16[8,4,8,576]{3,2,1,0:T(8,128)(2,1)S(1)}, bf16[8,4,8,576]{3,2,1,0:T(8,128)(2,1)S(1)}, f32[8,128]{1,0:T(8,128)S(1)}) custom-call(s32[4,4]{1,0:T(4,128)S(1)} %copy-done.4, bf16[64,128]{1,0:T(8,128)(2,1)S(1)} %copy-done.3, bf16[1728,128]{1,0:T(8,128)(2,1)S(1)} %collective-permute-done.2.refs_0_, ...), custom_call_target="tpu_custom_call" | custom-call | flops 905969664 | bytes 8388608 | tf_op jit(solution)/shard_map/jit(products_of)/products/pallas_call | solution.py:191
  83.0 1.2 %collective-permute-start.14 = (bf16[8,4,8,576]{3,2,1,0:T(8,128)(2,1)S(1)}, bf16[8,4,8,576]{3,2,1,0:T(8,128)(2,1)S(1)}, u32[]{:S(2)}, u32[]{:S(2)}) collective-permute-start(bf16[8,4,8,576]{3,2,1,0:T(8,128)(2,1)S(1)} %get-tuple-element.34), channel_id=1, source_target_pairs={{0,1},{1,0},{2,3},{3,2},{4,5},{5,4},{6,7},{7,6},{8,9},{9,8},{10,11... | collective-permute-start | bytes 884744 | tf_op jit(solution)/shard_map/ppermute | solution.py:279
  84.3 0.8 bitcast_dynamic-update-slice_fusion.7
  85.0 0.0 collective-permute-done.11
  85.0 0.8 bitcast_dynamic-update-slice_fusion.6
  85.8 0.8 bitcast_dynamic-update-slice_fusion.5
  86.5 0.0 collective-permute-done.12
  86.5 0.8 bitcast_dynamic-update-slice_fusion.4
  87.3 0.8 bitcast_dynamic-update-slice_fusion.3
  88.0 0.0 collective-permute-done.13
  88.0 0.8 bitcast_dynamic-update-slice_fusion.2
  88.8 0.8 bitcast_dynamic-update-slice_fusion.1
  89.5 2.8 %collective-permute-done.14 = bf16[8,4,8,576]{3,2,1,0:T(8,128)(2,1)S(1)} collective-permute-done((bf16[8,4,8,576]{3,2,1,0:T(8,128)(2,1)S(1)}, bf16[8,4,8,576]{3,2,1,0:T(8,128)(2,1)S(1)}, u32[]{:S(2)}, u32[]{:S(2)}) %collective-permute-start.14) | collective-permute-done | bytes 294944 | tf_op jit(solution)/shard_map/ppermute | solution.py:279
  92.4 0.8 bitcast_dynamic-update-slice_fusion
  (3 shorter events, 0.0 us)
Async XLA Ops:
  3.0 24.7 %collective-permute-start = (bf16[3456,128]{1,0:T(8,128)(2,1)S(1)}, bf16[3456,128]{1,0:T(8,128)(2,1)S(1)}, u32[]{:S(2)}, u32[]{:S(2)}) collective-permute-start(bf16[3456,128]{1,0:T(8,128)(2,1)S(1)} %prepare.1.refs_0_), channel_id=1, source_target_pairs={{0,2},{1,3},{2,4},{3,5},{4,6},{5,7},{6,0},{7,1},{8,10},{9,11},{10,... | collective-permute-start | bytes 2654216 | tf_op jit(solution)/shard_map/ppermute | solution.py:282
  6.0 21.7 %collective-permute-start.4 = (bf16[3456,128]{1,0:T(8,128)(2,1)S(1)}, bf16[3456,128]{1,0:T(8,128)(2,1)S(1)}, u32[]{:S(2)}, u32[]{:S(2)}) collective-permute-start(bf16[3456,128]{1,0:T(8,128)(2,1)S(1)} %prepare.1.refs_0_), channel_id=1, source_target_pairs={{0,1},{1,0},{2,3},{3,2},{4,5},{5,4},{6,7},{7,6},{8,9},{9,8},{10,11... | collective-permute-start | bytes 2654216 | tf_op jit(solution)/shard_map/ppermute | solution.py:279
  7.5 20.8 %collective-permute-start.5 = (bf16[3456,128]{1,0:T(8,128)(2,1)S(1)}, bf16[3456,128]{1,0:T(8,128)(2,1)S(1)}, u32[]{:S(2)}, u32[]{:S(2)}) collective-permute-start(bf16[3456,128]{1,0:T(8,128)(2,1)S(1)} %prepare.1.refs_0_), channel_id=1, source_target_pairs={{0,16},{8,24},{16,0},{24,8},{1,17},{9,25},{17,1},{25,9},{2,18},{10... | collective-permute-start | bytes 2654216 | tf_op jit(solution)/shard_map/ppermute | solution.py:276
  28.6 18.9 %collective-permute-start.6 = (bf16[10368,128]{1,0:T(8,128)(2,1)S(1)}, bf16[10368,128]{1,0:T(8,128)(2,1)S(1)}, u32[]{:S(2)}, u32[]{:S(2)}) collective-permute-start(bf16[10368,128]{1,0:T(8,128)(2,1)S(1)} %get-tuple-element.22), channel_id=1, source_target_pairs={{0,8},{8,0},{16,24},{24,16},{1,9},{9,1},{17,25},{25,17},{2,10},{10... | collective-permute-start | bytes 7962632 | tf_op jit(solution)/shard_map/ppermute | solution.py:273
  28.7 12.6 %collective-permute-start.7 = (bf16[1728,128]{1,0:T(8,128)(2,1)S(1)}, bf16[1728,128]{1,0:T(8,128)(2,1)S(1)}, u32[]{:S(2)}, u32[]{:S(2)}) collective-permute-start(bf16[1728,128]{1,0:T(8,128)(2,1)S(1)} %get-tuple-element.23), channel_id=1, source_target_pairs={{0,16},{8,24},{16,0},{24,8},{1,17},{9,25},{17,1},{25,9},{2,18},{10... | collective-permute-start | bytes 1327112 | tf_op jit(solution)/shard_map/ppermute | solution.py:276
  30.3 12.3 %collective-permute-start.8 = (bf16[1728,128]{1,0:T(8,128)(2,1)S(1)}, bf16[1728,128]{1,0:T(8,128)(2,1)S(1)}, u32[]{:S(2)}, u32[]{:S(2)}) collective-permute-start(bf16[1728,128]{1,0:T(8,128)(2,1)S(1)} %get-tuple-element.24), channel_id=1, source_target_pairs={{0,1},{1,0},{2,3},{3,2},{4,5},{5,4},{6,7},{7,6},{8,9},{9,8},{10,11... | collective-permute-start | bytes 1327112 | tf_op jit(solution)/shard_map/ppermute | solution.py:279
  31.2 13.8 %collective-permute-start.1 = (bf16[1728,128]{1,0:T(8,128)(2,1)S(1)}, bf16[1728,128]{1,0:T(8,128)(2,1)S(1)}, u32[]{:S(2)}, u32[]{:S(2)}) collective-permute-start(bf16[1728,128]{1,0:T(8,128)(2,1)S(1)} %get-tuple-element.20), channel_id=1, source_target_pairs={{0,2},{1,3},{2,4},{3,5},{4,6},{5,7},{6,0},{7,1},{8,10},{9,11},{10,... | collective-permute-start | bytes 1327112 | tf_op jit(solution)/shard_map/ppermute | solution.py:282
  45.0 2.5 %collective-permute-start.9 = (bf16[3456,128]{1,0:T(8,128)(2,1)S(1)}, bf16[3456,128]{1,0:T(8,128)(2,1)S(1)}, u32[]{:S(2)}, u32[]{:S(2)}) collective-permute-start(bf16[3456,128]{1,0:T(8,128)(2,1)S(1)} %rearranged.6), channel_id=1, source_target_pairs={{0,8},{8,0},{16,24},{24,16},{1,9},{9,1},{17,25},{25,17},{2,10},{10... | collective-permute-start | bytes 2654216 | tf_op jit(solution)/shard_map/ppermute | solution.py:273
  45.1 2.9 %copy-start.3 = (bf16[64,128]{1,0:T(8,128)(2,1)S(1)}, bf16[64,128]{1,0:T(8,128)(2,1)}, u32[]{:S(2)}) copy-start(bf16[64,128]{1,0:T(8,128)(2,1)} %constant.51.clone.turn_ref) | copy-start | bytes 49156
  45.1 2.9 %copy-start.4 = (s32[4,4]{1,0:T(4,128)S(1)}, s32[4,4]{1,0:T(4,128)}, u32[]{:S(2)}) copy-start(s32[4,4]{1,0:T(4,128)} %mask_ref.5) | copy-start | bytes 196
  45.2 14.8 %collective-permute-start.3 = (bf16[1728,128]{1,0:T(8,128)(2,1)S(1)}, bf16[1728,128]{1,0:T(8,128)(2,1)S(1)}, u32[]{:S(2)}, u32[]{:S(2)}) collective-permute-start(bf16[1728,128]{1,0:T(8,128)(2,1)S(1)} %get-tuple-element.21), channel_id=1, source_target_pairs={{0,2},{1,3},{2,4},{3,5},{4,6},{5,7},{6,0},{7,1},{8,10},{9,11},{10,... | collective-permute-start | bytes 1327112 | tf_op jit(solution)/shard_map/ppermute | solution.py:282
  45.2 26.0 %collective-permute-start.2 = (bf16[1728,128]{1,0:T(8,128)(2,1)S(1)}, bf16[1728,128]{1,0:T(8,128)(2,1)S(1)}, u32[]{:S(2)}, u32[]{:S(2)}) collective-permute-start(bf16[1728,128]{1,0:T(8,128)(2,1)S(1)} %collective-permute-done.1.refs_2_.refs_0_), channel_id=1, source_target_pairs={{0,2},{1,3},{2,4},{3,5},{4,6},{5,7},{6,0},{7,1},{8,10},{9,11},{10,... | collective-permute-start | bytes 1327112 | tf_op jit(solution)/shard_map/ppermute | solution.py:282
  48.0 6.6 %copy-start = (bf16[27648,128]{1,0:T(8,128)(2,1)}, bf16[27648,128]{1,0:T(8,128)(2,1)S(1)}, u32[]{:S(2)}) copy-start(bf16[27648,128]{1,0:T(8,128)(2,1)S(1)} %rearranged.7.refs_2_) | copy-start | bytes 21233668
  60.0 18.5 %collective-permute-start.10 = (bf16[1728,128]{1,0:T(8,128)(2,1)S(1)}, bf16[1728,128]{1,0:T(8,128)(2,1)S(1)}, u32[]{:S(2)}, u32[]{:S(2)}) collective-permute-start(bf16[1728,128]{1,0:T(8,128)(2,1)S(1)} %paced.3.refs_1_), channel_id=1, source_target_pairs={{0,2},{1,3},{2,4},{3,5},{4,6},{5,7},{6,0},{7,1},{8,10},{9,11},{10,... | collective-permute-start | bytes 1327112 | tf_op jit(solution)/shard_map/ppermute | solution.py:282
  60.0 25.0 %collective-permute-start.11 = (bf16[8,4,8,576]{3,2,1,0:T(8,128)(2,1)S(1)}, bf16[8,4,8,576]{3,2,1,0:T(8,128)(2,1)S(1)}, u32[]{:S(2)}, u32[]{:S(2)}) collective-permute-start(bf16[8,4,8,576]{3,2,1,0:T(8,128)(2,1)S(1)} %get-tuple-element.28), channel_id=1, source_target_pairs={{0,1},{1,0},{2,3},{3,2},{4,5},{5,4},{6,7},{7,6},{8,9},{9,8},{10,11... | collective-permute-start | bytes 884744 | tf_op jit(solution)/shard_map/ppermute | solution.py:279
  61.2 25.4 %collective-permute-start.12 = (bf16[8,4,8,576]{3,2,1,0:T(8,128)(2,1)S(1)}, bf16[8,4,8,576]{3,2,1,0:T(8,128)(2,1)S(1)}, u32[]{:S(2)}, u32[]{:S(2)}) collective-permute-start(bf16[8,4,8,576]{3,2,1,0:T(8,128)(2,1)S(1)} %get-tuple-element.30), channel_id=1, source_target_pairs={{0,1},{1,0},{2,3},{3,2},{4,5},{5,4},{6,7},{7,6},{8,9},{9,8},{10,11... | collective-permute-start | bytes 884744 | tf_op jit(solution)/shard_map/ppermute | solution.py:279
  62.0 3.0 %copy-start.1 = (bf16[27648,128]{1,0:T(8,128)(2,1)S(1)}, bf16[27648,128]{1,0:T(8,128)(2,1)}, u32[]{:S(2)}) copy-start(bf16[27648,128]{1,0:T(8,128)(2,1)} %copy-done) | copy-start | bytes 21233668
  65.0 13.5 %copy-start.2 = (bf16[27648,128]{1,0:T(8,128)(2,1)S(1)}, bf16[27648,128]{1,0:T(8,128)(2,1)}, u32[]{:S(2)}) copy-start(bf16[27648,128]{1,0:T(8,128)(2,1)} %copy-done) | copy-start | bytes 21233668
  70.0 18.0 %collective-permute-start.13 = (bf16[8,4,8,576]{3,2,1,0:T(8,128)(2,1)S(1)}, bf16[8,4,8,576]{3,2,1,0:T(8,128)(2,1)S(1)}, u32[]{:S(2)}, u32[]{:S(2)}) collective-permute-start(bf16[8,4,8,576]{3,2,1,0:T(8,128)(2,1)S(1)} %get-tuple-element.32), channel_id=1, source_target_pairs={{0,1},{1,0},{2,3},{3,2},{4,5},{5,4},{6,7},{7,6},{8,9},{9,8},{10,11... | collective-permute-start | bytes 884744 | tf_op jit(solution)/shard_map/ppermute | solution.py:279
  83.0 9.3 %collective-permute-start.14 = (bf16[8,4,8,576]{3,2,1,0:T(8,128)(2,1)S(1)}, bf16[8,4,8,576]{3,2,1,0:T(8,128)(2,1)S(1)}, u32[]{:S(2)}, u32[]{:S(2)}) collective-permute-start(bf16[8,4,8,576]{3,2,1,0:T(8,128)(2,1)S(1)} %get-tuple-element.34), channel_id=1, source_target_pairs={{0,1},{1,0},{2,3},{3,2},{4,5},{5,4},{6,7},{7,6},{8,9},{9,8},{10,11... | collective-permute-start | bytes 884744 | tf_op jit(solution)/shard_map/ppermute | solution.py:279

commit v4 on v3

--- a/solution.py
+++ b/solution.py
@@ -16,7 +16,7 @@
 BLOCK_ROWS = GROUPS * GROUP_ROWS
 HALF_ROWS = BLOCK_ROWS // 2
 STATIONS = 8
-CUTS = (0, 4, 8)
+CUTS = (0, 5, 8)
 PACE = 80 * 2**20
 F32 = jnp.float32
 BF16 = jnp.bfloat16
@@ -289,17 +289,15 @@
     sources = [whole_at(own), whole_at(passing)]
     beside, high = over_x(own), over_high(own)
     cuts, ahead = [n * GROUP_ROWS for n in CUTS], []
-    if steps > 2:
-        listed = [[(0, start, end - start)] for start, end in zip(cuts, cuts[1:])]
-        ahead = [over_z(piece) for piece in rearranged([passing], listed)]
+    listed = [[(3, start, end - start)] for start, end in zip(cuts, cuts[1:])]
     mine, theirs = [whole_at(own)], [whole_at(beside)]
     if highs > 1:
         three = [(n, 0, BLOCK_ROWS) for n in range(3)]
-        joined, first, second = rearranged(
-            [own, beside, high],
-            [three, [(1, 0, HALF_ROWS)], [(2, HALF_ROWS, HALF_ROWS)]],
-            (passing,),
+        joined, first, second, *next_ = rearranged(
+            [own, beside, high, passing],
+            [three, [(1, 0, HALF_ROWS)], [(2, HALF_ROWS, HALF_ROWS)]] + (listed if steps > 2 else []),
         )
+        ahead = [over_z(piece) for piece in next_]
         joined = over_core(joined)
         mine += [whole_at(joined), whole_at(high), whole_at(joined, 2 * BLOCK_ROWS)]
         theirs += [whole_at(joined, BLOCK_ROWS)]
@@ -337,7 +335,8 @@
         *outs, token = products(block_mask, turn, batch, blocks, count, 1.0 / math.sqrt(segs))
         if k + 2 < steps:
             late = paced(late, (token,), PACE)
-        sources = [((early, 0), (late, 0))]
+        rows = [(n, 0, piece.shape[0]) for n, piece in enumerate((early, late))]
+        sources = [whole_at(rearranged([early, late], [rows])[0])]
         pieces += [(kept, over_x(sent)) for kept, sent in zip(outs[::2], outs[1::2])]
     result = blank((steps, 2, count, src_count, count, 576), token)
     for k, (kept, got) in enumerate(pieces):

time: 93.3 us -> 91.5 us (0.981)
  waiting for transfers between devices: 48.6 us -> 46.9 us
    ppermute x5, waiting for transfers between devices: 33.6 us -> 30.7 us  [over_z(): lax.ppermute(half, 'rcv', [(r, (r + 2) % rcv_count) for r in range(rcv_co...]
    ppermute x2, waiting for transfers between devices: 9.57 us -> 10.8 us  [over_high(): lax.ppermute(half, 'src', [(s, (s + 2) % src_count) for s in range(src_co...]
    ppermute x6, starting transfers between devices: 6.78 us -> 5.83 us  [over_x(): return lax.ppermute(half, 'rcv', [(r, r ^ 1) for r in range(rcv_count)])]
    unnamed x11 -> x9, local copies, waits for them, and re-layouts: 4.53 us -> 4.52 us
  transfers between devices with their start and end apart: 15 -> 15, of which waited for: 9 -> 10; matrix products, arithmetic and copies ran while one was open for 6% -> 6% of each run, Pallas kernels for 18% -> 18%
where the time goes in v4:
time: 91.5 us; the launch traced here: 91.3 us
  waiting for transfers between devices  46.9 us (51%)
  Pallas kernels  18.6 us (20%)
  starting transfers between devices  15.1 us (17%)
  local copies, waits for them, and re-layouts  10.5 us (11%)
    ppermute x5, waiting for transfers between devices, over_z(): lax.ppermute(half, 'rcv', [(r, (r + 2) % rcv_count) for r in range(rcv_co...  30.7 us
    pallas_call x3, Pallas kernels, products_of(): pl.pallas_call(functools.partial(products_kernel, layout, s, src_count, n...  16.2 us
    ppermute x2, waiting for transfers between devices, over_high(): lax.ppermute(half, 'src', [(s, (s + 2) % src_count) for s in range(src_co...  10.8 us
    ppermute x5, starting transfers between devices, over_z(): lax.ppermute(half, 'rcv', [(r, (r + 2) % rcv_count) for r in range(rcv_co...  6.11 us
    ppermute x6, starting transfers between devices, over_x(): return lax.ppermute(half, 'rcv', [(r, r ^ 1) for r in range(rcv_count)])  5.83 us
    unnamed x9, local copies, waits for them, and re-layouts  4.52 us
    ppermute x6, waiting for transfers between devices, over_x(): return lax.ppermute(half, 'rcv', [(r, r ^ 1) for r in range(rcv_count)])  4.37 us
    ppermute x2, starting transfers between devices, over_high(): lax.ppermute(half, 'src', [(s, (s + 2) % src_count) for s in range(src_co...  3.04 us
  transfers between devices with their start and end apart: 15, of which 10 were waited for; matrix products, arithmetic and copies ran while one was open for 6% of the time, Pallas kernels for 18%

profile of v4, /device:TPU:0, one launch (start us, length us, event | category | flops | bytes accessed | tf_op | source)
XLA Modules:
  0.0 91.3 jit_solution(13468207243462223271)
XLA Ops:
  0.0 1.5 %copy.6.x_ref = bf16[8,287,192]{2,1,0:T(8,128)(2,1)S(1)} copy(bf16[8,287,192]{2,0,1:T(8,128)(2,1)} %param.3) | data formatting | bytes 1763328 | tf_op args[0]
  1.5 1.5 %prepare.1.refs_0_ = bf16[3456,128]{1,0:T(8,128)(2,1)S(1)} custom-call(bf16[8,287,192]{2,1,0:T(8,128)(2,1)S(1)} %copy.6.x_ref), custom_call_target="tpu_custom_call" | custom-call | tf_op jit(solution)/shard_map/prepare/pallas_call | solution.py:72
  3.0 3.1 %collective-permute-start.2 = (bf16[3456,128]{1,0:T(8,128)(2,1)S(1)}, bf16[3456,128]{1,0:T(8,128)(2,1)S(1)}, u32[]{:S(2)}, u32[]{:S(2)}) collective-permute-start(bf16[3456,128]{1,0:T(8,128)(2,1)S(1)} %prepare.1.refs_0_), channel_id=1, source_target_pairs={{0,2},{1,3},{2,4},{3,5},{4,6},{5,7},{6,0},{7,1},{8,10},{9,11},{10,... | collective-permute-start | bytes 2654216 | tf_op jit(solution)/shard_map/ppermute | solution.py:282
  6.0 1.5 %collective-permute-start = (bf16[3456,128]{1,0:T(8,128)(2,1)S(1)}, bf16[3456,128]{1,0:T(8,128)(2,1)S(1)}, u32[]{:S(2)}, u32[]{:S(2)}) collective-permute-start(bf16[3456,128]{1,0:T(8,128)(2,1)S(1)} %prepare.1.refs_0_), channel_id=1, source_target_pairs={{0,1},{1,0},{2,3},{3,2},{4,5},{5,4},{6,7},{7,6},{8,9},{9,8},{10,11... | collective-permute-start | bytes 2654216 | tf_op jit(solution)/shard_map/ppermute | solution.py:279
  7.5 1.5 %collective-permute-start.1 = (bf16[3456,128]{1,0:T(8,128)(2,1)S(1)}, bf16[3456,128]{1,0:T(8,128)(2,1)S(1)}, u32[]{:S(2)}, u32[]{:S(2)}) collective-permute-start(bf16[3456,128]{1,0:T(8,128)(2,1)S(1)} %prepare.1.refs_0_), channel_id=1, source_target_pairs={{0,16},{8,24},{16,0},{24,8},{1,17},{9,25},{17,1},{25,9},{2,18},{10... | collective-permute-start | bytes 2654216 | tf_op jit(solution)/shard_map/ppermute | solution.py:276
  9.1 18.7 %collective-permute-done.2.refs_0_ = bf16[3456,128]{1,0:T(8,128)(2,1)S(1)} collective-permute-done((bf16[3456,128]{1,0:T(8,128)(2,1)S(1)}, bf16[3456,128]{1,0:T(8,128)(2,1)S(1)}, u32[]{:S(2)}, u32[]{:S(2)}) %collective-permute-start.2) | collective-permute-done | bytes 884768 | tf_op jit(solution)/shard_map/ppermute | solution.py:282
  27.7 0.0 collective-permute-done.refs_1_.refs_3_
  27.7 0.6 collective-permute-done.1.refs_2_
  28.4 0.3 rearranged.5
  28.7 0.1 collective-permute-start.6
  28.7 1.6 %collective-permute-start.3 = (bf16[2160,128]{1,0:T(8,128)(2,1)S(1)}, bf16[2160,128]{1,0:T(8,128)(2,1)S(1)}, u32[]{:S(2)}, u32[]{:S(2)}) collective-permute-start(bf16[2160,128]{1,0:T(8,128)(2,1)S(1)} %get-tuple-element.20), channel_id=1, source_target_pairs={{0,2},{1,3},{2,4},{3,5},{4,6},{5,7},{6,0},{7,1},{8,10},{9,11},{10,... | collective-permute-start | bytes 1658888 | tf_op jit(solution)/shard_map/ppermute | solution.py:282
  30.4 1.5 %collective-permute-start.7 = (bf16[1728,128]{1,0:T(8,128)(2,1)S(1)}, bf16[1728,128]{1,0:T(8,128)(2,1)S(1)}, u32[]{:S(2)}, u32[]{:S(2)}) collective-permute-start(bf16[1728,128]{1,0:T(8,128)(2,1)S(1)} %get-tuple-element.23), channel_id=1, source_target_pairs={{0,16},{8,24},{16,0},{24,8},{1,17},{9,25},{17,1},{25,9},{2,18},{10... | collective-permute-start | bytes 1327112 | tf_op jit(solution)/shard_map/ppermute | solution.py:276
  31.9 0.5 collective-permute-start.8
  32.4 10.2 %collective-permute-done.7.refs_0_.refs_4_ = bf16[1728,128]{1,0:T(8,128)(2,1)S(1)} collective-permute-done((bf16[1728,128]{1,0:T(8,128)(2,1)S(1)}, bf16[1728,128]{1,0:T(8,128)(2,1)S(1)}, u32[]{:S(2)}, u32[]{:S(2)}) %collective-permute-start.7) | collective-permute-done | bytes 442400 | tf_op jit(solution)/shard_map/ppermute | solution.py:276
  42.6 1.2 %collective-permute-done.8.refs_1_.refs_5_ = bf16[1728,128]{1,0:T(8,128)(2,1)S(1)} collective-permute-done((bf16[1728,128]{1,0:T(8,128)(2,1)S(1)}, bf16[1728,128]{1,0:T(8,128)(2,1)S(1)}, u32[]{:S(2)}, u32[]{:S(2)}) %collective-permute-start.8) | collective-permute-done | bytes 442400 | tf_op jit(solution)/shard_map/ppermute | solution.py:279
  43.8 1.6 %collective-permute-done.3.refs_2_.refs_0_ = bf16[2160,128]{1,0:T(8,128)(2,1)S(1)} collective-permute-done((bf16[2160,128]{1,0:T(8,128)(2,1)S(1)}, bf16[2160,128]{1,0:T(8,128)(2,1)S(1)}, u32[]{:S(2)}, u32[]{:S(2)}) %collective-permute-start.3) | collective-permute-done | bytes 552992 | tf_op jit(solution)/shard_map/ppermute | solution.py:282
  45.5 0.1 rearranged.6
  45.5 0.1 collective-permute-start.9
  45.6 0.0 copy-start.2
  45.6 0.0 copy-start.3
  45.6 0.1 collective-permute-start.5
  45.7 1.3 %collective-permute-start.4 = (bf16[2160,128]{1,0:T(8,128)(2,1)S(1)}, bf16[2160,128]{1,0:T(8,128)(2,1)S(1)}, u32[]{:S(2)}, u32[]{:S(2)}) collective-permute-start(bf16[2160,128]{1,0:T(8,128)(2,1)S(1)} %collective-permute-done.3.refs_2_.refs_0_), channel_id=1, source_target_pairs={{0,2},{1,3},{2,4},{3,5},{4,6},{5,7},{6,0},{7,1},{8,10},{9,11},{10,... | collective-permute-start | bytes 1658888 | tf_op jit(solution)/shard_map/ppermute | solution.py:282
  47.0 1.0 %collective-permute-done.9.refs_6_ = bf16[3456,128]{1,0:T(8,128)(2,1)S(1)} collective-permute-done((bf16[3456,128]{1,0:T(8,128)(2,1)S(1)}, bf16[3456,128]{1,0:T(8,128)(2,1)S(1)}, u32[]{:S(2)}, u32[]{:S(2)}) %collective-permute-start.9) | collective-permute-done | bytes 884768 | tf_op jit(solution)/shard_map/ppermute | solution.py:273
  48.0 0.0 collective-permute-done.6.refs_1_
  48.0 0.5 rearranged.7.refs_2_.refs_1_
  48.5 0.0 copy-done.2
  48.5 0.0 copy-done.3
  48.5 0.0 copy-start
  48.5 6.6 %products.3 = (bf16[8,4,8,576]{3,2,1,0:T(8,128)(2,1)S(1)}, bf16[8,4,8,576]{3,2,1,0:T(8,128)(2,1)S(1)}, bf16[8,4,8,576]{3,2,1,0:T(8,128)(2,1)S(1)}, bf16[8,4,8,576]{3,2,1,0:T(8,128)(2,1)S(1)}, f32[8,128]{1,0:T(8,128)S(1)}) custom-call(s32[4,4]{1,0:T(4,128)S(1)} %copy-done.3, bf16[64,128]{1,0:T(8,128)(2,1)S(1)} %copy-done.2, ...), custom_call_target="tpu_custom_call" | custom-call | flops 1811939328 | bytes 8388608 | tf_op jit(solution)/shard_map/jit(products_of)/products/pallas_call | solution.py:191
  55.1 0.0 copy-done
  55.1 2.9 %collective-permute-done.5.refs_0_ = bf16[1296,128]{1,0:T(8,128)(2,1)S(1)} collective-permute-done((bf16[1296,128]{1,0:T(8,128)(2,1)S(1)}, bf16[1296,128]{1,0:T(8,128)(2,1)S(1)}, u32[]{:S(2)}, u32[]{:S(2)}) %collective-permute-start.5) | collective-permute-done | bytes 331808 | tf_op jit(solution)/shard_map/ppermute | solution.py:282
  58.1 0.0 collective-permute-start.10
  58.1 0.9 collective-permute-start.11
  59.0 1.2 %collective-permute-start.12 = (bf16[8,4,8,576]{3,2,1,0:T(8,128)(2,1)S(1)}, bf16[8,4,8,576]{3,2,1,0:T(8,128)(2,1)S(1)}, u32[]{:S(2)}, u32[]{:S(2)}) collective-permute-start(bf16[8,4,8,576]{3,2,1,0:T(8,128)(2,1)S(1)} %get-tuple-element.30), channel_id=1, source_target_pairs={{0,1},{1,0},{2,3},{3,2},{4,5},{5,4},{6,7},{7,6},{8,9},{9,8},{10,11... | collective-permute-start | bytes 884744 | tf_op jit(solution)/shard_map/ppermute | solution.py:279
  60.1 0.1 rearranged.9.refs_0_
  60.2 0.0 copy-start.1
  60.2 3.0 %copy-done.1 = bf16[27648,128]{1,0:T(8,128)(2,1)S(1)} copy-done((bf16[27648,128]{1,0:T(8,128)(2,1)S(1)}, bf16[27648,128]{1,0:T(8,128)(2,1)}, u32[]{:S(2)}) %copy-start.1) | copy-done | bytes 7077912
  63.2 5.0 %products.5 = (bf16[8,4,8,576]{3,2,1,0:T(8,128)(2,1)S(1)}, bf16[8,4,8,576]{3,2,1,0:T(8,128)(2,1)S(1)}, f32[8,128]{1,0:T(8,128)}) custom-call(s32[4,4]{1,0:T(4,128)S(1)} %copy-done.3, bf16[64,128]{1,0:T(8,128)(2,1)S(1)} %copy-done.2, bf16[3456,128]{1,0:T(8,128)(2,1)S(1)} %rearranged.9.refs_0_, bf16[27648,128]{1,0:T(8,128)(2,1)S(1)} %copy-done.1), custom_call_target="tpu_custom_call" | custom-call | flops 905969664 | bytes 8388608 | tf_op jit(solution)/shard_map/jit(products_of)/products/pallas_call | solution.py:191
  68.2 0.9 collective-permute-start.13
  69.1 0.8 collective-permute-done.4.refs_0_
  69.9 6.6 %collective-permute-done.10.refs_1_ = bf16[1296,128]{1,0:T(8,128)(2,1)S(1)} collective-permute-done((bf16[1296,128]{1,0:T(8,128)(2,1)S(1)}, bf16[1296,128]{1,0:T(8,128)(2,1)S(1)}, u32[]{:S(2)}, u32[]{:S(2)}) %collective-permute-start.10) | collective-permute-done | bytes 331808 | tf_op jit(solution)/shard_map/ppermute | solution.py:282
  76.6 0.1 rearranged.8.refs_0_
  76.7 4.5 %products.4 = (bf16[8,4,8,576]{3,2,1,0:T(8,128)(2,1)S(1)}, bf16[8,4,8,576]{3,2,1,0:T(8,128)(2,1)S(1)}, f32[8,128]{1,0:T(8,128)S(1)}) custom-call(s32[4,4]{1,0:T(4,128)S(1)} %copy-done.3, bf16[64,128]{1,0:T(8,128)(2,1)S(1)} %copy-done.2, bf16[3456,128]{1,0:T(8,128)(2,1)S(1)} %rearranged.8.refs_0_, bf16[27648,128]{1,0:T(8,128)(2,1)S(1)} %copy-done.1), custom_call_target="tpu_custom_call" | custom-call | flops 905969664 | bytes 8388608 | tf_op jit(solution)/shard_map/jit(products_of)/products/pallas_call | solution.py:191
  81.2 0.9 %collective-permute-start.14 = (bf16[8,4,8,576]{3,2,1,0:T(8,128)(2,1)S(1)}, bf16[8,4,8,576]{3,2,1,0:T(8,128)(2,1)S(1)}, u32[]{:S(2)}, u32[]{:S(2)}) collective-permute-start(bf16[8,4,8,576]{3,2,1,0:T(8,128)(2,1)S(1)} %get-tuple-element.34), channel_id=1, source_target_pairs={{0,1},{1,0},{2,3},{3,2},{4,5},{5,4},{6,7},{7,6},{8,9},{9,8},{10,11... | collective-permute-start | bytes 884744 | tf_op jit(solution)/shard_map/ppermute | solution.py:279
  82.1 0.8 bitcast_dynamic-update-slice_fusion.7
  82.9 0.0 collective-permute-done.11
  82.9 0.8 bitcast_dynamic-update-slice_fusion.6
  83.6 0.8 bitcast_dynamic-update-slice_fusion.5
  84.4 0.0 collective-permute-done.12
  84.4 0.8 bitcast_dynamic-update-slice_fusion.4
  85.1 0.8 bitcast_dynamic-update-slice_fusion.3
  85.9 0.0 collective-permute-done.13
  85.9 0.8 bitcast_dynamic-update-slice_fusion.2
  86.7 0.8 bitcast_dynamic-update-slice_fusion.1
  87.4 3.1 %collective-permute-done.14 = bf16[8,4,8,576]{3,2,1,0:T(8,128)(2,1)S(1)} collective-permute-done((bf16[8,4,8,576]{3,2,1,0:T(8,128)(2,1)S(1)}, bf16[8,4,8,576]{3,2,1,0:T(8,128)(2,1)S(1)}, u32[]{:S(2)}, u32[]{:S(2)}) %collective-permute-start.14) | collective-permute-done | bytes 294944 | tf_op jit(solution)/shard_map/ppermute | solution.py:279
  90.5 0.8 bitcast_dynamic-update-slice_fusion
  (3 shorter events, 0.0 us)
Async XLA Ops:
  3.0 24.7 %collective-permute-start.2 = (bf16[3456,128]{1,0:T(8,128)(2,1)S(1)}, bf16[3456,128]{1,0:T(8,128)(2,1)S(1)}, u32[]{:S(2)}, u32[]{:S(2)}) collective-permute-start(bf16[3456,128]{1,0:T(8,128)(2,1)S(1)} %prepare.1.refs_0_), channel_id=1, source_target_pairs={{0,2},{1,3},{2,4},{3,5},{4,6},{5,7},{6,0},{7,1},{8,10},{9,11},{10,... | collective-permute-start | bytes 2654216 | tf_op jit(solution)/shard_map/ppermute | solution.py:282
  6.0 21.7 %collective-permute-start = (bf16[3456,128]{1,0:T(8,128)(2,1)S(1)}, bf16[3456,128]{1,0:T(8,128)(2,1)S(1)}, u32[]{:S(2)}, u32[]{:S(2)}) collective-permute-start(bf16[3456,128]{1,0:T(8,128)(2,1)S(1)} %prepare.1.refs_0_), channel_id=1, source_target_pairs={{0,1},{1,0},{2,3},{3,2},{4,5},{5,4},{6,7},{7,6},{8,9},{9,8},{10,11... | collective-permute-start | bytes 2654216 | tf_op jit(solution)/shard_map/ppermute | solution.py:279
  7.5 20.8 %collective-permute-start.1 = (bf16[3456,128]{1,0:T(8,128)(2,1)S(1)}, bf16[3456,128]{1,0:T(8,128)(2,1)S(1)}, u32[]{:S(2)}, u32[]{:S(2)}) collective-permute-start(bf16[3456,128]{1,0:T(8,128)(2,1)S(1)} %prepare.1.refs_0_), channel_id=1, source_target_pairs={{0,16},{8,24},{16,0},{24,8},{1,17},{9,25},{17,1},{25,9},{2,18},{10... | collective-permute-start | bytes 2654216 | tf_op jit(solution)/shard_map/ppermute | solution.py:276
  28.7 19.4 %collective-permute-start.6 = (bf16[10368,128]{1,0:T(8,128)(2,1)S(1)}, bf16[10368,128]{1,0:T(8,128)(2,1)S(1)}, u32[]{:S(2)}, u32[]{:S(2)}) collective-permute-start(bf16[10368,128]{1,0:T(8,128)(2,1)S(1)} %get-tuple-element.22), channel_id=1, source_target_pairs={{0,8},{8,0},{16,24},{24,16},{1,9},{9,1},{17,25},{25,17},{2,10},{10... | collective-permute-start | bytes 7962632 | tf_op jit(solution)/shard_map/ppermute | solution.py:273
  28.7 16.7 %collective-permute-start.3 = (bf16[2160,128]{1,0:T(8,128)(2,1)S(1)}, bf16[2160,128]{1,0:T(8,128)(2,1)S(1)}, u32[]{:S(2)}, u32[]{:S(2)}) collective-permute-start(bf16[2160,128]{1,0:T(8,128)(2,1)S(1)} %get-tuple-element.20), channel_id=1, source_target_pairs={{0,2},{1,3},{2,4},{3,5},{4,6},{5,7},{6,0},{7,1},{8,10},{9,11},{10,... | collective-permute-start | bytes 1658888 | tf_op jit(solution)/shard_map/ppermute | solution.py:282
  30.4 12.2 %collective-permute-start.7 = (bf16[1728,128]{1,0:T(8,128)(2,1)S(1)}, bf16[1728,128]{1,0:T(8,128)(2,1)S(1)}, u32[]{:S(2)}, u32[]{:S(2)}) collective-permute-start(bf16[1728,128]{1,0:T(8,128)(2,1)S(1)} %get-tuple-element.23), channel_id=1, source_target_pairs={{0,16},{8,24},{16,0},{24,8},{1,17},{9,25},{17,1},{25,9},{2,18},{10... | collective-permute-start | bytes 1327112 | tf_op jit(solution)/shard_map/ppermute | solution.py:276
  31.9 12.0 %collective-permute-start.8 = (bf16[1728,128]{1,0:T(8,128)(2,1)S(1)}, bf16[1728,128]{1,0:T(8,128)(2,1)S(1)}, u32[]{:S(2)}, u32[]{:S(2)}) collective-permute-start(bf16[1728,128]{1,0:T(8,128)(2,1)S(1)} %get-tuple-element.24), channel_id=1, source_target_pairs={{0,1},{1,0},{2,3},{3,2},{4,5},{5,4},{6,7},{7,6},{8,9},{9,8},{10,11... | collective-permute-start | bytes 1327112 | tf_op jit(solution)/shard_map/ppermute | solution.py:279
  45.5 2.5 %collective-permute-start.9 = (bf16[3456,128]{1,0:T(8,128)(2,1)S(1)}, bf16[3456,128]{1,0:T(8,128)(2,1)S(1)}, u32[]{:S(2)}, u32[]{:S(2)}) collective-permute-start(bf16[3456,128]{1,0:T(8,128)(2,1)S(1)} %rearranged.6), channel_id=1, source_target_pairs={{0,8},{8,0},{16,24},{24,16},{1,9},{9,1},{17,25},{25,17},{2,10},{10... | collective-permute-start | bytes 2654216 | tf_op jit(solution)/shard_map/ppermute | solution.py:273
  45.6 2.9 %copy-start.2 = (bf16[64,128]{1,0:T(8,128)(2,1)S(1)}, bf16[64,128]{1,0:T(8,128)(2,1)}, u32[]{:S(2)}) copy-start(bf16[64,128]{1,0:T(8,128)(2,1)} %constant.51.clone.turn_ref) | copy-start | bytes 49156
  45.6 2.9 %copy-start.3 = (s32[4,4]{1,0:T(4,128)S(1)}, s32[4,4]{1,0:T(4,128)}, u32[]{:S(2)}) copy-start(s32[4,4]{1,0:T(4,128)} %mask_ref.5) | copy-start | bytes 196
  45.6 12.5 %collective-permute-start.5 = (bf16[1296,128]{1,0:T(8,128)(2,1)S(1)}, bf16[1296,128]{1,0:T(8,128)(2,1)S(1)}, u32[]{:S(2)}, u32[]{:S(2)}) collective-permute-start(bf16[1296,128]{1,0:T(8,128)(2,1)S(1)} %get-tuple-element.21), channel_id=1, source_target_pairs={{0,2},{1,3},{2,4},{3,5},{4,6},{5,7},{6,0},{7,1},{8,10},{9,11},{10,... | collective-permute-start | bytes 995336 | tf_op jit(solution)/shard_map/ppermute | solution.py:282
  45.7 24.2 %collective-permute-start.4 = (bf16[2160,128]{1,0:T(8,128)(2,1)S(1)}, bf16[2160,128]{1,0:T(8,128)(2,1)S(1)}, u32[]{:S(2)}, u32[]{:S(2)}) collective-permute-start(bf16[2160,128]{1,0:T(8,128)(2,1)S(1)} %collective-permute-done.3.refs_2_.refs_0_), channel_id=1, source_target_pairs={{0,2},{1,3},{2,4},{3,5},{4,6},{5,7},{6,0},{7,1},{8,10},{9,11},{10,... | collective-permute-start | bytes 1658888 | tf_op jit(solution)/shard_map/ppermute | solution.py:282
  48.5 6.6 %copy-start = (bf16[27648,128]{1,0:T(8,128)(2,1)}, bf16[27648,128]{1,0:T(8,128)(2,1)S(1)}, u32[]{:S(2)}) copy-start(bf16[27648,128]{1,0:T(8,128)(2,1)S(1)} %rearranged.7.refs_2_.refs_1_) | copy-start | bytes 21233668
  58.1 18.5 %collective-permute-start.10 = (bf16[1296,128]{1,0:T(8,128)(2,1)S(1)}, bf16[1296,128]{1,0:T(8,128)(2,1)S(1)}, u32[]{:S(2)}, u32[]{:S(2)}) collective-permute-start(bf16[1296,128]{1,0:T(8,128)(2,1)S(1)} %paced.3.refs_1_), channel_id=1, source_target_pairs={{0,2},{1,3},{2,4},{3,5},{4,6},{5,7},{6,0},{7,1},{8,10},{9,11},{10,... | collective-permute-start | bytes 995336 | tf_op jit(solution)/shard_map/ppermute | solution.py:282
  58.1 24.8 %collective-permute-start.11 = (bf16[8,4,8,576]{3,2,1,0:T(8,128)(2,1)S(1)}, bf16[8,4,8,576]{3,2,1,0:T(8,128)(2,1)S(1)}, u32[]{:S(2)}, u32[]{:S(2)}) collective-permute-start(bf16[8,4,8,576]{3,2,1,0:T(8,128)(2,1)S(1)} %get-tuple-element.28), channel_id=1, source_target_pairs={{0,1},{1,0},{2,3},{3,2},{4,5},{5,4},{6,7},{7,6},{8,9},{9,8},{10,11... | collective-permute-start | bytes 884744 | tf_op jit(solution)/shard_map/ppermute | solution.py:279
  59.0 25.4 %collective-permute-start.12 = (bf16[8,4,8,576]{3,2,1,0:T(8,128)(2,1)S(1)}, bf16[8,4,8,576]{3,2,1,0:T(8,128)(2,1)S(1)}, u32[]{:S(2)}, u32[]{:S(2)}) collective-permute-start(bf16[8,4,8,576]{3,2,1,0:T(8,128)(2,1)S(1)} %get-tuple-element.30), channel_id=1, source_target_pairs={{0,1},{1,0},{2,3},{3,2},{4,5},{5,4},{6,7},{7,6},{8,9},{9,8},{10,11... | collective-permute-start | bytes 884744 | tf_op jit(solution)/shard_map/ppermute | solution.py:279
  60.2 3.0 %copy-start.1 = (bf16[27648,128]{1,0:T(8,128)(2,1)S(1)}, bf16[27648,128]{1,0:T(8,128)(2,1)}, u32[]{:S(2)}) copy-start(bf16[27648,128]{1,0:T(8,128)(2,1)} %copy-done) | copy-start | bytes 21233668
  68.2 17.7 %collective-permute-start.13 = (bf16[8,4,8,576]{3,2,1,0:T(8,128)(2,1)S(1)}, bf16[8,4,8,576]{3,2,1,0:T(8,128)(2,1)S(1)}, u32[]{:S(2)}, u32[]{:S(2)}) collective-permute-start(bf16[8,4,8,576]{3,2,1,0:T(8,128)(2,1)S(1)} %get-tuple-element.32), channel_id=1, source_target_pairs={{0,1},{1,0},{2,3},{3,2},{4,5},{5,4},{6,7},{7,6},{8,9},{9,8},{10,11... | collective-permute-start | bytes 884744 | tf_op jit(solution)/shard_map/ppermute | solution.py:279
  81.2 9.3 %collective-permute-start.14 = (bf16[8,4,8,576]{3,2,1,0:T(8,128)(2,1)S(1)}, bf16[8,4,8,576]{3,2,1,0:T(8,128)(2,1)S(1)}, u32[]{:S(2)}, u32[]{:S(2)}) collective-permute-start(bf16[8,4,8,576]{3,2,1,0:T(8,128)(2,1)S(1)} %get-tuple-element.34), channel_id=1, source_target_pairs={{0,1},{1,0},{2,3},{3,2},{4,5},{5,4},{6,7},{7,6},{8,9},{9,8},{10,11... | collective-permute-start | bytes 884744 | tf_op jit(solution)/shard_map/ppermute | solution.py:279

commit v5 on v4

--- a/solution.py
+++ b/solution.py
@@ -278,8 +278,14 @@
     def over_x(half):
         return lax.ppermute(half, "rcv", [(r, r ^ 1) for r in range(rcv_count)])
 
+    ring = [*range(0, steps, 2), *reversed(range(1, steps, 2))]
+
+    def behind(plane, k):
+        return ring[(ring.index(plane) - k) % steps]
+
     def over_z(half):
-        return lax.ppermute(half, "rcv", [(r, (r + 2) % rcv_count) for r in range(rcv_count)])
+        moves = [(behind(r // 2, 1) * 2 + r % 2, r) for r in range(rcv_count)]
+        return lax.ppermute(half, "rcv", moves)
 
     def whole_at(array, start=0):
         return (array, start), (array, start + HALF_ROWS)
@@ -340,7 +346,7 @@
         pieces += [(kept, over_x(sent)) for kept, sent in zip(outs[::2], outs[1::2])]
     result = blank((steps, 2, count, src_count, count, 576), token)
     for k, (kept, got) in enumerate(pieces):
-        at = lax.rem(z - k + steps, steps)
+        at = sum(jnp.where(z == plane, behind(plane, k), 0) for plane in range(steps))
         result = lax.dynamic_update_slice(result, kept[None, None], (at, x, 0, 0, 0, 0))
         result = lax.dynamic_update_slice(result, got[None, None], (at, 1 - x, 0, 0, 0, 0))
     return result.reshape(steps * 2 * count, src_count, count, 576)

time: 91.5 us -> 89.4 us (0.977)
  waiting for transfers between devices: 46.9 us -> 40.3 us
  starting transfers between devices: 15.1 us -> 19.7 us
    ppermute x5, waiting for transfers between devices: 30.7 us -> 21.6 us  [over_z(): return lax.ppermute(half, 'rcv', moves)]
    ppermute x5, starting transfers between devices: 6.11 us -> 11.4 us  [over_z(): return lax.ppermute(half, 'rcv', moves)]
    ppermute x6, waiting for transfers between devices: 4.37 us -> 7.25 us  [over_x(): return lax.ppermute(half, 'rcv', [(r, r ^ 1) for r in range(rcv_count)])]
    ppermute x2, waiting for transfers between devices: 0.98 us -> 0.01 us  [over_core(): return lax.ppermute(half, 'src', [(s, s ^ 1) for s in range(src_count)])]
  transfers between devices with their start and end apart: 15 -> 15, of which waited for: 10 -> 8; matrix products, arithmetic and copies ran while one was open for 6% -> 6% of each run, Pallas kernels for 18% -> 19%
where the time goes in v5:
time: 89.4 us; the launch traced here: 89.2 us
  waiting for transfers between devices  40.3 us (45%)
  starting transfers between devices  19.7 us (22%)
  Pallas kernels  18.6 us (21%)
  local copies, waits for them, and re-layouts  10.5 us (12%)
    ppermute x5, waiting for transfers between devices, over_z(): return lax.ppermute(half, 'rcv', moves)  21.6 us
    pallas_call x3, Pallas kernels, products_of(): pl.pallas_call(functools.partial(products_kernel, layout, s, src_count, n...  16.2 us
    ppermute x2, waiting for transfers between devices, over_high(): lax.ppermute(half, 'src', [(s, (s + 2) % src_count) for s in range(src_co...  11.4 us
    ppermute x5, starting transfers between devices, over_z(): return lax.ppermute(half, 'rcv', moves)  11.4 us
    ppermute x6, waiting for transfers between devices, over_x(): return lax.ppermute(half, 'rcv', [(r, r ^ 1) for r in range(rcv_count)])  7.25 us
    ppermute x6, starting transfers between devices, over_x(): return lax.ppermute(half, 'rcv', [(r, r ^ 1) for r in range(rcv_count)])  5.19 us
    unnamed x9, local copies, waits for them, and re-layouts  4.52 us
    ppermute x2, starting transfers between devices, over_high(): lax.ppermute(half, 'src', [(s, (s + 2) % src_count) for s in range(src_co...  3.04 us
  transfers between devices with their start and end apart: 15, of which 8 were waited for; matrix products, arithmetic and copies ran while one was open for 6% of the time, Pallas kernels for 19%

profile of v5, /device:TPU:0, one launch (start us, length us, event | category | flops | bytes accessed | tf_op | source)
XLA Modules:
  0.0 89.2 jit_solution(15542869563195878155)
XLA Ops:
  0.0 1.5 %copy.6.x_ref = bf16[8,287,192]{2,1,0:T(8,128)(2,1)S(1)} copy(bf16[8,287,192]{2,0,1:T(8,128)(2,1)} %param.3) | data formatting | bytes 1763328 | tf_op args[0]
  1.5 1.5 %prepare.1.refs_0_ = bf16[3456,128]{1,0:T(8,128)(2,1)S(1)} custom-call(bf16[8,287,192]{2,1,0:T(8,128)(2,1)S(1)} %copy.6.x_ref), custom_call_target="tpu_custom_call" | custom-call | tf_op jit(solution)/shard_map/prepare/pallas_call | solution.py:72
  3.0 4.1 %collective-permute-start.2 = (bf16[3456,128]{1,0:T(8,128)(2,1)S(1)}, bf16[3456,128]{1,0:T(8,128)(2,1)S(1)}, u32[]{:S(2)}, u32[]{:S(2)}) collective-permute-start(bf16[3456,128]{1,0:T(8,128)(2,1)S(1)} %prepare.1.refs_0_), channel_id=1, source_target_pairs={{2,0},{3,1},{6,2},{7,3},{0,4},{1,5},{4,6},{5,7},{10,8},{11,9},{14,... | collective-permute-start | bytes 2654216 | tf_op jit(solution)/shard_map/ppermute | solution.py:288
  7.1 1.5 %collective-permute-start = (bf16[3456,128]{1,0:T(8,128)(2,1)S(1)}, bf16[3456,128]{1,0:T(8,128)(2,1)S(1)}, u32[]{:S(2)}, u32[]{:S(2)}) collective-permute-start(bf16[3456,128]{1,0:T(8,128)(2,1)S(1)} %prepare.1.refs_0_), channel_id=1, source_target_pairs={{0,1},{1,0},{2,3},{3,2},{4,5},{5,4},{6,7},{7,6},{8,9},{9,8},{10,11... | collective-permute-start | bytes 2654216 | tf_op jit(solution)/shard_map/ppermute | solution.py:279
  8.6 1.5 %collective-permute-start.1 = (bf16[3456,128]{1,0:T(8,128)(2,1)S(1)}, bf16[3456,128]{1,0:T(8,128)(2,1)S(1)}, u32[]{:S(2)}, u32[]{:S(2)}) collective-permute-start(bf16[3456,128]{1,0:T(8,128)(2,1)S(1)} %prepare.1.refs_0_), channel_id=1, source_target_pairs={{0,16},{8,24},{16,0},{24,8},{1,17},{9,25},{17,1},{25,9},{2,18},{10... | collective-permute-start | bytes 2654216 | tf_op jit(solution)/shard_map/ppermute | solution.py:276
  10.1 15.9 %collective-permute-done.2.refs_0_ = bf16[3456,128]{1,0:T(8,128)(2,1)S(1)} collective-permute-done((bf16[3456,128]{1,0:T(8,128)(2,1)S(1)}, bf16[3456,128]{1,0:T(8,128)(2,1)S(1)}, u32[]{:S(2)}, u32[]{:S(2)}) %collective-permute-start.2) | collective-permute-done | bytes 884768 | tf_op jit(solution)/shard_map/ppermute | solution.py:288
  26.0 2.2 %collective-permute-done.refs_1_.refs_3_ = bf16[3456,128]{1,0:T(8,128)(2,1)S(1)} collective-permute-done((bf16[3456,128]{1,0:T(8,128)(2,1)S(1)}, bf16[3456,128]{1,0:T(8,128)(2,1)S(1)}, u32[]{:S(2)}, u32[]{:S(2)}) %collective-permute-start) | collective-permute-done | bytes 884768 | tf_op jit(solution)/shard_map/ppermute | solution.py:279
  28.2 1.2 %collective-permute-done.1.refs_2_ = bf16[3456,128]{1,0:T(8,128)(2,1)S(1)} collective-permute-done((bf16[3456,128]{1,0:T(8,128)(2,1)S(1)}, bf16[3456,128]{1,0:T(8,128)(2,1)S(1)}, u32[]{:S(2)}, u32[]{:S(2)}) %collective-permute-start.1) | collective-permute-done | bytes 884768 | tf_op jit(solution)/shard_map/ppermute | solution.py:276
  29.4 0.3 rearranged.5
  29.7 0.1 collective-permute-start.6
  29.7 1.6 %collective-permute-start.3 = (bf16[2160,128]{1,0:T(8,128)(2,1)S(1)}, bf16[2160,128]{1,0:T(8,128)(2,1)S(1)}, u32[]{:S(2)}, u32[]{:S(2)}) collective-permute-start(bf16[2160,128]{1,0:T(8,128)(2,1)S(1)} %get-tuple-element.20), channel_id=1, source_target_pairs={{2,0},{3,1},{6,2},{7,3},{0,4},{1,5},{4,6},{5,7},{10,8},{11,9},{14,... | collective-permute-start | bytes 1658888 | tf_op jit(solution)/shard_map/ppermute | solution.py:288
  31.4 1.5 %collective-permute-start.7 = (bf16[1728,128]{1,0:T(8,128)(2,1)S(1)}, bf16[1728,128]{1,0:T(8,128)(2,1)S(1)}, u32[]{:S(2)}, u32[]{:S(2)}) collective-permute-start(bf16[1728,128]{1,0:T(8,128)(2,1)S(1)} %get-tuple-element.23), channel_id=1, source_target_pairs={{0,16},{8,24},{16,0},{24,8},{1,17},{9,25},{17,1},{25,9},{2,18},{10... | collective-permute-start | bytes 1327112 | tf_op jit(solution)/shard_map/ppermute | solution.py:276
  32.9 0.5 collective-permute-start.8
  33.4 10.2 %collective-permute-done.7.refs_0_.refs_4_ = bf16[1728,128]{1,0:T(8,128)(2,1)S(1)} collective-permute-done((bf16[1728,128]{1,0:T(8,128)(2,1)S(1)}, bf16[1728,128]{1,0:T(8,128)(2,1)S(1)}, u32[]{:S(2)}, u32[]{:S(2)}) %collective-permute-start.7) | collective-permute-done | bytes 442400 | tf_op jit(solution)/shard_map/ppermute | solution.py:276
  43.6 1.2 %collective-permute-done.8.refs_1_.refs_5_ = bf16[1728,128]{1,0:T(8,128)(2,1)S(1)} collective-permute-done((bf16[1728,128]{1,0:T(8,128)(2,1)S(1)}, bf16[1728,128]{1,0:T(8,128)(2,1)S(1)}, u32[]{:S(2)}, u32[]{:S(2)}) %collective-permute-start.8) | collective-permute-done | bytes 442400 | tf_op jit(solution)/shard_map/ppermute | solution.py:279
  44.9 0.0 collective-permute-done.3.refs_2_.refs_0_
  44.9 0.1 rearranged.6
  44.9 0.1 collective-permute-start.9
  45.0 0.0 copy-start.2
  45.0 0.0 copy-start.3
  45.0 2.4 %collective-permute-start.5 = (bf16[1296,128]{1,0:T(8,128)(2,1)S(1)}, bf16[1296,128]{1,0:T(8,128)(2,1)S(1)}, u32[]{:S(2)}, u32[]{:S(2)}) collective-permute-start(bf16[1296,128]{1,0:T(8,128)(2,1)S(1)} %get-tuple-element.21), channel_id=1, source_target_pairs={{2,0},{3,1},{6,2},{7,3},{0,4},{1,5},{4,6},{5,7},{10,8},{11,9},{14,... | collective-permute-start | bytes 995336 | tf_op jit(solution)/shard_map/ppermute | solution.py:288
  47.4 0.1 collective-permute-start.4
  47.5 0.0 collective-permute-done.9.refs_6_
  47.5 0.0 collective-permute-done.6.refs_1_
  47.5 0.5 rearranged.7.refs_2_.refs_1_
  47.9 0.0 copy-done.2
  47.9 0.0 copy-done.3
  48.0 0.0 copy-start
  48.0 6.6 %products.3 = (bf16[8,4,8,576]{3,2,1,0:T(8,128)(2,1)S(1)}, bf16[8,4,8,576]{3,2,1,0:T(8,128)(2,1)S(1)}, bf16[8,4,8,576]{3,2,1,0:T(8,128)(2,1)S(1)}, bf16[8,4,8,576]{3,2,1,0:T(8,128)(2,1)S(1)}, f32[8,128]{1,0:T(8,128)S(1)}) custom-call(s32[4,4]{1,0:T(4,128)S(1)} %copy-done.3, bf16[64,128]{1,0:T(8,128)(2,1)S(1)} %copy-done.2, ...), custom_call_target="tpu_custom_call" | custom-call | flops 1811939328 | bytes 8388608 | tf_op jit(solution)/shard_map/jit(products_of)/products/pallas_call | solution.py:191
  54.6 0.0 copy-done
  54.6 1.1 %collective-permute-done.5.refs_0_ = bf16[1296,128]{1,0:T(8,128)(2,1)S(1)} collective-permute-done((bf16[1296,128]{1,0:T(8,128)(2,1)S(1)}, bf16[1296,128]{1,0:T(8,128)(2,1)S(1)}, u32[]{:S(2)}, u32[]{:S(2)}) %collective-permute-start.5) | collective-permute-done | bytes 331808 | tf_op jit(solution)/shard_map/ppermute | solution.py:288
  55.7 3.2 %collective-permute-start.10 = (bf16[1296,128]{1,0:T(8,128)(2,1)S(1)}, bf16[1296,128]{1,0:T(8,128)(2,1)S(1)}, u32[]{:S(2)}, u32[]{:S(2)}) collective-permute-start(bf16[1296,128]{1,0:T(8,128)(2,1)S(1)} %paced.3.refs_1_), channel_id=1, source_target_pairs={{2,0},{3,1},{6,2},{7,3},{0,4},{1,5},{4,6},{5,7},{10,8},{11,9},{14,... | collective-permute-start | bytes 995336 | tf_op jit(solution)/shard_map/ppermute | solution.py:288
  58.9 0.5 collective-permute-start.11
  59.4 1.5 %collective-permute-start.12 = (bf16[8,4,8,576]{3,2,1,0:T(8,128)(2,1)S(1)}, bf16[8,4,8,576]{3,2,1,0:T(8,128)(2,1)S(1)}, u32[]{:S(2)}, u32[]{:S(2)}) collective-permute-start(bf16[8,4,8,576]{3,2,1,0:T(8,128)(2,1)S(1)} %get-tuple-element.30), channel_id=1, source_target_pairs={{0,1},{1,0},{2,3},{3,2},{4,5},{5,4},{6,7},{7,6},{8,9},{9,8},{10,11... | collective-permute-start | bytes 884744 | tf_op jit(solution)/shard_map/ppermute | solution.py:279
  60.9 0.1 rearranged.9.refs_0_
  61.0 0.0 copy-start.1
  61.0 3.0 %copy-done.1 = bf16[27648,128]{1,0:T(8,128)(2,1)S(1)} copy-done((bf16[27648,128]{1,0:T(8,128)(2,1)S(1)}, bf16[27648,128]{1,0:T(8,128)(2,1)}, u32[]{:S(2)}) %copy-start.1) | copy-done | bytes 7077912
  64.0 5.0 %products.5 = (bf16[8,4,8,576]{3,2,1,0:T(8,128)(2,1)S(1)}, bf16[8,4,8,576]{3,2,1,0:T(8,128)(2,1)S(1)}, f32[8,128]{1,0:T(8,128)}) custom-call(s32[4,4]{1,0:T(4,128)S(1)} %copy-done.3, bf16[64,128]{1,0:T(8,128)(2,1)S(1)} %copy-done.2, bf16[3456,128]{1,0:T(8,128)(2,1)S(1)} %rearranged.9.refs_0_, bf16[27648,128]{1,0:T(8,128)(2,1)S(1)} %copy-done.1), custom_call_target="tpu_custom_call" | custom-call | flops 905969664 | bytes 8388608 | tf_op jit(solution)/shard_map/jit(products_of)/products/pallas_call | solution.py:191
  69.0 0.5 collective-permute-start.13
  69.6 0.0 collective-permute-done.4.refs_0_
  69.6 4.6 %collective-permute-done.10.refs_1_ = bf16[1296,128]{1,0:T(8,128)(2,1)S(1)} collective-permute-done((bf16[1296,128]{1,0:T(8,128)(2,1)S(1)}, bf16[1296,128]{1,0:T(8,128)(2,1)S(1)}, u32[]{:S(2)}, u32[]{:S(2)}) %collective-permute-start.10) | collective-permute-done | bytes 331808 | tf_op jit(solution)/shard_map/ppermute | solution.py:288
  74.2 0.1 rearranged.8.refs_0_
  74.2 4.5 %products.4 = (bf16[8,4,8,576]{3,2,1,0:T(8,128)(2,1)S(1)}, bf16[8,4,8,576]{3,2,1,0:T(8,128)(2,1)S(1)}, f32[8,128]{1,0:T(8,128)S(1)}) custom-call(s32[4,4]{1,0:T(4,128)S(1)} %copy-done.3, bf16[64,128]{1,0:T(8,128)(2,1)S(1)} %copy-done.2, bf16[3456,128]{1,0:T(8,128)(2,1)S(1)} %rearranged.8.refs_0_, bf16[27648,128]{1,0:T(8,128)(2,1)S(1)} %copy-done.1), custom_call_target="tpu_custom_call" | custom-call | flops 905969664 | bytes 8388608 | tf_op jit(solution)/shard_map/jit(products_of)/products/pallas_call | solution.py:191
  78.8 0.6 collective-permute-start.14
  79.4 0.8 bitcast_dynamic-update-slice_fusion.7
  80.1 0.0 collective-permute-done.11
  80.1 0.8 bitcast_dynamic-update-slice_fusion.6
  80.9 0.8 bitcast_dynamic-update-slice_fusion.5
  81.7 0.0 collective-permute-done.12
  81.7 0.8 bitcast_dynamic-update-slice_fusion.4
  82.4 0.8 bitcast_dynamic-update-slice_fusion.3
  83.2 0.0 collective-permute-done.13
  83.2 0.8 bitcast_dynamic-update-slice_fusion.2
  83.9 0.8 bitcast_dynamic-update-slice_fusion.1
  84.7 3.8 %collective-permute-done.14 = bf16[8,4,8,576]{3,2,1,0:T(8,128)(2,1)S(1)} collective-permute-done((bf16[8,4,8,576]{3,2,1,0:T(8,128)(2,1)S(1)}, bf16[8,4,8,576]{3,2,1,0:T(8,128)(2,1)S(1)}, u32[]{:S(2)}, u32[]{:S(2)}) %collective-permute-start.14) | collective-permute-done | bytes 294944 | tf_op jit(solution)/shard_map/ppermute | solution.py:279
  88.5 0.8 bitcast_dynamic-update-slice_fusion
  (3 shorter events, 0.0 us)
Async XLA Ops:
  3.0 23.0 %collective-permute-start.2 = (bf16[3456,128]{1,0:T(8,128)(2,1)S(1)}, bf16[3456,128]{1,0:T(8,128)(2,1)S(1)}, u32[]{:S(2)}, u32[]{:S(2)}) collective-permute-start(bf16[3456,128]{1,0:T(8,128)(2,1)S(1)} %prepare.1.refs_0_), channel_id=1, source_target_pairs={{2,0},{3,1},{6,2},{7,3},{0,4},{1,5},{4,6},{5,7},{10,8},{11,9},{14,... | collective-permute-start | bytes 2654216 | tf_op jit(solution)/shard_map/ppermute | solution.py:288
  7.1 21.1 %collective-permute-start = (bf16[3456,128]{1,0:T(8,128)(2,1)S(1)}, bf16[3456,128]{1,0:T(8,128)(2,1)S(1)}, u32[]{:S(2)}, u32[]{:S(2)}) collective-permute-start(bf16[3456,128]{1,0:T(8,128)(2,1)S(1)} %prepare.1.refs_0_), channel_id=1, source_target_pairs={{0,1},{1,0},{2,3},{3,2},{4,5},{5,4},{6,7},{7,6},{8,9},{9,8},{10,11... | collective-permute-start | bytes 2654216 | tf_op jit(solution)/shard_map/ppermute | solution.py:279
  8.6 20.8 %collective-permute-start.1 = (bf16[3456,128]{1,0:T(8,128)(2,1)S(1)}, bf16[3456,128]{1,0:T(8,128)(2,1)S(1)}, u32[]{:S(2)}, u32[]{:S(2)}) collective-permute-start(bf16[3456,128]{1,0:T(8,128)(2,1)S(1)} %prepare.1.refs_0_), channel_id=1, source_target_pairs={{0,16},{8,24},{16,0},{24,8},{1,17},{9,25},{17,1},{25,9},{2,18},{10... | collective-permute-start | bytes 2654216 | tf_op jit(solution)/shard_map/ppermute | solution.py:276
  29.7 17.8 %collective-permute-start.6 = (bf16[10368,128]{1,0:T(8,128)(2,1)S(1)}, bf16[10368,128]{1,0:T(8,128)(2,1)S(1)}, u32[]{:S(2)}, u32[]{:S(2)}) collective-permute-start(bf16[10368,128]{1,0:T(8,128)(2,1)S(1)} %get-tuple-element.22), channel_id=1, source_target_pairs={{0,8},{8,0},{16,24},{24,16},{1,9},{9,1},{17,25},{25,17},{2,10},{10... | collective-permute-start | bytes 7962632 | tf_op jit(solution)/shard_map/ppermute | solution.py:273
  29.7 15.1 %collective-permute-start.3 = (bf16[2160,128]{1,0:T(8,128)(2,1)S(1)}, bf16[2160,128]{1,0:T(8,128)(2,1)S(1)}, u32[]{:S(2)}, u32[]{:S(2)}) collective-permute-start(bf16[2160,128]{1,0:T(8,128)(2,1)S(1)} %get-tuple-element.20), channel_id=1, source_target_pairs={{2,0},{3,1},{6,2},{7,3},{0,4},{1,5},{4,6},{5,7},{10,8},{11,9},{14,... | collective-permute-start | bytes 1658888 | tf_op jit(solution)/shard_map/ppermute | solution.py:288
  31.4 12.2 %collective-permute-start.7 = (bf16[1728,128]{1,0:T(8,128)(2,1)S(1)}, bf16[1728,128]{1,0:T(8,128)(2,1)S(1)}, u32[]{:S(2)}, u32[]{:S(2)}) collective-permute-start(bf16[1728,128]{1,0:T(8,128)(2,1)S(1)} %get-tuple-element.23), channel_id=1, source_target_pairs={{0,16},{8,24},{16,0},{24,8},{1,17},{9,25},{17,1},{25,9},{2,18},{10... | collective-permute-start | bytes 1327112 | tf_op jit(solution)/shard_map/ppermute | solution.py:276
  32.9 12.0 %collective-permute-start.8 = (bf16[1728,128]{1,0:T(8,128)(2,1)S(1)}, bf16[1728,128]{1,0:T(8,128)(2,1)S(1)}, u32[]{:S(2)}, u32[]{:S(2)}) collective-permute-start(bf16[1728,128]{1,0:T(8,128)(2,1)S(1)} %get-tuple-element.24), channel_id=1, source_target_pairs={{0,1},{1,0},{2,3},{3,2},{4,5},{5,4},{6,7},{7,6},{8,9},{9,8},{10,11... | collective-permute-start | bytes 1327112 | tf_op jit(solution)/shard_map/ppermute | solution.py:279
  44.9 2.5 %collective-permute-start.9 = (bf16[3456,128]{1,0:T(8,128)(2,1)S(1)}, bf16[3456,128]{1,0:T(8,128)(2,1)S(1)}, u32[]{:S(2)}, u32[]{:S(2)}) collective-permute-start(bf16[3456,128]{1,0:T(8,128)(2,1)S(1)} %rearranged.6), channel_id=1, source_target_pairs={{0,8},{8,0},{16,24},{24,16},{1,9},{9,1},{17,25},{25,17},{2,10},{10... | collective-permute-start | bytes 2654216 | tf_op jit(solution)/shard_map/ppermute | solution.py:273
  45.0 2.9 %copy-start.2 = (bf16[64,128]{1,0:T(8,128)(2,1)S(1)}, bf16[64,128]{1,0:T(8,128)(2,1)}, u32[]{:S(2)}) copy-start(bf16[64,128]{1,0:T(8,128)(2,1)} %constant.37.clone.turn_ref) | copy-start | bytes 49156
  45.0 2.9 %copy-start.3 = (s32[4,4]{1,0:T(4,128)S(1)}, s32[4,4]{1,0:T(4,128)}, u32[]{:S(2)}) copy-start(s32[4,4]{1,0:T(4,128)} %mask_ref.5) | copy-start | bytes 196
  45.0 10.7 %collective-permute-start.5 = (bf16[1296,128]{1,0:T(8,128)(2,1)S(1)}, bf16[1296,128]{1,0:T(8,128)(2,1)S(1)}, u32[]{:S(2)}, u32[]{:S(2)}) collective-permute-start(bf16[1296,128]{1,0:T(8,128)(2,1)S(1)} %get-tuple-element.21), channel_id=1, source_target_pairs={{2,0},{3,1},{6,2},{7,3},{0,4},{1,5},{4,6},{5,7},{10,8},{11,9},{14,... | collective-permute-start | bytes 995336 | tf_op jit(solution)/shard_map/ppermute | solution.py:288
  47.4 22.2 %collective-permute-start.4 = (bf16[2160,128]{1,0:T(8,128)(2,1)S(1)}, bf16[2160,128]{1,0:T(8,128)(2,1)S(1)}, u32[]{:S(2)}, u32[]{:S(2)}) collective-permute-start(bf16[2160,128]{1,0:T(8,128)(2,1)S(1)} %collective-permute-done.3.refs_2_.refs_0_), channel_id=1, source_target_pairs={{2,0},{3,1},{6,2},{7,3},{0,4},{1,5},{4,6},{5,7},{10,8},{11,9},{14,... | collective-permute-start | bytes 1658888 | tf_op jit(solution)/shard_map/ppermute | solution.py:288
  48.0 6.6 %copy-start = (bf16[27648,128]{1,0:T(8,128)(2,1)}, bf16[27648,128]{1,0:T(8,128)(2,1)S(1)}, u32[]{:S(2)}) copy-start(bf16[27648,128]{1,0:T(8,128)(2,1)S(1)} %rearranged.7.refs_2_.refs_1_) | copy-start | bytes 21233668
  55.7 18.5 %collective-permute-start.10 = (bf16[1296,128]{1,0:T(8,128)(2,1)S(1)}, bf16[1296,128]{1,0:T(8,128)(2,1)S(1)}, u32[]{:S(2)}, u32[]{:S(2)}) collective-permute-start(bf16[1296,128]{1,0:T(8,128)(2,1)S(1)} %paced.3.refs_1_), channel_id=1, source_target_pairs={{2,0},{3,1},{6,2},{7,3},{0,4},{1,5},{4,6},{5,7},{10,8},{11,9},{14,... | collective-permute-start | bytes 995336 | tf_op jit(solution)/shard_map/ppermute | solution.py:288
  58.9 21.3 %collective-permute-start.11 = (bf16[8,4,8,576]{3,2,1,0:T(8,128)(2,1)S(1)}, bf16[8,4,8,576]{3,2,1,0:T(8,128)(2,1)S(1)}, u32[]{:S(2)}, u32[]{:S(2)}) collective-permute-start(bf16[8,4,8,576]{3,2,1,0:T(8,128)(2,1)S(1)} %get-tuple-element.28), channel_id=1, source_target_pairs={{0,1},{1,0},{2,3},{3,2},{4,5},{5,4},{6,7},{7,6},{8,9},{9,8},{10,11... | collective-permute-start | bytes 884744 | tf_op jit(solution)/shard_map/ppermute | solution.py:279
  59.4 22.2 %collective-permute-start.12 = (bf16[8,4,8,576]{3,2,1,0:T(8,128)(2,1)S(1)}, bf16[8,4,8,576]{3,2,1,0:T(8,128)(2,1)S(1)}, u32[]{:S(2)}, u32[]{:S(2)}) collective-permute-start(bf16[8,4,8,576]{3,2,1,0:T(8,128)(2,1)S(1)} %get-tuple-element.30), channel_id=1, source_target_pairs={{0,1},{1,0},{2,3},{3,2},{4,5},{5,4},{6,7},{7,6},{8,9},{9,8},{10,11... | collective-permute-start | bytes 884744 | tf_op jit(solution)/shard_map/ppermute | solution.py:279
  61.0 3.0 %copy-start.1 = (bf16[27648,128]{1,0:T(8,128)(2,1)S(1)}, bf16[27648,128]{1,0:T(8,128)(2,1)}, u32[]{:S(2)}) copy-start(bf16[27648,128]{1,0:T(8,128)(2,1)} %copy-done) | copy-start | bytes 21233668
  69.0 14.1 %collective-permute-start.13 = (bf16[8,4,8,576]{3,2,1,0:T(8,128)(2,1)S(1)}, bf16[8,4,8,576]{3,2,1,0:T(8,128)(2,1)S(1)}, u32[]{:S(2)}, u32[]{:S(2)}) collective-permute-start(bf16[8,4,8,576]{3,2,1,0:T(8,128)(2,1)S(1)} %get-tuple-element.32), channel_id=1, source_target_pairs={{0,1},{1,0},{2,3},{3,2},{4,5},{5,4},{6,7},{7,6},{8,9},{9,8},{10,11... | collective-permute-start | bytes 884744 | tf_op jit(solution)/shard_map/ppermute | solution.py:279
  78.8 9.7 %collective-permute-start.14 = (bf16[8,4,8,576]{3,2,1,0:T(8,128)(2,1)S(1)}, bf16[8,4,8,576]{3,2,1,0:T(8,128)(2,1)S(1)}, u32[]{:S(2)}, u32[]{:S(2)}) collective-permute-start(bf16[8,4,8,576]{3,2,1,0:T(8,128)(2,1)S(1)} %get-tuple-element.34), channel_id=1, source_target_pairs={{0,1},{1,0},{2,3},{3,2},{4,5},{5,4},{6,7},{7,6},{8,9},{9,8},{10,11... | collective-permute-start | bytes 884744 | tf_op jit(solution)/shard_map/ppermute | solution.py:279

commit v6 on v5

--- a/solution.py
+++ b/solution.py
@@ -16,7 +16,7 @@
 BLOCK_ROWS = GROUPS * GROUP_ROWS
 HALF_ROWS = BLOCK_ROWS // 2
 STATIONS = 8
-CUTS = (0, 5, 8)
+CUTS = (0, 1, 5, 8)
 PACE = 80 * 2**20
 F32 = jnp.float32
 BF16 = jnp.bfloat16
@@ -295,15 +295,17 @@
     sources = [whole_at(own), whole_at(passing)]
     beside, high = over_x(own), over_high(own)
     cuts, ahead = [n * GROUP_ROWS for n in CUTS], []
-    listed = [[(3, start, end - start)] for start, end in zip(cuts, cuts[1:])]
+    if steps > 2:
+        listed = [[(0, start, end - start)] for start, end in zip(cuts, cuts[1:])]
+        ahead = [over_z(piece) for piece in rearranged([passing], listed)]
     mine, theirs = [whole_at(own)], [whole_at(beside)]
     if highs > 1:
         three = [(n, 0, BLOCK_ROWS) for n in range(3)]
-        joined, first, second, *next_ = rearranged(
-            [own, beside, high, passing],
-            [three, [(1, 0, HALF_ROWS)], [(2, HALF_ROWS, HALF_ROWS)]] + (listed if steps > 2 else []),
+        joined, first, second = rearranged(
+            [own, beside, high],
+            [three, [(1, 0, HALF_ROWS)], [(2, HALF_ROWS, HALF_ROWS)]],
+            (passing, *ahead[:1]),
         )
-        ahead = [over_z(piece) for piece in next_]
         joined = over_core(joined)
         mine += [whole_at(joined), whole_at(high), whole_at(joined, 2 * BLOCK_ROWS)]
         theirs += [whole_at(joined, BLOCK_ROWS)]
@@ -317,7 +319,7 @@
             mine += [whole_at(high), whole_at(over_core(high))]
         first, across = over_high(first), over_x(second)
         (pair,) = rearranged(
-            [first, across], [[(0, 0, HALF_ROWS), (1, 0, HALF_ROWS)]], ahead[:1] if k == 1 else ()
+            [first, across], [[(0, 0, HALF_ROWS), (1, 0, HALF_ROWS)]], ahead[1:2] if k == 1 else ()
         )
         theirs += [((first, 0), (across, 0)), whole_at(over_core(pair))]
     blocks = mine + theirs
@@ -328,7 +330,7 @@
                 if not any(array is known for known in arrays):
                     arrays.append(array)
                 listed.append(([array is known for known in arrays].index(True), at, HALF_ROWS))
-        (together,) = rearranged(arrays, [listed], ahead[1:-1])
+        (together,) = rearranged(arrays, [listed])
         blocks = [whole_at(together, n * BLOCK_ROWS) for n in range(len(blocks))]
     held = list({id(array): array for block in blocks for array, _ in block}.values())
     turn = turn_matrix()
@@ -337,7 +339,11 @@
     for k in range(1, steps):
         batch = sources
         if k + 1 < steps:
-            early, late = ahead if k == 1 else (over_z(early), over_z(late))
+            if k == 1:
+                rows = [(n, 0, piece.shape[0]) for n, piece in enumerate(ahead[:2])]
+                (early,), late = rearranged(ahead[:2], [rows]), ahead[2]
+            else:
+                early, late = over_z(early), over_z(late)
         *outs, token = products(block_mask, turn, batch, blocks, count, 1.0 / math.sqrt(segs))
         if k + 2 < steps:
             late = paced(late, (token,), PACE)

time: 89.4 us -> 93.1 us (1.041)
  starting transfers between devices: 19.7 us -> 25.4 us
  waiting for transfers between devices: 40.3 us -> 38.3 us
    ppermute x5 -> x6, waiting for transfers between devices: 21.6 us -> 32 us  [over_z(): return lax.ppermute(half, 'rcv', moves)]
    ppermute x2, waiting for transfers between devices: 11.4 us -> 2.2 us  [over_high(): lax.ppermute(half, 'src', [(s, (s + 2) % src_count) for s in range(src_co...]
    ppermute x6, waiting for transfers between devices: 7.25 us -> 3.75 us  [over_x(): return lax.ppermute(half, 'rcv', [(r, r ^ 1) for r in range(rcv_count)])]
    ppermute x6, starting transfers between devices: 5.19 us -> 8.13 us  [over_x(): return lax.ppermute(half, 'rcv', [(r, r ^ 1) for r in range(rcv_count)])]
    ppermute x5 -> x6, starting transfers between devices: 11.4 us -> 14.1 us  [over_z(): return lax.ppermute(half, 'rcv', moves)]
  transfers between devices with their start and end apart: 15 -> 16, of which waited for: 8 -> 9; matrix products, arithmetic and copies ran while one was open for 6% -> 6% of each run, Pallas kernels for 19% -> 18%
where the time goes in v6:
time: 93.1 us; the launch traced here: 93 us
  waiting for transfers between devices  38.3 us (41%)
  starting transfers between devices  25.4 us (27%)
  Pallas kernels  18.6 us (20%)
  local copies, waits for them, and re-layouts  10.5 us (11%)
    ppermute x6, waiting for transfers between devices, over_z(): return lax.ppermute(half, 'rcv', moves)  32 us
    pallas_call x3, Pallas kernels, products_of(): pl.pallas_call(functools.partial(products_kernel, layout, s, src_count, n...  16.2 us
    ppermute x6, starting transfers between devices, over_z(): return lax.ppermute(half, 'rcv', moves)  14.1 us
    ppermute x6, starting transfers between devices, over_x(): return lax.ppermute(half, 'rcv', [(r, r ^ 1) for r in range(rcv_count)])  8.13 us
    unnamed x9, local copies, waits for them, and re-layouts  4.53 us
    ppermute x6, waiting for transfers between devices, over_x(): return lax.ppermute(half, 'rcv', [(r, r ^ 1) for r in range(rcv_count)])  3.75 us
    ppermute x2, starting transfers between devices, over_high(): lax.ppermute(half, 'src', [(s, (s + 2) % src_count) for s in range(src_co...  3.04 us
    dynamic_update_slice x4, local copies, waits for them, and re-layouts, on_device(): lax.dynamic_update_slice(result, got[None, None], (at, 1 - x, 0, 0, 0, 0))  3.01 us
  transfers between devices with their start and end apart: 16, of which 9 were waited for; matrix products, arithmetic and copies ran while one was open for 6% of the time, Pallas kernels for 18%

profile of v6, /device:TPU:0, one launch (start us, length us, event | category | flops | bytes accessed | tf_op | source)
XLA Modules:
  0.0 93.0 jit_solution(14000626487592532531)
XLA Ops:
  0.0 1.5 %copy.6.x_ref = bf16[8,287,192]{2,1,0:T(8,128)(2,1)S(1)} copy(bf16[8,287,192]{2,0,1:T(8,128)(2,1)} %param.3) | data formatting | bytes 1763328 | tf_op args[0]
  1.5 1.5 %prepare.1.refs_0_ = bf16[3456,128]{1,0:T(8,128)(2,1)S(1)} custom-call(bf16[8,287,192]{2,1,0:T(8,128)(2,1)S(1)} %copy.6.x_ref), custom_call_target="tpu_custom_call" | custom-call | tf_op jit(solution)/shard_map/prepare/pallas_call | solution.py:72
  3.0 4.1 %collective-permute-start = (bf16[3456,128]{1,0:T(8,128)(2,1)S(1)}, bf16[3456,128]{1,0:T(8,128)(2,1)S(1)}, u32[]{:S(2)}, u32[]{:S(2)}) collective-permute-start(bf16[3456,128]{1,0:T(8,128)(2,1)S(1)} %prepare.1.refs_0_), channel_id=1, source_target_pairs={{2,0},{3,1},{6,2},{7,3},{0,4},{1,5},{4,6},{5,7},{10,8},{11,9},{14,... | collective-permute-start | bytes 2654216 | tf_op jit(solution)/shard_map/ppermute | solution.py:288
  7.1 1.5 %collective-permute-start.5 = (bf16[3456,128]{1,0:T(8,128)(2,1)S(1)}, bf16[3456,128]{1,0:T(8,128)(2,1)S(1)}, u32[]{:S(2)}, u32[]{:S(2)}) collective-permute-start(bf16[3456,128]{1,0:T(8,128)(2,1)S(1)} %prepare.1.refs_0_), channel_id=1, source_target_pairs={{0,1},{1,0},{2,3},{3,2},{4,5},{5,4},{6,7},{7,6},{8,9},{9,8},{10,11... | collective-permute-start | bytes 2654216 | tf_op jit(solution)/shard_map/ppermute | solution.py:279
  8.6 1.5 %collective-permute-start.6 = (bf16[3456,128]{1,0:T(8,128)(2,1)S(1)}, bf16[3456,128]{1,0:T(8,128)(2,1)S(1)}, u32[]{:S(2)}, u32[]{:S(2)}) collective-permute-start(bf16[3456,128]{1,0:T(8,128)(2,1)S(1)} %prepare.1.refs_0_), channel_id=1, source_target_pairs={{0,16},{8,24},{16,0},{24,8},{1,17},{9,25},{17,1},{25,9},{2,18},{10... | collective-permute-start | bytes 2654216 | tf_op jit(solution)/shard_map/ppermute | solution.py:276
  10.1 15.9 %collective-permute-done.refs_0_ = bf16[3456,128]{1,0:T(8,128)(2,1)S(1)} collective-permute-done((bf16[3456,128]{1,0:T(8,128)(2,1)S(1)}, bf16[3456,128]{1,0:T(8,128)(2,1)S(1)}, u32[]{:S(2)}, u32[]{:S(2)}) %collective-permute-start) | collective-permute-done | bytes 884768 | tf_op jit(solution)/shard_map/ppermute | solution.py:288
  26.0 0.1 rearranged.7
  26.0 3.4 %collective-permute-start.1 = (bf16[432,128]{1,0:T(8,128)(2,1)S(1)}, bf16[432,128]{1,0:T(8,128)(2,1)S(1)}, u32[]{:S(2)}, u32[]{:S(2)}) collective-permute-start(bf16[432,128]{1,0:T(8,128)(2,1)S(1)} %get-tuple-element.21), channel_id=1, source_target_pairs={{2,0},{3,1},{6,2},{7,3},{0,4},{1,5},{4,6},{5,7},{10,8},{11,9},{14,... | collective-permute-start | bytes 331784 | tf_op jit(solution)/shard_map/ppermute | solution.py:288
  29.5 0.0 collective-permute-done.5.refs_1_.refs_3_
  29.5 0.0 collective-permute-done.6.refs_2_
  29.5 2.3 %collective-permute-done.1.refs_0_.refs_4_ = bf16[432,128]{1,0:T(8,128)(2,1)S(1)} collective-permute-done((bf16[432,128]{1,0:T(8,128)(2,1)S(1)}, bf16[432,128]{1,0:T(8,128)(2,1)S(1)}, u32[]{:S(2)}, u32[]{:S(2)}) %collective-permute-start.1) | collective-permute-done | bytes 110624 | tf_op jit(solution)/shard_map/ppermute | solution.py:288
  31.8 0.2 rearranged.9
  32.0 0.1 collective-permute-start.7
  32.1 3.4 %collective-permute-start.2 = (bf16[1728,128]{1,0:T(8,128)(2,1)S(1)}, bf16[1728,128]{1,0:T(8,128)(2,1)S(1)}, u32[]{:S(2)}, u32[]{:S(2)}) collective-permute-start(bf16[1728,128]{1,0:T(8,128)(2,1)S(1)} %get-tuple-element.22), channel_id=1, source_target_pairs={{2,0},{3,1},{6,2},{7,3},{0,4},{1,5},{4,6},{5,7},{10,8},{11,9},{14,... | collective-permute-start | bytes 1327112 | tf_op jit(solution)/shard_map/ppermute | solution.py:288
  35.5 1.5 %collective-permute-start.8 = (bf16[1728,128]{1,0:T(8,128)(2,1)S(1)}, bf16[1728,128]{1,0:T(8,128)(2,1)S(1)}, u32[]{:S(2)}, u32[]{:S(2)}) collective-permute-start(bf16[1728,128]{1,0:T(8,128)(2,1)S(1)} %get-tuple-element.25), channel_id=1, source_target_pairs={{0,16},{8,24},{16,0},{24,8},{1,17},{9,25},{17,1},{25,9},{2,18},{10... | collective-permute-start | bytes 1327112 | tf_op jit(solution)/shard_map/ppermute | solution.py:276
  37.0 1.5 %collective-permute-start.9 = (bf16[1728,128]{1,0:T(8,128)(2,1)S(1)}, bf16[1728,128]{1,0:T(8,128)(2,1)S(1)}, u32[]{:S(2)}, u32[]{:S(2)}) collective-permute-start(bf16[1728,128]{1,0:T(8,128)(2,1)S(1)} %get-tuple-element.26), channel_id=1, source_target_pairs={{0,1},{1,0},{2,3},{3,2},{4,5},{5,4},{6,7},{7,6},{8,9},{9,8},{10,11... | collective-permute-start | bytes 1327112 | tf_op jit(solution)/shard_map/ppermute | solution.py:279
  38.5 7.0 %collective-permute-done.2.refs_1_.refs_2_ = bf16[1728,128]{1,0:T(8,128)(2,1)S(1)} collective-permute-done((bf16[1728,128]{1,0:T(8,128)(2,1)S(1)}, bf16[1728,128]{1,0:T(8,128)(2,1)S(1)}, u32[]{:S(2)}, u32[]{:S(2)}) %collective-permute-start.2) | collective-permute-done | bytes 442400 | tf_op jit(solution)/shard_map/ppermute | solution.py:288
  45.5 2.2 %collective-permute-done.8.refs_0_.refs_4_ = bf16[1728,128]{1,0:T(8,128)(2,1)S(1)} collective-permute-done((bf16[1728,128]{1,0:T(8,128)(2,1)S(1)}, bf16[1728,128]{1,0:T(8,128)(2,1)S(1)}, u32[]{:S(2)}, u32[]{:S(2)}) %collective-permute-start.8) | collective-permute-done | bytes 442400 | tf_op jit(solution)/shard_map/ppermute | solution.py:276
  47.7 1.2 %collective-permute-done.9.refs_1_.refs_5_ = bf16[1728,128]{1,0:T(8,128)(2,1)S(1)} collective-permute-done((bf16[1728,128]{1,0:T(8,128)(2,1)S(1)}, bf16[1728,128]{1,0:T(8,128)(2,1)S(1)}, u32[]{:S(2)}, u32[]{:S(2)}) %collective-permute-start.9) | collective-permute-done | bytes 442400 | tf_op jit(solution)/shard_map/ppermute | solution.py:279
  49.0 0.1 rearranged.10
  49.0 0.1 collective-permute-start.10
  49.1 0.3 collective-permute-start.4
  49.5 0.0 copy-start.2
  49.5 0.0 copy-start.3
  49.5 1.7 %collective-permute-start.3 = (bf16[2160,128]{1,0:T(8,128)(2,1)S(1)}, bf16[2160,128]{1,0:T(8,128)(2,1)S(1)}, u32[]{:S(2)}, u32[]{:S(2)}) collective-permute-start(bf16[2160,128]{1,0:T(8,128)(2,1)S(1)} %rearranged.8.refs_0_), channel_id=1, source_target_pairs={{2,0},{3,1},{6,2},{7,3},{0,4},{1,5},{4,6},{5,7},{10,8},{11,9},{14,... | collective-permute-start | bytes 1658888 | tf_op jit(solution)/shard_map/ppermute | solution.py:288
  51.2 0.3 collective-permute-done.10.refs_6_
  51.5 0.0 collective-permute-done.7.refs_1_
  51.5 0.5 rearranged.11.refs_2_.refs_1_
  52.0 0.0 copy-done.2
  52.0 0.0 copy-done.3
  52.0 0.0 copy-start
  52.0 6.6 %products.3 = (bf16[8,4,8,576]{3,2,1,0:T(8,128)(2,1)S(1)}, bf16[8,4,8,576]{3,2,1,0:T(8,128)(2,1)S(1)}, bf16[8,4,8,576]{3,2,1,0:T(8,128)(2,1)S(1)}, bf16[8,4,8,576]{3,2,1,0:T(8,128)(2,1)S(1)}, f32[8,128]{1,0:T(8,128)S(1)}) custom-call(s32[4,4]{1,0:T(4,128)S(1)} %copy-done.3, bf16[64,128]{1,0:T(8,128)(2,1)S(1)} %copy-done.2, ...), custom_call_target="tpu_custom_call" | custom-call | flops 1811939328 | bytes 8388608 | tf_op jit(solution)/shard_map/jit(products_of)/products/pallas_call | solution.py:191
  58.6 0.0 copy-done
  58.6 1.1 %collective-permute-done.4.refs_0_ = bf16[1296,128]{1,0:T(8,128)(2,1)S(1)} collective-permute-done((bf16[1296,128]{1,0:T(8,128)(2,1)S(1)}, bf16[1296,128]{1,0:T(8,128)(2,1)S(1)}, u32[]{:S(2)}, u32[]{:S(2)}) %collective-permute-start.4) | collective-permute-done | bytes 331808 | tf_op jit(solution)/shard_map/ppermute | solution.py:288
  59.7 1.2 %collective-permute-start.11 = (bf16[1296,128]{1,0:T(8,128)(2,1)S(1)}, bf16[1296,128]{1,0:T(8,128)(2,1)S(1)}, u32[]{:S(2)}, u32[]{:S(2)}) collective-permute-start(bf16[1296,128]{1,0:T(8,128)(2,1)S(1)} %paced.3.refs_1_), channel_id=1, source_target_pairs={{2,0},{3,1},{6,2},{7,3},{0,4},{1,5},{4,6},{5,7},{10,8},{11,9},{14,... | collective-permute-start | bytes 995336 | tf_op jit(solution)/shard_map/ppermute | solution.py:288
  60.9 0.1 rearranged.13.refs_0_
  61.0 1.6 %collective-permute-start.12 = (bf16[8,4,8,576]{3,2,1,0:T(8,128)(2,1)S(1)}, bf16[8,4,8,576]{3,2,1,0:T(8,128)(2,1)S(1)}, u32[]{:S(2)}, u32[]{:S(2)}) collective-permute-start(bf16[8,4,8,576]{3,2,1,0:T(8,128)(2,1)S(1)} %get-tuple-element.30), channel_id=1, source_target_pairs={{0,1},{1,0},{2,3},{3,2},{4,5},{5,4},{6,7},{7,6},{8,9},{9,8},{10,11... | collective-permute-start | bytes 884744 | tf_op jit(solution)/shard_map/ppermute | solution.py:279
  62.5 0.5 collective-permute-start.13
  63.1 0.0 copy-start.1
  63.1 3.0 %copy-done.1 = bf16[27648,128]{1,0:T(8,128)(2,1)S(1)} copy-done((bf16[27648,128]{1,0:T(8,128)(2,1)S(1)}, bf16[27648,128]{1,0:T(8,128)(2,1)}, u32[]{:S(2)}) %copy-start.1) | copy-done | bytes 7077912
  66.1 5.0 %products.5 = (bf16[8,4,8,576]{3,2,1,0:T(8,128)(2,1)S(1)}, bf16[8,4,8,576]{3,2,1,0:T(8,128)(2,1)S(1)}, f32[8,128]{1,0:T(8,128)}) custom-call(s32[4,4]{1,0:T(4,128)S(1)} %copy-done.3, bf16[64,128]{1,0:T(8,128)(2,1)S(1)} %copy-done.2, bf16[3456,128]{1,0:T(8,128)(2,1)S(1)} %rearranged.13.refs_0_, bf16[27648,128]{1,0:T(8,128)(2,1)S(1)} %copy-done.1), custom_call_target="tpu_custom_call" | custom-call | flops 905969664 | bytes 8388608 | tf_op jit(solution)/shard_map/jit(products_of)/products/pallas_call | solution.py:191
  71.1 1.5 %collective-permute-start.14 = (bf16[8,4,8,576]{3,2,1,0:T(8,128)(2,1)S(1)}, bf16[8,4,8,576]{3,2,1,0:T(8,128)(2,1)S(1)}, u32[]{:S(2)}, u32[]{:S(2)}) collective-permute-start(bf16[8,4,8,576]{3,2,1,0:T(8,128)(2,1)S(1)} %get-tuple-element.34), channel_id=1, source_target_pairs={{0,1},{1,0},{2,3},{3,2},{4,5},{5,4},{6,7},{7,6},{8,9},{9,8},{10,11... | collective-permute-start | bytes 884744 | tf_op jit(solution)/shard_map/ppermute | solution.py:279
  72.6 0.0 collective-permute-done.3.refs_0_
  72.6 5.6 %collective-permute-done.11.refs_1_ = bf16[1296,128]{1,0:T(8,128)(2,1)S(1)} collective-permute-done((bf16[1296,128]{1,0:T(8,128)(2,1)S(1)}, bf16[1296,128]{1,0:T(8,128)(2,1)S(1)}, u32[]{:S(2)}, u32[]{:S(2)}) %collective-permute-start.11) | collective-permute-done | bytes 331808 | tf_op jit(solution)/shard_map/ppermute | solution.py:288
  78.3 0.1 rearranged.12.refs_0_
  78.3 4.5 %products.4 = (bf16[8,4,8,576]{3,2,1,0:T(8,128)(2,1)S(1)}, bf16[8,4,8,576]{3,2,1,0:T(8,128)(2,1)S(1)}, f32[8,128]{1,0:T(8,128)S(1)}) custom-call(s32[4,4]{1,0:T(4,128)S(1)} %copy-done.3, bf16[64,128]{1,0:T(8,128)(2,1)S(1)} %copy-done.2, bf16[3456,128]{1,0:T(8,128)(2,1)S(1)} %rearranged.12.refs_0_, bf16[27648,128]{1,0:T(8,128)(2,1)S(1)} %copy-done.1), custom_call_target="tpu_custom_call" | custom-call | flops 905969664 | bytes 8388608 | tf_op jit(solution)/shard_map/jit(products_of)/products/pallas_call | solution.py:191
  82.9 1.6 %collective-permute-start.15 = (bf16[8,4,8,576]{3,2,1,0:T(8,128)(2,1)S(1)}, bf16[8,4,8,576]{3,2,1,0:T(8,128)(2,1)S(1)}, u32[]{:S(2)}, u32[]{:S(2)}) collective-permute-start(bf16[8,4,8,576]{3,2,1,0:T(8,128)(2,1)S(1)} %get-tuple-element.36), channel_id=1, source_target_pairs={{0,1},{1,0},{2,3},{3,2},{4,5},{5,4},{6,7},{7,6},{8,9},{9,8},{10,11... | collective-permute-start | bytes 884744 | tf_op jit(solution)/shard_map/ppermute | solution.py:279
  84.4 0.8 bitcast_dynamic-update-slice_fusion.7
  85.2 0.0 collective-permute-done.12
  85.2 0.8 bitcast_dynamic-update-slice_fusion.6
  85.9 0.8 bitcast_dynamic-update-slice_fusion.5
  86.7 0.0 collective-permute-done.13
  86.7 0.8 bitcast_dynamic-update-slice_fusion.4
  87.4 0.8 bitcast_dynamic-update-slice_fusion.3
  88.2 0.0 collective-permute-done.14
  88.2 0.8 bitcast_dynamic-update-slice_fusion.2
  89.0 0.8 bitcast_dynamic-update-slice_fusion.1
  89.7 2.5 %collective-permute-done.15 = bf16[8,4,8,576]{3,2,1,0:T(8,128)(2,1)S(1)} collective-permute-done((bf16[8,4,8,576]{3,2,1,0:T(8,128)(2,1)S(1)}, bf16[8,4,8,576]{3,2,1,0:T(8,128)(2,1)S(1)}, u32[]{:S(2)}, u32[]{:S(2)}) %collective-permute-start.15) | collective-permute-done | bytes 294944 | tf_op jit(solution)/shard_map/ppermute | solution.py:279
  92.2 0.8 bitcast_dynamic-update-slice_fusion
  (4 shorter events, 0.0 us)
Async XLA Ops:
  3.0 23.0 %collective-permute-start = (bf16[3456,128]{1,0:T(8,128)(2,1)S(1)}, bf16[3456,128]{1,0:T(8,128)(2,1)S(1)}, u32[]{:S(2)}, u32[]{:S(2)}) collective-permute-start(bf16[3456,128]{1,0:T(8,128)(2,1)S(1)} %prepare.1.refs_0_), channel_id=1, source_target_pairs={{2,0},{3,1},{6,2},{7,3},{0,4},{1,5},{4,6},{5,7},{10,8},{11,9},{14,... | collective-permute-start | bytes 2654216 | tf_op jit(solution)/shard_map/ppermute | solution.py:288
  7.1 22.4 %collective-permute-start.5 = (bf16[3456,128]{1,0:T(8,128)(2,1)S(1)}, bf16[3456,128]{1,0:T(8,128)(2,1)S(1)}, u32[]{:S(2)}, u32[]{:S(2)}) collective-permute-start(bf16[3456,128]{1,0:T(8,128)(2,1)S(1)} %prepare.1.refs_0_), channel_id=1, source_target_pairs={{0,1},{1,0},{2,3},{3,2},{4,5},{5,4},{6,7},{7,6},{8,9},{9,8},{10,11... | collective-permute-start | bytes 2654216 | tf_op jit(solution)/shard_map/ppermute | solution.py:279
  8.6 20.9 %collective-permute-start.6 = (bf16[3456,128]{1,0:T(8,128)(2,1)S(1)}, bf16[3456,128]{1,0:T(8,128)(2,1)S(1)}, u32[]{:S(2)}, u32[]{:S(2)}) collective-permute-start(bf16[3456,128]{1,0:T(8,128)(2,1)S(1)} %prepare.1.refs_0_), channel_id=1, source_target_pairs={{0,16},{8,24},{16,0},{24,8},{1,17},{9,25},{17,1},{25,9},{2,18},{10... | collective-permute-start | bytes 2654216 | tf_op jit(solution)/shard_map/ppermute | solution.py:276
  26.0 5.8 %collective-permute-start.1 = (bf16[432,128]{1,0:T(8,128)(2,1)S(1)}, bf16[432,128]{1,0:T(8,128)(2,1)S(1)}, u32[]{:S(2)}, u32[]{:S(2)}) collective-permute-start(bf16[432,128]{1,0:T(8,128)(2,1)S(1)} %get-tuple-element.21), channel_id=1, source_target_pairs={{2,0},{3,1},{6,2},{7,3},{0,4},{1,5},{4,6},{5,7},{10,8},{11,9},{14,... | collective-permute-start | bytes 331784 | tf_op jit(solution)/shard_map/ppermute | solution.py:288
  32.0 19.5 %collective-permute-start.7 = (bf16[10368,128]{1,0:T(8,128)(2,1)S(1)}, bf16[10368,128]{1,0:T(8,128)(2,1)S(1)}, u32[]{:S(2)}, u32[]{:S(2)}) collective-permute-start(bf16[10368,128]{1,0:T(8,128)(2,1)S(1)} %get-tuple-element.24), channel_id=1, source_target_pairs={{0,8},{8,0},{16,24},{24,16},{1,9},{9,1},{17,25},{25,17},{2,10},{10... | collective-permute-start | bytes 7962632 | tf_op jit(solution)/shard_map/ppermute | solution.py:273
  32.1 13.4 %collective-permute-start.2 = (bf16[1728,128]{1,0:T(8,128)(2,1)S(1)}, bf16[1728,128]{1,0:T(8,128)(2,1)S(1)}, u32[]{:S(2)}, u32[]{:S(2)}) collective-permute-start(bf16[1728,128]{1,0:T(8,128)(2,1)S(1)} %get-tuple-element.22), channel_id=1, source_target_pairs={{2,0},{3,1},{6,2},{7,3},{0,4},{1,5},{4,6},{5,7},{10,8},{11,9},{14,... | collective-permute-start | bytes 1327112 | tf_op jit(solution)/shard_map/ppermute | solution.py:288
  35.5 12.2 %collective-permute-start.8 = (bf16[1728,128]{1,0:T(8,128)(2,1)S(1)}, bf16[1728,128]{1,0:T(8,128)(2,1)S(1)}, u32[]{:S(2)}, u32[]{:S(2)}) collective-permute-start(bf16[1728,128]{1,0:T(8,128)(2,1)S(1)} %get-tuple-element.25), channel_id=1, source_target_pairs={{0,16},{8,24},{16,0},{24,8},{1,17},{9,25},{17,1},{25,9},{2,18},{10... | collective-permute-start | bytes 1327112 | tf_op jit(solution)/shard_map/ppermute | solution.py:276
  37.0 12.0 %collective-permute-start.9 = (bf16[1728,128]{1,0:T(8,128)(2,1)S(1)}, bf16[1728,128]{1,0:T(8,128)(2,1)S(1)}, u32[]{:S(2)}, u32[]{:S(2)}) collective-permute-start(bf16[1728,128]{1,0:T(8,128)(2,1)S(1)} %get-tuple-element.26), channel_id=1, source_target_pairs={{0,1},{1,0},{2,3},{3,2},{4,5},{5,4},{6,7},{7,6},{8,9},{9,8},{10,11... | collective-permute-start | bytes 1327112 | tf_op jit(solution)/shard_map/ppermute | solution.py:279
  49.0 2.5 %collective-permute-start.10 = (bf16[3456,128]{1,0:T(8,128)(2,1)S(1)}, bf16[3456,128]{1,0:T(8,128)(2,1)S(1)}, u32[]{:S(2)}, u32[]{:S(2)}) collective-permute-start(bf16[3456,128]{1,0:T(8,128)(2,1)S(1)} %rearranged.10), channel_id=1, source_target_pairs={{0,8},{8,0},{16,24},{24,16},{1,9},{9,1},{17,25},{25,17},{2,10},{10... | collective-permute-start | bytes 2654216 | tf_op jit(solution)/shard_map/ppermute | solution.py:273
  49.1 10.7 %collective-permute-start.4 = (bf16[1296,128]{1,0:T(8,128)(2,1)S(1)}, bf16[1296,128]{1,0:T(8,128)(2,1)S(1)}, u32[]{:S(2)}, u32[]{:S(2)}) collective-permute-start(bf16[1296,128]{1,0:T(8,128)(2,1)S(1)} %get-tuple-element.23), channel_id=1, source_target_pairs={{2,0},{3,1},{6,2},{7,3},{0,4},{1,5},{4,6},{5,7},{10,8},{11,9},{14,... | collective-permute-start | bytes 995336 | tf_op jit(solution)/shard_map/ppermute | solution.py:288
  49.5 2.5 %copy-start.2 = (bf16[64,128]{1,0:T(8,128)(2,1)S(1)}, bf16[64,128]{1,0:T(8,128)(2,1)}, u32[]{:S(2)}) copy-start(bf16[64,128]{1,0:T(8,128)(2,1)} %constant.37.clone.turn_ref) | copy-start | bytes 49156
  49.5 2.5 %copy-start.3 = (s32[4,4]{1,0:T(4,128)S(1)}, s32[4,4]{1,0:T(4,128)}, u32[]{:S(2)}) copy-start(s32[4,4]{1,0:T(4,128)} %mask_ref.5) | copy-start | bytes 196
  49.5 23.1 %collective-permute-start.3 = (bf16[2160,128]{1,0:T(8,128)(2,1)S(1)}, bf16[2160,128]{1,0:T(8,128)(2,1)S(1)}, u32[]{:S(2)}, u32[]{:S(2)}) collective-permute-start(bf16[2160,128]{1,0:T(8,128)(2,1)S(1)} %rearranged.8.refs_0_), channel_id=1, source_target_pairs={{2,0},{3,1},{6,2},{7,3},{0,4},{1,5},{4,6},{5,7},{10,8},{11,9},{14,... | collective-permute-start | bytes 1658888 | tf_op jit(solution)/shard_map/ppermute | solution.py:288
  52.0 6.6 %copy-start = (bf16[27648,128]{1,0:T(8,128)(2,1)}, bf16[27648,128]{1,0:T(8,128)(2,1)S(1)}, u32[]{:S(2)}) copy-start(bf16[27648,128]{1,0:T(8,128)(2,1)S(1)} %rearranged.11.refs_2_.refs_1_) | copy-start | bytes 21233668
  59.7 18.5 %collective-permute-start.11 = (bf16[1296,128]{1,0:T(8,128)(2,1)S(1)}, bf16[1296,128]{1,0:T(8,128)(2,1)S(1)}, u32[]{:S(2)}, u32[]{:S(2)}) collective-permute-start(bf16[1296,128]{1,0:T(8,128)(2,1)S(1)} %paced.3.refs_1_), channel_id=1, source_target_pairs={{2,0},{3,1},{6,2},{7,3},{0,4},{1,5},{4,6},{5,7},{10,8},{11,9},{14,... | collective-permute-start | bytes 995336 | tf_op jit(solution)/shard_map/ppermute | solution.py:288
  61.0 24.2 %collective-permute-start.12 = (bf16[8,4,8,576]{3,2,1,0:T(8,128)(2,1)S(1)}, bf16[8,4,8,576]{3,2,1,0:T(8,128)(2,1)S(1)}, u32[]{:S(2)}, u32[]{:S(2)}) collective-permute-start(bf16[8,4,8,576]{3,2,1,0:T(8,128)(2,1)S(1)} %get-tuple-element.30), channel_id=1, source_target_pairs={{0,1},{1,0},{2,3},{3,2},{4,5},{5,4},{6,7},{7,6},{8,9},{9,8},{10,11... | collective-permute-start | bytes 884744 | tf_op jit(solution)/shard_map/ppermute | solution.py:279
  62.5 24.1 %collective-permute-start.13 = (bf16[8,4,8,576]{3,2,1,0:T(8,128)(2,1)S(1)}, bf16[8,4,8,576]{3,2,1,0:T(8,128)(2,1)S(1)}, u32[]{:S(2)}, u32[]{:S(2)}) collective-permute-start(bf16[8,4,8,576]{3,2,1,0:T(8,128)(2,1)S(1)} %get-tuple-element.32), channel_id=1, source_target_pairs={{0,1},{1,0},{2,3},{3,2},{4,5},{5,4},{6,7},{7,6},{8,9},{9,8},{10,11... | collective-permute-start | bytes 884744 | tf_op jit(solution)/shard_map/ppermute | solution.py:279
  63.1 3.0 %copy-start.1 = (bf16[27648,128]{1,0:T(8,128)(2,1)S(1)}, bf16[27648,128]{1,0:T(8,128)(2,1)}, u32[]{:S(2)}) copy-start(bf16[27648,128]{1,0:T(8,128)(2,1)} %copy-done) | copy-start | bytes 21233668
  71.1 17.1 %collective-permute-start.14 = (bf16[8,4,8,576]{3,2,1,0:T(8,128)(2,1)S(1)}, bf16[8,4,8,576]{3,2,1,0:T(8,128)(2,1)S(1)}, u32[]{:S(2)}, u32[]{:S(2)}) collective-permute-start(bf16[8,4,8,576]{3,2,1,0:T(8,128)(2,1)S(1)} %get-tuple-element.34), channel_id=1, source_target_pairs={{0,1},{1,0},{2,3},{3,2},{4,5},{5,4},{6,7},{7,6},{8,9},{9,8},{10,11... | collective-permute-start | bytes 884744 | tf_op jit(solution)/shard_map/ppermute | solution.py:279
  82.9 9.3 %collective-permute-start.15 = (bf16[8,4,8,576]{3,2,1,0:T(8,128)(2,1)S(1)}, bf16[8,4,8,576]{3,2,1,0:T(8,128)(2,1)S(1)}, u32[]{:S(2)}, u32[]{:S(2)}) collective-permute-start(bf16[8,4,8,576]{3,2,1,0:T(8,128)(2,1)S(1)} %get-tuple-element.36), channel_id=1, source_target_pairs={{0,1},{1,0},{2,3},{3,2},{4,5},{5,4},{6,7},{7,6},{8,9},{9,8},{10,11... | collective-permute-start | bytes 884744 | tf_op jit(solution)/shard_map/ppermute | solution.py:279

commit v7 on v5

--- a/solution.py
+++ b/solution.py
@@ -16,7 +16,7 @@
 BLOCK_ROWS = GROUPS * GROUP_ROWS
 HALF_ROWS = BLOCK_ROWS // 2
 STATIONS = 8
-CUTS = (0, 5, 8)
+CUTS = (0, 4, 8)
 PACE = 80 * 2**20
 F32 = jnp.float32
 BF16 = jnp.bfloat16

time: 89.4 us -> 91.4 us (1.022)
  waiting for transfers between devices: 40.3 us -> 45.8 us
  starting transfers between devices: 19.7 us -> 16.2 us
    ppermute x5, waiting for transfers between devices: 21.6 us -> 34.9 us  [over_z(): return lax.ppermute(half, 'rcv', moves)]
    ppermute x2, waiting for transfers between devices: 11.4 us -> 2.51 us  [over_high(): lax.ppermute(half, 'src', [(s, (s + 2) % src_count) for s in range(src_co...]
    ppermute x5, starting transfers between devices: 11.4 us -> 7.81 us  [over_z(): return lax.ppermute(half, 'rcv', moves)]
    ppermute x2, waiting for transfers between devices: 0.01 us -> 1.55 us  [over_core(): return lax.ppermute(half, 'src', [(s, s ^ 1) for s in range(src_count)])]
  transfers between devices with their start and end apart: 15 -> 15, of which waited for: 8 -> 10; matrix products, arithmetic and copies ran while one was open for 6% -> 6% of each run, Pallas kernels for 19% -> 18%
where the time goes in v7:
time: 91.4 us; the launch traced here: 91.2 us
  waiting for transfers between devices  45.8 us (50%)
  Pallas kernels  18.6 us (20%)
  starting transfers between devices  16.2 us (18%)
  local copies, waits for them, and re-layouts  10.5 us (11%)
    ppermute x5, waiting for transfers between devices, over_z(): return lax.ppermute(half, 'rcv', moves)  34.9 us
    pallas_call x3, Pallas kernels, products_of(): pl.pallas_call(functools.partial(products_kernel, layout, s, src_count, n...  16.2 us
    ppermute x5, starting transfers between devices, over_z(): return lax.ppermute(half, 'rcv', moves)  7.81 us
    ppermute x6, waiting for transfers between devices, over_x(): return lax.ppermute(half, 'rcv', [(r, r ^ 1) for r in range(rcv_count)])  6.9 us
    ppermute x6, starting transfers between devices, over_x(): return lax.ppermute(half, 'rcv', [(r, r ^ 1) for r in range(rcv_count)])  5.18 us
    unnamed x9, local copies, waits for them, and re-layouts  4.52 us
    ppermute x2, starting transfers between devices, over_high(): lax.ppermute(half, 'src', [(s, (s + 2) % src_count) for s in range(src_co...  3.04 us
    dynamic_update_slice x4, local copies, waits for them, and re-layouts, on_device(): lax.dynamic_update_slice(result, got[None, None], (at, 1 - x, 0, 0, 0, 0))  3.01 us
  transfers between devices with their start and end apart: 15, of which 10 were waited for; matrix products, arithmetic and copies ran while one was open for 6% of the time, Pallas kernels for 18%

profile of v7, /device:TPU:0, one launch (start us, length us, event | category | flops | bytes accessed | tf_op | source)
XLA Modules:
  0.0 91.2 jit_solution(16551476513104372021)
XLA Ops:
  0.0 1.5 %copy.6.x_ref = bf16[8,287,192]{2,1,0:T(8,128)(2,1)S(1)} copy(bf16[8,287,192]{2,0,1:T(8,128)(2,1)} %param.3) | data formatting | bytes 1763328 | tf_op args[0]
  1.5 1.5 %prepare.1.refs_0_ = bf16[3456,128]{1,0:T(8,128)(2,1)S(1)} custom-call(bf16[8,287,192]{2,1,0:T(8,128)(2,1)S(1)} %copy.6.x_ref), custom_call_target="tpu_custom_call" | custom-call | tf_op jit(solution)/shard_map/prepare/pallas_call | solution.py:72
  3.0 4.1 %collective-permute-start.2 = (bf16[3456,128]{1,0:T(8,128)(2,1)S(1)}, bf16[3456,128]{1,0:T(8,128)(2,1)S(1)}, u32[]{:S(2)}, u32[]{:S(2)}) collective-permute-start(bf16[3456,128]{1,0:T(8,128)(2,1)S(1)} %prepare.1.refs_0_), channel_id=1, source_target_pairs={{2,0},{3,1},{6,2},{7,3},{0,4},{1,5},{4,6},{5,7},{10,8},{11,9},{14,... | collective-permute-start | bytes 2654216 | tf_op jit(solution)/shard_map/ppermute | solution.py:288
  7.1 1.5 %collective-permute-start = (bf16[3456,128]{1,0:T(8,128)(2,1)S(1)}, bf16[3456,128]{1,0:T(8,128)(2,1)S(1)}, u32[]{:S(2)}, u32[]{:S(2)}) collective-permute-start(bf16[3456,128]{1,0:T(8,128)(2,1)S(1)} %prepare.1.refs_0_), channel_id=1, source_target_pairs={{0,1},{1,0},{2,3},{3,2},{4,5},{5,4},{6,7},{7,6},{8,9},{9,8},{10,11... | collective-permute-start | bytes 2654216 | tf_op jit(solution)/shard_map/ppermute | solution.py:279
  8.6 1.5 %collective-permute-start.1 = (bf16[3456,128]{1,0:T(8,128)(2,1)S(1)}, bf16[3456,128]{1,0:T(8,128)(2,1)S(1)}, u32[]{:S(2)}, u32[]{:S(2)}) collective-permute-start(bf16[3456,128]{1,0:T(8,128)(2,1)S(1)} %prepare.1.refs_0_), channel_id=1, source_target_pairs={{0,16},{8,24},{16,0},{24,8},{1,17},{9,25},{17,1},{25,9},{2,18},{10... | collective-permute-start | bytes 2654216 | tf_op jit(solution)/shard_map/ppermute | solution.py:276
  10.1 15.9 %collective-permute-done.2.refs_0_ = bf16[3456,128]{1,0:T(8,128)(2,1)S(1)} collective-permute-done((bf16[3456,128]{1,0:T(8,128)(2,1)S(1)}, bf16[3456,128]{1,0:T(8,128)(2,1)S(1)}, u32[]{:S(2)}, u32[]{:S(2)}) %collective-permute-start.2) | collective-permute-done | bytes 884768 | tf_op jit(solution)/shard_map/ppermute | solution.py:288
  26.0 2.2 %collective-permute-done.refs_1_.refs_3_ = bf16[3456,128]{1,0:T(8,128)(2,1)S(1)} collective-permute-done((bf16[3456,128]{1,0:T(8,128)(2,1)S(1)}, bf16[3456,128]{1,0:T(8,128)(2,1)S(1)}, u32[]{:S(2)}, u32[]{:S(2)}) %collective-permute-start) | collective-permute-done | bytes 884768 | tf_op jit(solution)/shard_map/ppermute | solution.py:279
  28.2 1.2 %collective-permute-done.1.refs_2_ = bf16[3456,128]{1,0:T(8,128)(2,1)S(1)} collective-permute-done((bf16[3456,128]{1,0:T(8,128)(2,1)S(1)}, bf16[3456,128]{1,0:T(8,128)(2,1)S(1)}, u32[]{:S(2)}, u32[]{:S(2)}) %collective-permute-start.1) | collective-permute-done | bytes 884768 | tf_op jit(solution)/shard_map/ppermute | solution.py:276
  29.4 0.3 rearranged.5
  29.7 0.1 collective-permute-start.6
  29.7 1.6 %collective-permute-start.3 = (bf16[1728,128]{1,0:T(8,128)(2,1)S(1)}, bf16[1728,128]{1,0:T(8,128)(2,1)S(1)}, u32[]{:S(2)}, u32[]{:S(2)}) collective-permute-start(bf16[1728,128]{1,0:T(8,128)(2,1)S(1)} %get-tuple-element.20), channel_id=1, source_target_pairs={{2,0},{3,1},{6,2},{7,3},{0,4},{1,5},{4,6},{5,7},{10,8},{11,9},{14,... | collective-permute-start | bytes 1327112 | tf_op jit(solution)/shard_map/ppermute | solution.py:288
  31.4 1.5 %collective-permute-start.7 = (bf16[1728,128]{1,0:T(8,128)(2,1)S(1)}, bf16[1728,128]{1,0:T(8,128)(2,1)S(1)}, u32[]{:S(2)}, u32[]{:S(2)}) collective-permute-start(bf16[1728,128]{1,0:T(8,128)(2,1)S(1)} %get-tuple-element.23), channel_id=1, source_target_pairs={{0,16},{8,24},{16,0},{24,8},{1,17},{9,25},{17,1},{25,9},{2,18},{10... | collective-permute-start | bytes 1327112 | tf_op jit(solution)/shard_map/ppermute | solution.py:276
  32.9 0.5 collective-permute-start.8
  33.4 8.9 %collective-permute-done.3.refs_2_.refs_0_ = bf16[1728,128]{1,0:T(8,128)(2,1)S(1)} collective-permute-done((bf16[1728,128]{1,0:T(8,128)(2,1)S(1)}, bf16[1728,128]{1,0:T(8,128)(2,1)S(1)}, u32[]{:S(2)}, u32[]{:S(2)}) %collective-permute-start.3) | collective-permute-done | bytes 442400 | tf_op jit(solution)/shard_map/ppermute | solution.py:288
  42.3 1.3 %collective-permute-done.7.refs_0_.refs_4_ = bf16[1728,128]{1,0:T(8,128)(2,1)S(1)} collective-permute-done((bf16[1728,128]{1,0:T(8,128)(2,1)S(1)}, bf16[1728,128]{1,0:T(8,128)(2,1)S(1)}, u32[]{:S(2)}, u32[]{:S(2)}) %collective-permute-start.7) | collective-permute-done | bytes 442400 | tf_op jit(solution)/shard_map/ppermute | solution.py:276
  43.6 1.2 %collective-permute-done.8.refs_1_.refs_5_ = bf16[1728,128]{1,0:T(8,128)(2,1)S(1)} collective-permute-done((bf16[1728,128]{1,0:T(8,128)(2,1)S(1)}, bf16[1728,128]{1,0:T(8,128)(2,1)S(1)}, u32[]{:S(2)}, u32[]{:S(2)}) %collective-permute-start.8) | collective-permute-done | bytes 442400 | tf_op jit(solution)/shard_map/ppermute | solution.py:279
  44.9 0.1 rearranged.6
  44.9 0.1 collective-permute-start.9
  45.0 0.0 copy-start.2
  45.0 0.0 copy-start.3
  45.0 0.4 collective-permute-start.5
  45.4 0.4 collective-permute-start.4
  45.9 1.5 %collective-permute-done.9.refs_6_ = bf16[3456,128]{1,0:T(8,128)(2,1)S(1)} collective-permute-done((bf16[3456,128]{1,0:T(8,128)(2,1)S(1)}, bf16[3456,128]{1,0:T(8,128)(2,1)S(1)}, u32[]{:S(2)}, u32[]{:S(2)}) %collective-permute-start.9) | collective-permute-done | bytes 884768 | tf_op jit(solution)/shard_map/ppermute | solution.py:273
  47.4 0.0 collective-permute-done.6.refs_1_
  47.4 0.5 rearranged.7.refs_2_.refs_1_
  47.9 0.0 copy-done.2
  47.9 0.0 copy-done.3
  47.9 0.0 copy-start
  47.9 6.6 %products.3 = (bf16[8,4,8,576]{3,2,1,0:T(8,128)(2,1)S(1)}, bf16[8,4,8,576]{3,2,1,0:T(8,128)(2,1)S(1)}, bf16[8,4,8,576]{3,2,1,0:T(8,128)(2,1)S(1)}, bf16[8,4,8,576]{3,2,1,0:T(8,128)(2,1)S(1)}, f32[8,128]{1,0:T(8,128)S(1)}) custom-call(s32[4,4]{1,0:T(4,128)S(1)} %copy-done.3, bf16[64,128]{1,0:T(8,128)(2,1)S(1)} %copy-done.2, ...), custom_call_target="tpu_custom_call" | custom-call | flops 1811939328 | bytes 8388608 | tf_op jit(solution)/shard_map/jit(products_of)/products/pallas_call | solution.py:191
  54.5 0.0 copy-done
  54.5 3.5 %collective-permute-done.5.refs_0_ = bf16[1728,128]{1,0:T(8,128)(2,1)S(1)} collective-permute-done((bf16[1728,128]{1,0:T(8,128)(2,1)S(1)}, bf16[1728,128]{1,0:T(8,128)(2,1)S(1)}, u32[]{:S(2)}, u32[]{:S(2)}) %collective-permute-start.5) | collective-permute-done | bytes 442400 | tf_op jit(solution)/shard_map/ppermute | solution.py:288
  58.0 1.3 %collective-permute-start.10 = (bf16[1728,128]{1,0:T(8,128)(2,1)S(1)}, bf16[1728,128]{1,0:T(8,128)(2,1)S(1)}, u32[]{:S(2)}, u32[]{:S(2)}) collective-permute-start(bf16[1728,128]{1,0:T(8,128)(2,1)S(1)} %paced.3.refs_1_), channel_id=1, source_target_pairs={{2,0},{3,1},{6,2},{7,3},{0,4},{1,5},{4,6},{5,7},{10,8},{11,9},{14,... | collective-permute-start | bytes 1327112 | tf_op jit(solution)/shard_map/ppermute | solution.py:288
  59.3 0.5 collective-permute-start.11
  59.8 1.5 %collective-permute-start.12 = (bf16[8,4,8,576]{3,2,1,0:T(8,128)(2,1)S(1)}, bf16[8,4,8,576]{3,2,1,0:T(8,128)(2,1)S(1)}, u32[]{:S(2)}, u32[]{:S(2)}) collective-permute-start(bf16[8,4,8,576]{3,2,1,0:T(8,128)(2,1)S(1)} %get-tuple-element.30), channel_id=1, source_target_pairs={{0,1},{1,0},{2,3},{3,2},{4,5},{5,4},{6,7},{7,6},{8,9},{9,8},{10,11... | collective-permute-start | bytes 884744 | tf_op jit(solution)/shard_map/ppermute | solution.py:279
  61.3 0.1 rearranged.9.refs_0_
  61.4 0.0 copy-start.1
  61.4 3.0 %copy-done.1 = bf16[27648,128]{1,0:T(8,128)(2,1)S(1)} copy-done((bf16[27648,128]{1,0:T(8,128)(2,1)S(1)}, bf16[27648,128]{1,0:T(8,128)(2,1)}, u32[]{:S(2)}) %copy-start.1) | copy-done | bytes 7077912
  64.4 5.0 %products.5 = (bf16[8,4,8,576]{3,2,1,0:T(8,128)(2,1)S(1)}, bf16[8,4,8,576]{3,2,1,0:T(8,128)(2,1)S(1)}, f32[8,128]{1,0:T(8,128)}) custom-call(s32[4,4]{1,0:T(4,128)S(1)} %copy-done.3, bf16[64,128]{1,0:T(8,128)(2,1)S(1)} %copy-done.2, bf16[3456,128]{1,0:T(8,128)(2,1)S(1)} %rearranged.9.refs_0_, bf16[27648,128]{1,0:T(8,128)(2,1)S(1)} %copy-done.1), custom_call_target="tpu_custom_call" | custom-call | flops 905969664 | bytes 8388608 | tf_op jit(solution)/shard_map/jit(products_of)/products/pallas_call | solution.py:191
  69.4 0.5 collective-permute-start.13
  70.0 0.0 collective-permute-done.4.refs_0_
  70.0 6.6 %collective-permute-done.10.refs_1_ = bf16[1728,128]{1,0:T(8,128)(2,1)S(1)} collective-permute-done((bf16[1728,128]{1,0:T(8,128)(2,1)S(1)}, bf16[1728,128]{1,0:T(8,128)(2,1)S(1)}, u32[]{:S(2)}, u32[]{:S(2)}) %collective-permute-start.10) | collective-permute-done | bytes 442400 | tf_op jit(solution)/shard_map/ppermute | solution.py:288
  76.5 0.1 rearranged.8.refs_0_
  76.6 4.5 %products.4 = (bf16[8,4,8,576]{3,2,1,0:T(8,128)(2,1)S(1)}, bf16[8,4,8,576]{3,2,1,0:T(8,128)(2,1)S(1)}, f32[8,128]{1,0:T(8,128)S(1)}) custom-call(s32[4,4]{1,0:T(4,128)S(1)} %copy-done.3, bf16[64,128]{1,0:T(8,128)(2,1)S(1)} %copy-done.2, bf16[3456,128]{1,0:T(8,128)(2,1)S(1)} %rearranged.8.refs_0_, bf16[27648,128]{1,0:T(8,128)(2,1)S(1)} %copy-done.1), custom_call_target="tpu_custom_call" | custom-call | flops 905969664 | bytes 8388608 | tf_op jit(solution)/shard_map/jit(products_of)/products/pallas_call | solution.py:191
  81.2 0.6 collective-permute-start.14
  81.8 0.8 bitcast_dynamic-update-slice_fusion.7
  82.5 0.0 collective-permute-done.11
  82.5 0.8 bitcast_dynamic-update-slice_fusion.6
  83.3 0.8 bitcast_dynamic-update-slice_fusion.5
  84.0 0.0 collective-permute-done.12
  84.0 0.8 bitcast_dynamic-update-slice_fusion.4
  84.8 0.8 bitcast_dynamic-update-slice_fusion.3
  85.5 0.0 collective-permute-done.13
  85.5 0.8 bitcast_dynamic-update-slice_fusion.2
  86.3 0.8 bitcast_dynamic-update-slice_fusion.1
  87.0 3.5 %collective-permute-done.14 = bf16[8,4,8,576]{3,2,1,0:T(8,128)(2,1)S(1)} collective-permute-done((bf16[8,4,8,576]{3,2,1,0:T(8,128)(2,1)S(1)}, bf16[8,4,8,576]{3,2,1,0:T(8,128)(2,1)S(1)}, u32[]{:S(2)}, u32[]{:S(2)}) %collective-permute-start.14) | collective-permute-done | bytes 294944 | tf_op jit(solution)/shard_map/ppermute | solution.py:279
  90.5 0.8 bitcast_dynamic-update-slice_fusion
  (3 shorter events, 0.0 us)
Async XLA Ops:
  3.0 23.0 %collective-permute-start.2 = (bf16[3456,128]{1,0:T(8,128)(2,1)S(1)}, bf16[3456,128]{1,0:T(8,128)(2,1)S(1)}, u32[]{:S(2)}, u32[]{:S(2)}) collective-permute-start(bf16[3456,128]{1,0:T(8,128)(2,1)S(1)} %prepare.1.refs_0_), channel_id=1, source_target_pairs={{2,0},{3,1},{6,2},{7,3},{0,4},{1,5},{4,6},{5,7},{10,8},{11,9},{14,... | collective-permute-start | bytes 2654216 | tf_op jit(solution)/shard_map/ppermute | solution.py:288
  7.1 21.1 %collective-permute-start = (bf16[3456,128]{1,0:T(8,128)(2,1)S(1)}, bf16[3456,128]{1,0:T(8,128)(2,1)S(1)}, u32[]{:S(2)}, u32[]{:S(2)}) collective-permute-start(bf16[3456,128]{1,0:T(8,128)(2,1)S(1)} %prepare.1.refs_0_), channel_id=1, source_target_pairs={{0,1},{1,0},{2,3},{3,2},{4,5},{5,4},{6,7},{7,6},{8,9},{9,8},{10,11... | collective-permute-start | bytes 2654216 | tf_op jit(solution)/shard_map/ppermute | solution.py:279
  8.6 20.8 %collective-permute-start.1 = (bf16[3456,128]{1,0:T(8,128)(2,1)S(1)}, bf16[3456,128]{1,0:T(8,128)(2,1)S(1)}, u32[]{:S(2)}, u32[]{:S(2)}) collective-permute-start(bf16[3456,128]{1,0:T(8,128)(2,1)S(1)} %prepare.1.refs_0_), channel_id=1, source_target_pairs={{0,16},{8,24},{16,0},{24,8},{1,17},{9,25},{17,1},{25,9},{2,18},{10... | collective-permute-start | bytes 2654216 | tf_op jit(solution)/shard_map/ppermute | solution.py:276
  29.7 17.7 %collective-permute-start.6 = (bf16[10368,128]{1,0:T(8,128)(2,1)S(1)}, bf16[10368,128]{1,0:T(8,128)(2,1)S(1)}, u32[]{:S(2)}, u32[]{:S(2)}) collective-permute-start(bf16[10368,128]{1,0:T(8,128)(2,1)S(1)} %get-tuple-element.22), channel_id=1, source_target_pairs={{0,8},{8,0},{16,24},{24,16},{1,9},{9,1},{17,25},{25,17},{2,10},{10... | collective-permute-start | bytes 7962632 | tf_op jit(solution)/shard_map/ppermute | solution.py:273
  29.7 12.6 %collective-permute-start.3 = (bf16[1728,128]{1,0:T(8,128)(2,1)S(1)}, bf16[1728,128]{1,0:T(8,128)(2,1)S(1)}, u32[]{:S(2)}, u32[]{:S(2)}) collective-permute-start(bf16[1728,128]{1,0:T(8,128)(2,1)S(1)} %get-tuple-element.20), channel_id=1, source_target_pairs={{2,0},{3,1},{6,2},{7,3},{0,4},{1,5},{4,6},{5,7},{10,8},{11,9},{14,... | collective-permute-start | bytes 1327112 | tf_op jit(solution)/shard_map/ppermute | solution.py:288
  31.4 12.2 %collective-permute-start.7 = (bf16[1728,128]{1,0:T(8,128)(2,1)S(1)}, bf16[1728,128]{1,0:T(8,128)(2,1)S(1)}, u32[]{:S(2)}, u32[]{:S(2)}) collective-permute-start(bf16[1728,128]{1,0:T(8,128)(2,1)S(1)} %get-tuple-element.23), channel_id=1, source_target_pairs={{0,16},{8,24},{16,0},{24,8},{1,17},{9,25},{17,1},{25,9},{2,18},{10... | collective-permute-start | bytes 1327112 | tf_op jit(solution)/shard_map/ppermute | solution.py:276
  32.9 12.0 %collective-permute-start.8 = (bf16[1728,128]{1,0:T(8,128)(2,1)S(1)}, bf16[1728,128]{1,0:T(8,128)(2,1)S(1)}, u32[]{:S(2)}, u32[]{:S(2)}) collective-permute-start(bf16[1728,128]{1,0:T(8,128)(2,1)S(1)} %get-tuple-element.24), channel_id=1, source_target_pairs={{0,1},{1,0},{2,3},{3,2},{4,5},{5,4},{6,7},{7,6},{8,9},{9,8},{10,11... | collective-permute-start | bytes 1327112 | tf_op jit(solution)/shard_map/ppermute | solution.py:279
  44.9 2.5 %collective-permute-start.9 = (bf16[3456,128]{1,0:T(8,128)(2,1)S(1)}, bf16[3456,128]{1,0:T(8,128)(2,1)S(1)}, u32[]{:S(2)}, u32[]{:S(2)}) collective-permute-start(bf16[3456,128]{1,0:T(8,128)(2,1)S(1)} %rearranged.6), channel_id=1, source_target_pairs={{0,8},{8,0},{16,24},{24,16},{1,9},{9,1},{17,25},{25,17},{2,10},{10... | collective-permute-start | bytes 2654216 | tf_op jit(solution)/shard_map/ppermute | solution.py:273
  45.0 2.9 %copy-start.2 = (bf16[64,128]{1,0:T(8,128)(2,1)S(1)}, bf16[64,128]{1,0:T(8,128)(2,1)}, u32[]{:S(2)}) copy-start(bf16[64,128]{1,0:T(8,128)(2,1)} %constant.37.clone.turn_ref) | copy-start | bytes 49156
  45.0 2.9 %copy-start.3 = (s32[4,4]{1,0:T(4,128)S(1)}, s32[4,4]{1,0:T(4,128)}, u32[]{:S(2)}) copy-start(s32[4,4]{1,0:T(4,128)} %mask_ref.5) | copy-start | bytes 196
  45.0 13.0 %collective-permute-start.5 = (bf16[1728,128]{1,0:T(8,128)(2,1)S(1)}, bf16[1728,128]{1,0:T(8,128)(2,1)S(1)}, u32[]{:S(2)}, u32[]{:S(2)}) collective-permute-start(bf16[1728,128]{1,0:T(8,128)(2,1)S(1)} %get-tuple-element.21), channel_id=1, source_target_pairs={{2,0},{3,1},{6,2},{7,3},{0,4},{1,5},{4,6},{5,7},{10,8},{11,9},{14,... | collective-permute-start | bytes 1327112 | tf_op jit(solution)/shard_map/ppermute | solution.py:288
  45.4 24.6 %collective-permute-start.4 = (bf16[1728,128]{1,0:T(8,128)(2,1)S(1)}, bf16[1728,128]{1,0:T(8,128)(2,1)S(1)}, u32[]{:S(2)}, u32[]{:S(2)}) collective-permute-start(bf16[1728,128]{1,0:T(8,128)(2,1)S(1)} %collective-permute-done.3.refs_2_.refs_0_), channel_id=1, source_target_pairs={{2,0},{3,1},{6,2},{7,3},{0,4},{1,5},{4,6},{5,7},{10,8},{11,9},{14,... | collective-permute-start | bytes 1327112 | tf_op jit(solution)/shard_map/ppermute | solution.py:288
  47.9 6.6 %copy-start = (bf16[27648,128]{1,0:T(8,128)(2,1)}, bf16[27648,128]{1,0:T(8,128)(2,1)S(1)}, u32[]{:S(2)}) copy-start(bf16[27648,128]{1,0:T(8,128)(2,1)S(1)} %rearranged.7.refs_2_.refs_1_) | copy-start | bytes 21233668
  58.0 18.5 %collective-permute-start.10 = (bf16[1728,128]{1,0:T(8,128)(2,1)S(1)}, bf16[1728,128]{1,0:T(8,128)(2,1)S(1)}, u32[]{:S(2)}, u32[]{:S(2)}) collective-permute-start(bf16[1728,128]{1,0:T(8,128)(2,1)S(1)} %paced.3.refs_1_), channel_id=1, source_target_pairs={{2,0},{3,1},{6,2},{7,3},{0,4},{1,5},{4,6},{5,7},{10,8},{11,9},{14,... | collective-permute-start | bytes 1327112 | tf_op jit(solution)/shard_map/ppermute | solution.py:288
  59.3 23.2 %collective-permute-start.11 = (bf16[8,4,8,576]{3,2,1,0:T(8,128)(2,1)S(1)}, bf16[8,4,8,576]{3,2,1,0:T(8,128)(2,1)S(1)}, u32[]{:S(2)}, u32[]{:S(2)}) collective-permute-start(bf16[8,4,8,576]{3,2,1,0:T(8,128)(2,1)S(1)} %get-tuple-element.28), channel_id=1, source_target_pairs={{0,1},{1,0},{2,3},{3,2},{4,5},{5,4},{6,7},{7,6},{8,9},{9,8},{10,11... | collective-permute-start | bytes 884744 | tf_op jit(solution)/shard_map/ppermute | solution.py:279
  59.8 24.2 %collective-permute-start.12 = (bf16[8,4,8,576]{3,2,1,0:T(8,128)(2,1)S(1)}, bf16[8,4,8,576]{3,2,1,0:T(8,128)(2,1)S(1)}, u32[]{:S(2)}, u32[]{:S(2)}) collective-permute-start(bf16[8,4,8,576]{3,2,1,0:T(8,128)(2,1)S(1)} %get-tuple-element.30), channel_id=1, source_target_pairs={{0,1},{1,0},{2,3},{3,2},{4,5},{5,4},{6,7},{7,6},{8,9},{9,8},{10,11... | collective-permute-start | bytes 884744 | tf_op jit(solution)/shard_map/ppermute | solution.py:279
  61.4 3.0 %copy-start.1 = (bf16[27648,128]{1,0:T(8,128)(2,1)S(1)}, bf16[27648,128]{1,0:T(8,128)(2,1)}, u32[]{:S(2)}) copy-start(bf16[27648,128]{1,0:T(8,128)(2,1)} %copy-done) | copy-start | bytes 21233668
  69.4 16.1 %collective-permute-start.13 = (bf16[8,4,8,576]{3,2,1,0:T(8,128)(2,1)S(1)}, bf16[8,4,8,576]{3,2,1,0:T(8,128)(2,1)S(1)}, u32[]{:S(2)}, u32[]{:S(2)}) collective-permute-start(bf16[8,4,8,576]{3,2,1,0:T(8,128)(2,1)S(1)} %get-tuple-element.32), channel_id=1, source_target_pairs={{0,1},{1,0},{2,3},{3,2},{4,5},{5,4},{6,7},{7,6},{8,9},{9,8},{10,11... | collective-permute-start | bytes 884744 | tf_op jit(solution)/shard_map/ppermute | solution.py:279
  81.2 9.3 %collective-permute-start.14 = (bf16[8,4,8,576]{3,2,1,0:T(8,128)(2,1)S(1)}, bf16[8,4,8,576]{3,2,1,0:T(8,128)(2,1)S(1)}, u32[]{:S(2)}, u32[]{:S(2)}) collective-permute-start(bf16[8,4,8,576]{3,2,1,0:T(8,128)(2,1)S(1)} %get-tuple-element.34), channel_id=1, source_target_pairs={{0,1},{1,0},{2,3},{3,2},{4,5},{5,4},{6,7},{7,6},{8,9},{9,8},{10,11... | collective-permute-start | bytes 884744 | tf_op jit(solution)/shard_map/ppermute | solution.py:279
